TPU v7x, 256 devices: a whole 4x4x8 slice. The times are simulated.
256 devices in a mesh: blk: 32 (over x, z_lo, core), tensor: 8 (over z_hi, y).
Axes of the slice: x: 4, y: 4, z: 8 (z_hi: 2, z_lo: 4; z = z_hi * 4 + z_lo), core: 2. Of those that a mesh axis runs over, the one named last changes fastest.
Arguments:
- queries: bfloat16 [2048, 4096], P('blk', 'tensor'), may hold values from -64 to 64
- prefix_keys: bfloat16 [32768, 1024], P('blk', 'tensor'), may hold values from -6 to 6
- prefix_values: bfloat16 [32768, 1024], P('blk', 'tensor'), may hold values from -6 to 6
- suffix_keys: bfloat16 [2048, 128, 1024], P('blk', None, 'tensor'), may hold values from -16 to 16
- suffix_values: bfloat16 [2048, 128, 1024], P('blk', None, 'tensor'), may hold values from -6 to 6
- suffix_lengths: int32 [2048], P('blk'), may hold values from 32 to 128, as said below
- out_weight: bfloat16 [4096, 8192], P('tensor'), may hold values from -0.09375 to 0.09375
Outputs:
- attended: bfloat16 [2048, 8192], P('blk', 'tensor')
Inputs may be any that keep to these rules, and one draw needn't show every extreme that they name: `suffix_lengths`: some completion has exactly 128 live suffix slots.
All inputs are finite; a program needn't handle non-finite values.
Results may differ from a plain program's by a relative error of at most 0.01555.
Values may be sent and summed in bfloat16 or wider, within the bound.
No kernel may reach another device: no remote copies, remote signals or barrier semaphores. Data moves between devices by JAX's collectives and lax.ppermute only.
A program may use at most 128 MiB of HBM per device.

v0:
```python
import math

import jax
import jax.numpy as jnp
from jax import lax
from jax.sharding import PartitionSpec as P

DH = 128


def merge_pair(carry, part):
    peak_a, total_a, mixed_a = carry
    peak_b, total_b, mixed_b = part
    peak_new = jnp.maximum(peak_a, peak_b)
    factor_a = jnp.exp(peak_a - peak_new)
    factor_b = jnp.exp(peak_b - peak_new)
    return (
        peak_new,
        total_a * factor_a + total_b * factor_b,
        mixed_a * factor_a[..., None] + mixed_b * factor_b[..., None],
    )


def block_partial(query_block, key_block, value_block, score_scale):
    scores = (
        jnp.einsum("rhgd,phd->rhgp", query_block, key_block, preferred_element_type=jnp.float32)
        * score_scale
    )
    peaks = jnp.max(scores, axis=-1)
    weights = jnp.exp(scores - peaks[..., None])
    totals = jnp.sum(weights, axis=-1)
    mixed = jnp.einsum(
        "rhgp,phd->rhgd",
        weights.astype(jnp.bfloat16),
        value_block,
        preferred_element_type=jnp.float32,
    )
    return (peaks, totals, mixed)


def on_device(
    queries, prefix_keys, prefix_values, suffix_keys, suffix_values, suffix_lengths, out_weight
):
    row_count = queries.shape[0]
    kv_local = prefix_keys.shape[1] // DH
    group = queries.shape[1] // (kv_local * DH)
    block_len = prefix_keys.shape[0]
    slot_count = suffix_keys.shape[1]
    score_scale = 1.0 / math.sqrt(DH)
    query_heads = queries.reshape(row_count, kv_local, group, DH)
    key_cache = suffix_keys.reshape(row_count, slot_count, kv_local, DH)
    value_cache = suffix_values.reshape(row_count, slot_count, kv_local, DH)
    scores = (
        jnp.einsum("rhgd,rshd->rhgs", query_heads, key_cache, preferred_element_type=jnp.float32)
        * score_scale
    )
    live = (jnp.arange(slot_count, dtype=jnp.int32)[None, :] < suffix_lengths[:, None])[
        :, None, None, :
    ]
    peaks = jnp.max(jnp.where(live, scores, -jnp.inf), axis=-1)
    weights = jnp.where(live, jnp.exp(scores - peaks[..., None]), jnp.zeros_like(scores))
    totals = jnp.sum(weights, axis=-1)
    mixed = jnp.einsum(
        "rhgs,rshd->rhgd",
        weights.astype(jnp.bfloat16),
        value_cache,
        preferred_element_type=jnp.float32,
    )
    state = (peaks, totals, mixed)
    carry = state
    key_piece = lax.all_gather(prefix_keys, "blk", axis=0, tiled=True)
    value_piece = lax.all_gather(prefix_values, "blk", axis=0, tiled=True)
    count = key_piece.shape[0] // block_len
    key_stack = key_piece.reshape(count, block_len, kv_local, DH)
    value_stack = value_piece.reshape(count, block_len, kv_local, DH)

    def one_block(inner, blocks):
        return (
            merge_pair(inner, block_partial(query_heads, blocks[0], blocks[1], score_scale)),
            None,
        )

    carry, _ = lax.scan(one_block, carry, (key_stack, value_stack))
    state = carry
    attention = (
        (state[2] / state[1][..., None])
        .astype(jnp.bfloat16)
        .reshape(row_count, kv_local * group * DH)
    )
    projected = jnp.dot(attention, out_weight, preferred_element_type=jnp.float32)
    return lax.psum_scatter(
        projected.astype(jnp.bfloat16), "tensor", scatter_dimension=1, tiled=True
    )


def solution(mesh):
    in_specs = (
        P("blk", "tensor"),
        P("blk", "tensor"),
        P("blk", "tensor"),
        P("blk", None, "tensor"),
        P("blk", None, "tensor"),
        P("blk"),
        P("tensor", None),
    )
    out_specs = P("blk", "tensor")
    return jax.shard_map(
        on_device, mesh=mesh, in_specs=in_specs, out_specs=out_specs, check_vma=False
    )
```

profile of v0, /device:TPU:2, one launch (start us, length us, event | category | flops | bytes accessed | tf_op | source)
XLA Modules:
  0.0 347.2 jit_solution(16608628202525481686)
XLA Ops:
  11.8 2.3 convolution_bitcast_fusion.1
  14.5 66.8 %all-gather.3.cloned.1.call-done = bf16[32768,128]{1,0:T(8,128)(2,1)} async-done(((bf16[1024,128]{1,0:T(8,128)(2,1)}), bf16[32768,128]{1,0:T(8,128)(2,1)}) %all-gather.3.cloned.1.call-update) | async-done | bytes 8388624 | tf_op jit(solution)/shard_map/all_gather | solution.py:71
  81.4 69.8 %all-gather.5.cloned.1.call-done = bf16[32768,128]{1,0:T(8,128)(2,1)} async-done(((bf16[1024,128]{1,0:T(8,128)(2,1)}), bf16[32768,128]{1,0:T(8,128)(2,1)}) %all-gather.5.cloned.1.call-update) | async-done | bytes 8388624 | tf_op jit(solution)/shard_map/all_gather | solution.py:72
  151.2 97.8 %while.14 = (s32[]{:T(128)}, f32[64,1,4]{0,2,1:T(4,128)S(1)}, f32[64,1,4]{0,2,1:T(4,128)S(1)}, f32[64,1,4,128]{3,0,2,1:T(8,128)S(1)}, bf16[32,1024,1,128]{3,1,2,...) while((s32[]{:T(128)}, f32[64,1,4]{0,2,1:T(4,128)S(1)}, ...), condition=%wide.region_5.6_spmd, body=%wide.region_2.5_spmd.sunk | while | flops 135890176 | bytes 4018261 | solution.py:83
  152.8 1.3 fusion.47
  155.9 1.3 fusion.47
  159.0 1.3 fusion.47
  162.0 1.3 fusion.47
  165.1 1.3 fusion.47
  168.1 1.3 fusion.47
  171.2 1.3 fusion.47
  174.2 1.3 fusion.47
  177.3 1.3 fusion.47
  180.4 1.3 fusion.47
  183.4 1.3 fusion.47
  186.5 1.3 fusion.47
  189.5 1.3 fusion.47
  192.6 1.3 fusion.47
  195.6 1.3 fusion.47
  198.7 1.3 fusion.47
  220.1 1.3 fusion.47
  223.1 1.3 fusion.47
  249.1 5.9 %convolution_convert_fusion = bf16[64,8192]{1,0:T(8,128)(2,1)} fusion(bf16[512,8192]{1,0:T(8,128)(2,1)} %param.15, bf16[8,8,4,128]{3,2,1,0:T(4,128)(2,1)S(1)} %bitcast.90), kind=kOutput, calls=%fused_computation.26 | convolution fusion | flops 537395200 | bytes 9502720 | tf_op jit(solution)/shard_map/dot_general | solution.py:90
  255.1 85.6 %reduce-scatter.2.cloned.1.call-done = bf16[64,1024]{1,0:T(8,128)(2,1)} async-done(((bf16[64,8192]{1,0:T(8,128)(2,1)}), bf16[64,1024]{1,0:T(8,128)(2,1)}) %reduce-scatter.2.cloned.1.call-update) | async-done | bytes 131088 | tf_op jit(solution)/shard_map/reduce_scatter | solution.py:91
  (193 shorter events, 78.1 us)
Async XLA Ops:
  6.5 4.0 %copy-start = (bf16[64,128,128]{2,1,0:T(8,128)(2,1)S(1)}, bf16[64,128,128]{2,1,0:T(8,128)(2,1)}, u32[]{:S(2)}) copy-start(bf16[64,128,128]{2,1,0:T(8,128)(2,1)} %param.12) | copy-start | bytes 6291460
  6.5 74.8 %all-gather.3.cloned.1.call-start = ((), (), s32[]{:S(2)}) async-start(), calls=%async_computation.1 | async-start | bytes 8650752 | tf_op jit(solution)/shard_map/all_gather | solution.py:71
  7.3 143.9 %all-gather.5.cloned.1.call-start = ((), (), s32[]{:S(2)}) async-start(), calls=%async_computation.2 | async-start | bytes 8650752 | tf_op jit(solution)/shard_map/all_gather | solution.py:72
  8.0 332.7 %reduce-scatter.2.cloned.1.call-start = ((), (), s32[]{:S(2)}) async-start(), calls=%async_computation.3 | async-start | bytes 1179648 | tf_op jit(solution)/shard_map/reduce_scatter | solution.py:91
Sparse Core Ops, SparseCore 0:
  9.2 72.0 all-gather.2
  83.2 67.9 all-gather.4
  255.2 85.4 reduce-scatter.1
where the time goes:
time: 349 us; the launch traced here: 347 us
  waiting for transfers between devices  224 us (64%)
  matrix products  95.1 us (27%)
  between operations  13.2 us (4%)
  other arithmetic  11.9 us (3%)
    reduce_scatter x1, waiting for transfers between devices, on_device(): lax.psum_scatter(projected.astype(jnp.bfloat16), 'tensor', scatter_dimens...  85.6 us
    all_gather x1, waiting for transfers between devices, on_device(): value_piece = lax.all_gather(prefix_values, 'blk', axis=0, tiled=True)  69.8 us
    all_gather x1, waiting for transfers between devices, on_device(): key_piece = lax.all_gather(prefix_keys, 'blk', axis=0, tiled=True)  66.8 us
    dot_general x32, matrix products, block_partial(): jnp.einsum('rhgp,phd->rhgd', weights.astype(jnp.bfloat16), value_block, p...  43 us
    dot_general x32, matrix products, block_partial(): jnp.einsum('rhgd,phd->rhgp', query_block, key_block, preferred_element_ty...  42.6 us
    reduce_sum x32, other arithmetic, block_partial(): totals = jnp.sum(weights, axis=-1)  10.1 us
  transfers between devices with their start and end apart: 3, of which 3 were waited for; matrix products, arithmetic and copies ran while one was open for 2% of the time, Pallas kernels for 0%

commit v1 on v0

v1 whole, which is shorter than its diff:
```python
import functools
import math

import jax
import jax.numpy as jnp
from jax import lax
from jax.experimental import pallas as pl
from jax.experimental.pallas import tpu as pltpu
from jax.sharding import PartitionSpec as P

DH = 128
GROUP = 4
WIDTH = GROUP * DH
LOG2E = math.log2(math.e)
SCALE2 = LOG2E / math.sqrt(DH)
F32 = jnp.float32
BF16 = jnp.bfloat16
VMEM_LIMIT = 56 << 20

NX, NZ, NC = 4, 4, 2
NH, NY = 2, 4


def blk_perm(dx=0, dz=0, dc=0):
    pairs = []
    for x in range(NX):
        for z in range(NZ):
            for c in range(NC):
                there = ((x + dx) % NX * NZ + (z + dz) % NZ) * NC + (c + dc) % NC
                pairs.append(((x * NZ + z) * NC + c, there))
    return pairs


def tensor_perm(dh=0, dy=0):
    return [
        (h * NY + y, (h + dh) % NH * NY + (y + dy) % NY) for h in range(NH) for y in range(NY)
    ]


def params():
    return pltpu.CompilerParams(vmem_limit_bytes=VMEM_LIMIT)


def cost(flops, nbytes, transcendentals=0):
    return pl.CostEstimate(flops=flops, bytes_accessed=nbytes, transcendentals=transcendentals)


def heads_of(q):
    return jnp.concatenate([q[:, h * DH : (h + 1) * DH] for h in range(GROUP)], axis=0)


SUB = 16


def suffix_kernel(len_ref, q_ref, k_ref, v_ref, o_ref, lse_ref):
    slots = k_ref.shape[1]
    first = pl.program_id(0) * SUB
    q = heads_of(q_ref[...])
    k = k_ref[...].reshape(SUB * slots, DH)
    v = v_ref[...].reshape(SUB * slots, DH)
    s = lax.dot_general(q, k, (((1,), (1,)), ((), ())), preferred_element_type=F32)
    row = lax.broadcasted_iota(jnp.int32, (SUB, slots), 0)
    col = lax.broadcasted_iota(jnp.int32, (SUB, slots), 1)
    tiles = [(row == j) & (col < len_ref[first + j]) for j in range(SUB)]
    live = jnp.concatenate(tiles, axis=1)
    live = jnp.concatenate([live] * GROUP, axis=0)
    s = jnp.where(live, s * SCALE2, -jnp.inf)
    peak = jnp.max(s, axis=1, keepdims=True)
    p = jnp.exp2(s - peak)
    total = jnp.sum(p, axis=1, keepdims=True)
    mixed = jnp.dot(p.astype(BF16), v, preferred_element_type=F32) / total
    lse = peak + jnp.log2(total)
    lane = lax.broadcasted_iota(jnp.int32, (SUB, DH), 1)
    stat = jnp.zeros((SUB, DH), F32)
    for h in range(GROUP):
        o_ref[:, h * DH : (h + 1) * DH] = mixed[h * SUB : (h + 1) * SUB]
        stat = jnp.where(lane == h, lse[h * SUB : (h + 1) * SUB], stat)
    lse_ref[...] = stat


def suffix_partial(q, sk, sv, lengths):
    rows, slots, _ = sk.shape
    return pl.pallas_call(
        suffix_kernel,
        grid_spec=pltpu.PrefetchScalarGridSpec(
            num_scalar_prefetch=1,
            grid=(rows // SUB,),
            in_specs=[
                pl.BlockSpec((SUB, WIDTH), lambda i, _: (i, 0)),
                pl.BlockSpec((SUB, slots, DH), lambda i, _: (i, 0, 0)),
                pl.BlockSpec((SUB, slots, DH), lambda i, _: (i, 0, 0)),
            ],
            out_specs=[
                pl.BlockSpec((SUB, WIDTH), lambda i, _: (i, 0)),
                pl.BlockSpec((SUB, DH), lambda i, _: (i, 0)),
            ],
        ),
        out_shape=[
            jax.ShapeDtypeStruct((rows, WIDTH), F32),
            jax.ShapeDtypeStruct((rows, DH), F32),
        ],
        compiler_params=params(),
        cost_estimate=cost(4 * rows * WIDTH * slots * SUB, 4 * rows * slots * DH),
    )(lengths, q, sk, sv)


def prefix_kernel(groups, blocks, first, last, *refs):
    refs = list(refs)
    qs = [refs.pop(0) for _ in range(groups)]
    kvs = []
    for kind in blocks:
        if kind == "pair":
            kvs.append((refs.pop(0), 0, refs.pop(0), 0))
        else:
            both = refs.pop(0)
            kvs.append((both, 0, both, both.shape[0] // 2))
    if not first:
        acc_in, stat_in = refs.pop(0), refs.pop(0)
    rows = qs[0].shape[0]
    total_rows = GROUP * rows
    lane = lax.broadcasted_iota(jnp.int32, (total_rows, DH), 1)
    for g in range(groups):
        q = heads_of(qs[g][...])
        span = slice(g * total_rows, (g + 1) * total_rows)
        peak = None
        if not first:
            acc = acc_in[span, :]
            peak = stat_in[span, 0:1]
            total = stat_in[span, DH // 2 : DH // 2 + 1]
        for k_ref, k_at, v_ref, v_at in kvs:
            size = v_ref.shape[0] - v_at
            k = k_ref[k_at : k_at + size, :]
            v = v_ref[v_at : v_at + size, :]
            s = lax.dot_general(q, k, (((1,), (1,)), ((), ())), preferred_element_type=F32)
            top = jnp.max(s, axis=1, keepdims=True) * SCALE2
            new = top if peak is None else jnp.maximum(peak, top)
            p = jnp.exp2(s * SCALE2 - new).astype(BF16)
            both = jnp.dot(
                p,
                jnp.concatenate([v, jnp.ones_like(v)], axis=1),
                preferred_element_type=F32,
            )
            if peak is None:
                acc, total = both[:, :DH], both[:, DH : DH + 1]
            else:
                fade = jnp.exp2(peak - new)
                acc = acc * fade + both[:, :DH]
                total = total * fade + both[:, DH : DH + 1]
            peak = new
        if last:
            o_ref = refs[g]
            mixed = (acc / total).astype(BF16)
            lse = peak + jnp.log2(total)
            stat = jnp.zeros((rows, DH), F32)
            for h in range(GROUP):
                part = slice(h * rows, (h + 1) * rows)
                o_ref[:, h * DH : (h + 1) * DH] = mixed[part]
                rest = lse[part]
                for j in range(3):
                    piece = rest.astype(BF16).astype(F32)
                    rest = rest - piece
                    stat = jnp.where(lane[:rows] == 3 * h + j, piece, stat)
            o_ref[:, WIDTH:] = stat.astype(BF16)
        else:
            refs[0][span, :] = acc
            refs[1][span, :] = jnp.where(lane < DH // 2, peak, total)


def prefix_partial(queries, blocks, state, last):
    rows = queries[0].shape[0]
    groups = len(queries)
    all_rows = groups * GROUP * rows
    kinds, arrays, keys = [], [], 0
    for block in blocks:
        if isinstance(block, tuple):
            kinds.append("pair")
            arrays += list(block)
            keys += block[0].shape[0]
        else:
            kinds.append("both")
            arrays.append(block)
            keys += block.shape[0] // 2
    if last:
        outs = [jax.ShapeDtypeStruct((rows, WIDTH + DH), BF16)] * groups
    else:
        outs = [jax.ShapeDtypeStruct((all_rows, DH), F32)] * 2
    return pl.pallas_call(
        functools.partial(prefix_kernel, groups, tuple(kinds), state is None, last),
        out_shape=outs,
        compiler_params=params(),
        cost_estimate=cost(8 * all_rows * DH * keys, 4 * keys * DH, all_rows * keys),
    )(*queries, *arrays, *(state or ()))


def merged(parts, mixed, lse):
    columns = []
    for h in range(GROUP):
        span = slice(h * DH, (h + 1) * DH)
        logs, values = [lse[:, h : h + 1]], [mixed[:, span]]
        for part in parts:
            stat = part[:, WIDTH:].astype(F32)
            at = 3 * h
            logs.append(stat[:, at : at + 1] + stat[:, at + 1 : at + 2] + stat[:, at + 2 : at + 3])
            values.append(part[:, span].astype(F32))
        peak = functools.reduce(jnp.maximum, logs)
        weights = [jnp.exp2(log - peak) for log in logs]
        total = functools.reduce(jnp.add, weights)
        value = functools.reduce(jnp.add, [w * o for w, o in zip(weights, values)])
        columns.append((value / total).astype(BF16))
    return jnp.concatenate(columns, axis=1)


def project_kernel(n_parts, merge, index_ref, *refs):
    refs = list(refs)
    if merge:
        parts = [refs.pop(0) for _ in range(n_parts)]
        mixed, lse = refs.pop(0), refs.pop(0)
        weights, refs = refs[:NY], refs[NY:]
        outs, att_ref = refs[:NY], refs[NY]

        @pl.when(pl.program_id(0) == 0)
        def _():
            att_ref[...] = merged([p[...] for p in parts], mixed[...], lse[...])
    else:
        att_ref = refs.pop(0)
        weights, outs = refs[:NY], refs[NY:]
    att = att_ref[...]
    for w, o in zip(weights, outs):
        o[...] = jnp.dot(att, w[...], preferred_element_type=F32).astype(o.dtype)


STEPS = 4


def project(index, inputs, weight, merge):
    rows = inputs[0].shape[0]
    depth, columns = weight.shape
    piece = columns // (NH * NY)
    tile = piece // STEPS

    def whole(a):
        return pl.BlockSpec(a.shape, lambda i, _: (0, 0))

    def block(k):
        return pl.BlockSpec((depth, tile), lambda i, at: (0, at[k] * STEPS + i))

    out_shape = [jax.ShapeDtypeStruct((rows, piece), F32 if k == 0 else BF16) for k in range(NY)]
    out_specs = [pl.BlockSpec((rows, tile), lambda i, _: (0, i)) for _ in range(NY)]
    if merge:
        out_shape.append(jax.ShapeDtypeStruct((rows, depth), BF16))
        out_specs.append(pl.BlockSpec((rows, depth), lambda i, _: (0, 0)))
    return pl.pallas_call(
        functools.partial(project_kernel, len(inputs) - 2, merge),
        grid_spec=pltpu.PrefetchScalarGridSpec(
            num_scalar_prefetch=1,
            grid=(STEPS,),
            in_specs=[whole(a) for a in inputs] + [block(k) for k in range(NY)],
            out_specs=out_specs,
        ),
        out_shape=out_shape,
        compiler_params=params(),
        cost_estimate=cost(2 * rows * depth * piece * NY, 2 * depth * piece * NY),
    )(index, *inputs, *([weight] * NY))


def on_device(
    queries, prefix_keys, prefix_values, suffix_keys, suffix_values, suffix_lengths, out_weight
):
    send = functools.partial(lax.ppermute, axis_name="blk")
    both = jnp.concatenate([prefix_keys, prefix_values], axis=0)
    peer = send(both, perm=blk_perm(dc=1))
    near = [send(both, perm=blk_perm(dx=d)) for d in (1, 3)]
    far = send(both, perm=blk_perm(dx=2))
    group = [queries] + [send(queries, perm=blk_perm(dz=d)) for d in (1, 2, 3)]

    mixed, lse = suffix_partial(queries, suffix_keys, suffix_values, suffix_lengths)

    state = prefix_partial(group, [(prefix_keys, prefix_values), peer], None, False)
    near_peer = [send(b, perm=blk_perm(dc=1)) for b in near]
    state = prefix_partial(group, near, state, False)
    far_peer = send(far, perm=blk_perm(dc=1))
    parts = prefix_partial(group, near_peer + [far, far_peer], state, True)
    parts = [parts[0]] + [send(parts[d], perm=blk_perm(dz=-d)) for d in (1, 2, 3)]

    here = lax.axis_index("tensor")
    half, line = here // NY, here % NY
    lines = (line + jnp.arange(NY, dtype=jnp.int32)) % NY
    send = functools.partial(lax.ppermute, axis_name="tensor")
    *away, attention = project((NH - 1 - half) * NY + lines, parts + [mixed, lse], out_weight, True)
    away = [away[0]] + [send(away[d], perm=tensor_perm(dy=d)) for d in (1, 2, 3)]
    home = project(half * NY + lines, [attention], out_weight, False)
    home = [home[0]] + [send(home[d], perm=tensor_perm(dy=d)) for d in (1, 2, 3)]

    def summed(pieces):
        return functools.reduce(jnp.add, [p.astype(F32) for p in pieces])

    other = send(summed(away).astype(BF16), perm=tensor_perm(dh=1))
    return summed(home + [other]).astype(BF16)


def solution(mesh):
    in_specs = (
        P("blk", "tensor"),
        P("blk", "tensor"),
        P("blk", "tensor"),
        P("blk", None, "tensor"),
        P("blk", None, "tensor"),
        P("blk"),
        P("tensor", None),
    )
    out_specs = P("blk", "tensor")
    return jax.shard_map(
        on_device, mesh=mesh, in_specs=in_specs, out_specs=out_specs, check_vma=False
    )
```

time: 349 us -> 105 us (0.30)
  waiting for transfers between devices: 224 us -> 31.2 us
  matrix products: 95.1 us -> 0 us
  Pallas kernels: 0 us -> 38.6 us
  starting transfers between devices: 0.08 us -> 27.7 us
  between operations: 13.2 us -> 0.14 us
  other arithmetic: 11.9 us -> 2.95 us
    all_gather x2 -> x0, waiting for transfers between devices: 137 us -> none  [the longest x1 69.8 us: on_device(): value_piece = lax.all_gather(prefix_values, 'blk', axis=0, tiled=True)]
    dot_general x67 -> x0, matrix products: 95.1 us -> none  [the longest x32 43 us: block_partial(): jnp.einsum('rhgp,phd->rhgd', weights.astype(jnp.bfloat16), value_block, p...]
    reduce_scatter x1 -> x0, waiting for transfers between devices: 85.6 us -> none  [on_device(): lax.psum_scatter(projected.astype(jnp.bfloat16), 'tensor', scatter_dimens...]
    pallas_call x0 -> x6, Pallas kernels: none -> 38.6 us  [the longest x3 21.5 us: prefix_partial(): pl.pallas_call(functools.partial(prefix_kernel, groups, tuple(kinds), sta...]
    ppermute x0 -> x20, waiting for transfers between devices: none -> 31.2 us  [the longest x1 10.8 us: on_device(): far = send(both, perm=blk_perm(dx=2))]
    ppermute x0 -> x20, starting transfers between devices: none -> 27.7 us  [the longest x3 6.82 us: on_device(): group = [queries] + [send(queries, perm=blk_perm(dz=d)) for d in (1, 2, 3)]]
    reduce_sum x33 -> x0, other arithmetic: 10.3 us -> none  [the longest x32 10.1 us: block_partial(): totals = jnp.sum(weights, axis=-1)]
  transfers between devices with their start and end apart: 3 -> 20, of which waited for: 3 -> 8; matrix products, arithmetic and copies ran while one was open for 2% -> 1% of each run, Pallas kernels for 0% -> 21%
where the time goes in v1:
time: 105 us
  Pallas kernels  38.6 us (37%)
  waiting for transfers between devices  31.2 us (30%)
  starting transfers between devices  27.7 us (26%)
  local copies, waits for them, and re-layouts  4.21 us (4%)
  other arithmetic  2.95 us (3%)
    pallas_call x3, Pallas kernels, prefix_partial(): pl.pallas_call(functools.partial(prefix_kernel, groups, tuple(kinds), sta...  21.5 us
    pallas_call x2, Pallas kernels, project(): pl.pallas_call(functools.partial(project_kernel, len(inputs) - 2, merge),...  11.5 us
    ppermute x1, waiting for transfers between devices, on_device(): far = send(both, perm=blk_perm(dx=2))  10.8 us
    ppermute x3, waiting for transfers between devices, on_device(): send(parts[d], perm=blk_perm(dz=-d))  6.83 us
    ppermute x3, starting transfers between devices, on_device(): group = [queries] + [send(queries, perm=blk_perm(dz=d)) for d in (1, 2, 3)]  6.82 us
    ppermute x3, starting transfers between devices, on_device(): send(away[d], perm=tensor_perm(dy=d))  5.88 us
    ppermute x3, waiting for transfers between devices, on_device(): group = [queries] + [send(queries, perm=blk_perm(dz=d)) for d in (1, 2, 3)]  5.68 us
    pallas_call x1, Pallas kernels, suffix_partial(): pl.pallas_call(suffix_kernel, grid_spec=pltpu.PrefetchScalarGridSpec(num_...  5.59 us
  transfers between devices with their start and end apart: 20, of which 8 were waited for; matrix products, arithmetic and copies ran while one was open for 1% of the time, Pallas kernels for 21%

profile of v1, /device:TPU:2, one launch (start us, length us, event | category | flops | bytes accessed | tf_op | source)
XLA Modules:
  0.0 104.8 jit_solution(6647283700000179043)
XLA Ops:
  1.0 1.0 constant_dynamic-update-slice_fusion
  2.0 1.6 %collective-permute-start.3 = (bf16[2048,128]{1,0:T(8,128)(2,1)S(1)}, bf16[2048,128]{1,0:T(8,128)(2,1)S(1)}, u32[]{:S(2)}, u32[]{:S(2)}) collective-permute-start(bf16[2048,128]{1,0:T(8,128)(2,1)S(1)} %constant_dynamic-update-slice_fusion), channel_id=1, source_target_pairs={{0,64},{8,72},{16,80},{24,88},{32,96},{40,104},{48,112},{56,120},{... | collective-permute-start | bytes 1572872 | tf_op jit(solution)/shard_map/ppermute | solution.py:272
  4.4 2.0 %collective-permute-start.7 = (bf16[2048,128]{1,0:T(8,128)(2,1)S(1)}, bf16[2048,128]{1,0:T(8,128)(2,1)S(1)}, u32[]{:S(2)}, u32[]{:S(2)}) collective-permute-start(bf16[2048,128]{1,0:T(8,128)(2,1)S(1)} %constant_dynamic-update-slice_fusion), channel_id=1, source_target_pairs={{0,128},{8,136},{16,144},{24,152},{32,160},{40,168},{48,176},{56,1... | collective-permute-start | bytes 1572872 | tf_op jit(solution)/shard_map/ppermute | solution.py:273
  6.4 1.7 %collective-permute-start = (bf16[64,512]{1,0:T(8,128)(2,1)}, bf16[64,512]{1,0:T(8,128)(2,1)S(1)}, u32[]{:S(2)}, u32[]{:S(2)}) collective-permute-start(bf16[64,512]{1,0:T(8,128)(2,1)} %q_ref.1), channel_id=1, source_target_pairs={{0,16},{8,24},{16,32},{24,40},{32,48},{40,56},{48,0},{56,8},{64,80... | collective-permute-start | bytes 196616 | tf_op jit(solution)/shard_map/ppermute | solution.py:274
  8.1 5.7 %collective-permute-done.refs_1_ = bf16[64,512]{1,0:T(8,128)(2,1)S(1)} collective-permute-done((bf16[64,512]{1,0:T(8,128)(2,1)}, bf16[64,512]{1,0:T(8,128)(2,1)S(1)}, u32[]{:S(2)}, u32[]{:S(2)}) %collective-permute-start) | collective-permute-done | bytes 65568 | tf_op jit(solution)/shard_map/ppermute | solution.py:274
  14.2 3.0 %collective-permute-done.3.refs_4_ = bf16[2048,128]{1,0:T(8,128)(2,1)S(1)} collective-permute-done((bf16[2048,128]{1,0:T(8,128)(2,1)S(1)}, bf16[2048,128]{1,0:T(8,128)(2,1)S(1)}, u32[]{:S(2)}, u32[]{:S(2)}) %collective-permute-start.3) | collective-permute-done | bytes 524320 | tf_op jit(solution)/shard_map/ppermute | solution.py:272
  17.9 10.8 %collective-permute-done.7.refs_6_ = bf16[2048,128]{1,0:T(8,128)(2,1)S(1)} collective-permute-done((bf16[2048,128]{1,0:T(8,128)(2,1)S(1)}, bf16[2048,128]{1,0:T(8,128)(2,1)S(1)}, u32[]{:S(2)}, u32[]{:S(2)}) %collective-permute-start.7) | collective-permute-done | bytes 524320 | tf_op jit(solution)/shard_map/ppermute | solution.py:273
  28.8 4.7 %collective-permute-start.2 = (bf16[64,512]{1,0:T(8,128)(2,1)}, bf16[64,512]{1,0:T(8,128)(2,1)S(1)}, u32[]{:S(2)}, u32[]{:S(2)}) collective-permute-start(bf16[64,512]{1,0:T(8,128)(2,1)} %q_ref.1), channel_id=1, source_target_pairs={{0,48},{8,56},{16,0},{24,8},{32,16},{40,24},{48,32},{56,40},{64,11... | collective-permute-start | bytes 196616 | tf_op jit(solution)/shard_map/ppermute | solution.py:274
  33.5 5.6 %shard_map.76 = (f32[64,512]{1,0:T(8,128)}, f32[64,128]{1,0:T(8,128)}) custom-call(s32[64]{0:T(128)} %len_ref.1, bf16[64,512]{1,0:T(8,128)(2,1)} %q_ref.1, bf16[64,128,128]{2,1,0:T(8,128)(2,1)} %k_ref.1, bf16[64,128,128]{2,1,0:T(8,128)(2,1)} %v_ref.1), custom_call_target="tpu_custom_call" | custom-call | flops 268435456 | bytes 4194304 | tf_op jit(solution)/shard_map/pallas_call | solution.py:83
  39.8 5.3 %shard_map.73 = (f32[1024,128]{1,0:T(8,128)}, f32[1024,128]{1,0:T(8,128)}) custom-call(bf16[64,512]{1,0:T(8,128)(2,1)} %q_ref.1, bf16[64,512]{1,0:T(8,128)(2,1)} %copy-done.9, bf16[64,512]{1,0:T(8,128)(2,1)} %copy-done.10, bf16[64,512]{1,0:T(8,128)(2,1)} %copy-done.11, bf16[1024,128]{1,0:T(8,128)(2,1)} %refs_4_.2, bf16[1024,128]{1,0:T(8,128)(2,1)} %refs_5_.1, ...), custom_call_target="tpu_custom_call" | custom-call | flops 2147483648 | bytes 1048576 | tf_op jit(solution)/shard_map/pallas_call | solution.py:187
  45.1 5.9 %shard_map.74 = (f32[1024,128]{1,0:T(8,128)}, f32[1024,128]{1,0:T(8,128)}) custom-call(bf16[64,512]{1,0:T(8,128)(2,1)} %q_ref.1, bf16[64,512]{1,0:T(8,128)(2,1)} %copy-done.9, bf16[64,512]{1,0:T(8,128)(2,1)} %copy-done.10, bf16[64,512]{1,0:T(8,128)(2,1)} %copy-done.11, bf16[2048,128]{1,0:T(8,128)(2,1)} %copy-done.5, bf16[2048,128]{1,0:T(8,128)(2,1)} %copy-done.6, ...), custom_call_target="tpu_custom_call" | custom-call | flops 2147483648 | bytes 1048576 | tf_op jit(solution)/shard_map/pallas_call | solution.py:187
  51.9 10.3 %shard_map.75 = (bf16[64,640]{1,0:T(8,128)(2,1)}, bf16[64,640]{1,0:T(8,128)(2,1)}, bf16[64,640]{1,0:T(8,128)(2,1)}, bf16[64,640]{1,0:T(8,128)(2,1)}) custom-call(bf16[64,512]{1,0:T(8,128)(2,1)} %q_ref.1, bf16[64,512]{1,0:T(8,128)(2,1)} %copy-done.9, bf16[64,512]{1,0:T(8,128)(2,1)} %copy-done.10, bf16[64,512]{1,0:T(8,128)(2,1)} %copy-done.11, ...), custom_call_target="tpu_custom_call" | custom-call | flops 4294967296 | bytes 2097152 | tf_op jit(solution)/shard_map/pallas_call | solution.py:187
  63.1 1.2 %collective-permute-start.12 = (bf16[64,640]{1,0:T(8,128)(2,1)}, bf16[64,640]{1,0:T(8,128)(2,1)S(1)}, u32[]{:S(2)}, u32[]{:S(2)}) collective-permute-start(bf16[64,640]{1,0:T(8,128)(2,1)} %get-tuple-element.31), channel_id=1, source_target_pairs={{0,16},{8,24},{16,32},{24,40},{32,48},{40,56},{48,0},{56,8},{64,80... | collective-permute-start | bytes 245768 | tf_op jit(solution)/shard_map/ppermute | solution.py:283
  64.9 3.0 %collective-permute-done.10.refs_1_ = bf16[64,640]{1,0:T(8,128)(2,1)S(1)} collective-permute-done((bf16[64,640]{1,0:T(8,128)(2,1)}, bf16[64,640]{1,0:T(8,128)(2,1)S(1)}, u32[]{:S(2)}, u32[]{:S(2)}) %collective-permute-start.10) | collective-permute-done | bytes 81952 | tf_op jit(solution)/shard_map/ppermute | solution.py:283
  67.9 3.8 %collective-permute-done.11.refs_2_ = bf16[64,640]{1,0:T(8,128)(2,1)S(1)} collective-permute-done((bf16[64,640]{1,0:T(8,128)(2,1)}, bf16[64,640]{1,0:T(8,128)(2,1)S(1)}, u32[]{:S(2)}, u32[]{:S(2)}) %collective-permute-start.11) | collective-permute-done | bytes 81952 | tf_op jit(solution)/shard_map/ppermute | solution.py:283
  72.4 6.3 %shard_map.77 = (f32[64,1024]{1,0:T(8,128)}, bf16[64,1024]{1,0:T(8,128)(2,1)}, bf16[64,1024]{1,0:T(8,128)(2,1)}, bf16[64,1024]{1,0:T(8,128)(2,1)}, bf16[64,512]{1,0:T(8,128)(2,1)}) custom-call(s32[4]{0:T(128)} %broadcast_add_fusion.index_ref, bf16[64,640]{1,0:T(8,128)(2,1)} %get-tuple-element.28.refs_0_, bf16[64,640]{1,0:T(8,128)(2,1)} %copy-done.1, ...), custom_call_target="tpu_custom_call" | custom-call | flops 268435456 | bytes 4194304 | tf_op jit(solution)/shard_map/pallas_call | solution.py:252
  78.7 1.6 %collective-permute-start.16 = (bf16[64,1024]{1,0:T(8,128)(2,1)}, bf16[64,1024]{1,0:T(8,128)(2,1)S(1)}, u32[]{:S(2)}, u32[]{:S(2)}) collective-permute-start(bf16[64,1024]{1,0:T(8,128)(2,1)} %get-tuple-element.40), channel_id=1, source_target_pairs={{0,1},{1,2},{2,3},{3,0},{4,5},{5,6},{6,7},{7,4},{8,9},{9,10},{10,1... | collective-permute-start | bytes 393224 | tf_op jit(solution)/shard_map/ppermute | solution.py:290
  80.4 2.9 %collective-permute-start.17 = (bf16[64,1024]{1,0:T(8,128)(2,1)}, bf16[64,1024]{1,0:T(8,128)(2,1)S(1)}, u32[]{:S(2)}, u32[]{:S(2)}) collective-permute-start(bf16[64,1024]{1,0:T(8,128)(2,1)} %get-tuple-element.41), channel_id=1, source_target_pairs={{0,2},{1,3},{2,0},{3,1},{4,6},{5,7},{6,4},{7,5},{8,10},{9,11},{10,... | collective-permute-start | bytes 393224 | tf_op jit(solution)/shard_map/ppermute | solution.py:290
  83.2 1.3 %collective-permute-start.18 = (bf16[64,1024]{1,0:T(8,128)(2,1)}, bf16[64,1024]{1,0:T(8,128)(2,1)S(1)}, u32[]{:S(2)}, u32[]{:S(2)}) collective-permute-start(bf16[64,1024]{1,0:T(8,128)(2,1)} %get-tuple-element.42), channel_id=1, source_target_pairs={{0,3},{1,0},{2,1},{3,2},{4,7},{5,4},{6,5},{7,6},{8,11},{9,8},{10,9... | collective-permute-start | bytes 393224 | tf_op jit(solution)/shard_map/ppermute | solution.py:290
  85.2 5.2 %shard_map.78 = (f32[64,1024]{1,0:T(8,128)}, bf16[64,1024]{1,0:T(8,128)(2,1)}, bf16[64,1024]{1,0:T(8,128)(2,1)}, bf16[64,1024]{1,0:T(8,128)(2,1)}) custom-call(s32[4]{0:T(128)} %fusion.1.index_ref, bf16[64,512]{1,0:T(8,128)(2,1)} %get-tuple-element.34.refs_0_, bf16[512,8192]{1,0:T(8,128)(2,1)} %refs_4_.3, bf16[512,8192]{1,0:T(8,128)(2,1)} %refs_4_.3, ...), custom_call_target="tpu_custom_call" | custom-call | flops 268435456 | bytes 4194304 | tf_op jit(solution)/shard_map/pallas_call | solution.py:252
  91.9 2.0 %collective-permute-start.15 = (bf16[64,1024]{1,0:T(8,128)(2,1)}, bf16[64,1024]{1,0:T(8,128)(2,1)S(1)}, u32[]{:S(2)}, u32[]{:S(2)}) collective-permute-start(bf16[64,1024]{1,0:T(8,128)(2,1)} %get-tuple-element.38), channel_id=1, source_target_pairs={{0,3},{1,0},{2,1},{3,2},{4,7},{5,4},{6,5},{7,6},{8,11},{9,8},{10,9... | collective-permute-start | bytes 393224 | tf_op jit(solution)/shard_map/ppermute | solution.py:292
  94.0 5.0 %collective-permute-start.19 = (bf16[64,1024]{1,0:T(8,128)(2,1)S(1)}, bf16[64,1024]{1,0:T(8,128)(2,1)S(1)}, u32[]{:S(2)}, u32[]{:S(2)}) collective-permute-start(bf16[64,1024]{1,0:T(8,128)(2,1)S(1)} %add_convert_fusion.1), channel_id=1, source_target_pairs={{0,4},{1,5},{2,6},{3,7},{4,0},{5,1},{6,2},{7,3},{8,12},{9,13},{10,... | collective-permute-start | bytes 393224 | tf_op jit(solution)/shard_map/ppermute | solution.py:297
  99.2 3.9 %collective-permute-done.19 = bf16[64,1024]{1,0:T(8,128)(2,1)S(1)} collective-permute-done((bf16[64,1024]{1,0:T(8,128)(2,1)S(1)}, bf16[64,1024]{1,0:T(8,128)(2,1)S(1)}, u32[]{:S(2)}, u32[]{:S(2)}) %collective-permute-start.19) | collective-permute-done | bytes 131104 | tf_op jit(solution)/shard_map/ppermute | solution.py:297
  103.1 1.7 %add_convert_fusion = bf16[64,1024]{1,0:T(8,128)(2,1)} fusion(bf16[64,1024]{1,0:T(8,128)(2,1)S(1)} %collective-permute-done.19, bf16[64,1024]{1,0:T(8,128)(2,1)S(1)} %collective-permute-done.15, bf16[64,1024]{1,0:T(8,128)(2,1)S(1)} %collective-permute-done.14, f32[64,1024]{1,0:T(8,128)} %get-tuple-element.35, bf16[64,1024]{1,0:T(8,128)(2,1)S(1)} %collective-permute-done.13), kind=kLoop, calls=%fused_computation | loop fusion | flops 589824 | bytes 917504 | tf_op jit(solution)/shard_map/convert_element_type | solution.py:298
  (52 shorter events, 9.0 us)
Async XLA Ops:
  2.0 15.2 %collective-permute-start.3 = (bf16[2048,128]{1,0:T(8,128)(2,1)S(1)}, bf16[2048,128]{1,0:T(8,128)(2,1)S(1)}, u32[]{:S(2)}, u32[]{:S(2)}) collective-permute-start(bf16[2048,128]{1,0:T(8,128)(2,1)S(1)} %constant_dynamic-update-slice_fusion), channel_id=1, source_target_pairs={{0,64},{8,72},{16,80},{24,88},{32,96},{40,104},{48,112},{56,120},{... | collective-permute-start | bytes 1572872 | tf_op jit(solution)/shard_map/ppermute | solution.py:272
  3.5 14.4 %collective-permute-start.5 = (bf16[2048,128]{1,0:T(8,128)(2,1)S(1)}, bf16[2048,128]{1,0:T(8,128)(2,1)S(1)}, u32[]{:S(2)}, u32[]{:S(2)}) collective-permute-start(bf16[2048,128]{1,0:T(8,128)(2,1)S(1)} %constant_dynamic-update-slice_fusion), channel_id=1, source_target_pairs={{0,192},{8,200},{16,208},{24,216},{32,224},{40,232},{48,240},{56,2... | collective-permute-start | bytes 1572872 | tf_op jit(solution)/shard_map/ppermute | solution.py:272
  4.4 24.4 %collective-permute-start.7 = (bf16[2048,128]{1,0:T(8,128)(2,1)S(1)}, bf16[2048,128]{1,0:T(8,128)(2,1)S(1)}, u32[]{:S(2)}, u32[]{:S(2)}) collective-permute-start(bf16[2048,128]{1,0:T(8,128)(2,1)S(1)} %constant_dynamic-update-slice_fusion), channel_id=1, source_target_pairs={{0,128},{8,136},{16,144},{24,152},{32,160},{40,168},{48,176},{56,1... | collective-permute-start | bytes 1572872 | tf_op jit(solution)/shard_map/ppermute | solution.py:273
  6.4 32.8 %collective-permute-start.9 = (bf16[2048,128]{1,0:T(8,128)(2,1)S(1)}, bf16[2048,128]{1,0:T(8,128)(2,1)}, u32[]{:S(2)}, u32[]{:S(2)}) collective-permute-start(bf16[2048,128]{1,0:T(8,128)(2,1)S(1)} %constant_dynamic-update-slice_fusion), channel_id=1, source_target_pairs={{0,8},{8,0},{16,24},{24,16},{32,40},{40,32},{48,56},{56,48},{64,72... | collective-permute-start | bytes 1572872 | tf_op jit(solution)/shard_map/ppermute | solution.py:271
  6.4 7.4 %collective-permute-start = (bf16[64,512]{1,0:T(8,128)(2,1)}, bf16[64,512]{1,0:T(8,128)(2,1)S(1)}, u32[]{:S(2)}, u32[]{:S(2)}) collective-permute-start(bf16[64,512]{1,0:T(8,128)(2,1)} %q_ref.1), channel_id=1, source_target_pairs={{0,16},{8,24},{16,32},{24,40},{32,48},{40,56},{48,0},{56,8},{64,80... | collective-permute-start | bytes 196616 | tf_op jit(solution)/shard_map/ppermute | solution.py:274
  13.8 25.3 %copy-start.9 = (bf16[64,512]{1,0:T(8,128)(2,1)}, bf16[64,512]{1,0:T(8,128)(2,1)S(1)}, u32[]{:S(2)}) copy-start(bf16[64,512]{1,0:T(8,128)(2,1)S(1)} %collective-permute-done.refs_1_) | copy-start | bytes 196612
  13.8 15.0 %collective-permute-start.1 = (bf16[64,512]{1,0:T(8,128)(2,1)}, bf16[64,512]{1,0:T(8,128)(2,1)S(1)}, u32[]{:S(2)}, u32[]{:S(2)}) collective-permute-start(bf16[64,512]{1,0:T(8,128)(2,1)} %q_ref.1), channel_id=1, source_target_pairs={{0,32},{8,40},{16,48},{24,56},{32,0},{40,8},{48,16},{56,24},{64,96... | collective-permute-start | bytes 196616 | tf_op jit(solution)/shard_map/ppermute | solution.py:274
  17.1 22.0 %copy-start.5 = (bf16[2048,128]{1,0:T(8,128)(2,1)}, bf16[2048,128]{1,0:T(8,128)(2,1)S(1)}, u32[]{:S(2)}) copy-start(bf16[2048,128]{1,0:T(8,128)(2,1)S(1)} %collective-permute-done.3.refs_4_) | copy-start | bytes 1572868
  17.1 33.8 %collective-permute-start.4 = (bf16[2048,128]{1,0:T(8,128)(2,1)S(1)}, bf16[2048,128]{1,0:T(8,128)(2,1)S(1)}, u32[]{:S(2)}, u32[]{:S(2)}) collective-permute-start(bf16[2048,128]{1,0:T(8,128)(2,1)S(1)} %collective-permute-done.3.refs_4_), channel_id=1, source_target_pairs={{0,8},{8,0},{16,24},{24,16},{32,40},{40,32},{48,56},{56,48},{64,72... | collective-permute-start | bytes 1572872 | tf_op jit(solution)/shard_map/ppermute | solution.py:279
  17.9 21.2 %copy-start.6 = (bf16[2048,128]{1,0:T(8,128)(2,1)}, bf16[2048,128]{1,0:T(8,128)(2,1)S(1)}, u32[]{:S(2)}) copy-start(bf16[2048,128]{1,0:T(8,128)(2,1)S(1)} %collective-permute-done.5.refs_5_) | copy-start | bytes 1572868
  17.9 33.0 %collective-permute-start.6 = (bf16[2048,128]{1,0:T(8,128)(2,1)S(1)}, bf16[2048,128]{1,0:T(8,128)(2,1)S(1)}, u32[]{:S(2)}, u32[]{:S(2)}) collective-permute-start(bf16[2048,128]{1,0:T(8,128)(2,1)S(1)} %collective-permute-done.5.refs_5_), channel_id=1, source_target_pairs={{0,8},{8,0},{16,24},{24,16},{32,40},{40,32},{48,56},{56,48},{64,72... | collective-permute-start | bytes 1572872 | tf_op jit(solution)/shard_map/ppermute | solution.py:279
  28.8 10.3 %copy-start.4 = (bf16[2048,128]{1,0:T(8,128)(2,1)}, bf16[2048,128]{1,0:T(8,128)(2,1)S(1)}, u32[]{:S(2)}) copy-start(bf16[2048,128]{1,0:T(8,128)(2,1)S(1)} %collective-permute-done.7.refs_6_) | copy-start | bytes 1572868
  28.8 22.2 %collective-permute-start.8 = (bf16[2048,128]{1,0:T(8,128)(2,1)S(1)}, bf16[2048,128]{1,0:T(8,128)(2,1)}, u32[]{:S(2)}, u32[]{:S(2)}) collective-permute-start(bf16[2048,128]{1,0:T(8,128)(2,1)S(1)} %collective-permute-done.7.refs_6_), channel_id=1, source_target_pairs={{0,8},{8,0},{16,24},{24,16},{32,40},{40,32},{48,56},{56,48},{64,72... | collective-permute-start | bytes 1572872 | tf_op jit(solution)/shard_map/ppermute | solution.py:281
  28.8 10.3 %collective-permute-start.2 = (bf16[64,512]{1,0:T(8,128)(2,1)}, bf16[64,512]{1,0:T(8,128)(2,1)S(1)}, u32[]{:S(2)}, u32[]{:S(2)}) collective-permute-start(bf16[64,512]{1,0:T(8,128)(2,1)} %q_ref.1), channel_id=1, source_target_pairs={{0,48},{8,56},{16,0},{24,8},{32,16},{40,24},{48,32},{56,40},{64,11... | collective-permute-start | bytes 196616 | tf_op jit(solution)/shard_map/ppermute | solution.py:274
  62.3 5.6 %collective-permute-start.10 = (bf16[64,640]{1,0:T(8,128)(2,1)}, bf16[64,640]{1,0:T(8,128)(2,1)S(1)}, u32[]{:S(2)}, u32[]{:S(2)}) collective-permute-start(bf16[64,640]{1,0:T(8,128)(2,1)} %get-tuple-element.29), channel_id=1, source_target_pairs={{0,48},{8,56},{16,0},{24,8},{32,16},{40,24},{48,32},{56,40},{64,11... | collective-permute-start | bytes 245768 | tf_op jit(solution)/shard_map/ppermute | solution.py:283
  63.1 8.6 %collective-permute-start.11 = (bf16[64,640]{1,0:T(8,128)(2,1)}, bf16[64,640]{1,0:T(8,128)(2,1)S(1)}, u32[]{:S(2)}, u32[]{:S(2)}) collective-permute-start(bf16[64,640]{1,0:T(8,128)(2,1)} %get-tuple-element.30), channel_id=1, source_target_pairs={{0,32},{8,40},{16,48},{24,56},{32,0},{40,8},{48,16},{56,24},{64,96... | collective-permute-start | bytes 245768 | tf_op jit(solution)/shard_map/ppermute | solution.py:283
  63.1 8.6 %collective-permute-start.12 = (bf16[64,640]{1,0:T(8,128)(2,1)}, bf16[64,640]{1,0:T(8,128)(2,1)S(1)}, u32[]{:S(2)}, u32[]{:S(2)}) collective-permute-start(bf16[64,640]{1,0:T(8,128)(2,1)} %get-tuple-element.31), channel_id=1, source_target_pairs={{0,16},{8,24},{16,32},{24,40},{32,48},{40,56},{48,0},{56,8},{64,80... | collective-permute-start | bytes 245768 | tf_op jit(solution)/shard_map/ppermute | solution.py:283
  78.7 13.2 %collective-permute-start.16 = (bf16[64,1024]{1,0:T(8,128)(2,1)}, bf16[64,1024]{1,0:T(8,128)(2,1)S(1)}, u32[]{:S(2)}, u32[]{:S(2)}) collective-permute-start(bf16[64,1024]{1,0:T(8,128)(2,1)} %get-tuple-element.40), channel_id=1, source_target_pairs={{0,1},{1,2},{2,3},{3,0},{4,5},{5,6},{6,7},{7,4},{8,9},{9,10},{10,1... | collective-permute-start | bytes 393224 | tf_op jit(solution)/shard_map/ppermute | solution.py:290
  80.4 13.6 %collective-permute-start.17 = (bf16[64,1024]{1,0:T(8,128)(2,1)}, bf16[64,1024]{1,0:T(8,128)(2,1)S(1)}, u32[]{:S(2)}, u32[]{:S(2)}) collective-permute-start(bf16[64,1024]{1,0:T(8,128)(2,1)} %get-tuple-element.41), channel_id=1, source_target_pairs={{0,2},{1,3},{2,0},{3,1},{4,6},{5,7},{6,4},{7,5},{8,10},{9,11},{10,... | collective-permute-start | bytes 393224 | tf_op jit(solution)/shard_map/ppermute | solution.py:290
  83.2 10.7 %collective-permute-start.18 = (bf16[64,1024]{1,0:T(8,128)(2,1)}, bf16[64,1024]{1,0:T(8,128)(2,1)S(1)}, u32[]{:S(2)}, u32[]{:S(2)}) collective-permute-start(bf16[64,1024]{1,0:T(8,128)(2,1)} %get-tuple-element.42), channel_id=1, source_target_pairs={{0,3},{1,0},{2,1},{3,2},{4,7},{5,4},{6,5},{7,6},{8,11},{9,8},{10,9... | collective-permute-start | bytes 393224 | tf_op jit(solution)/shard_map/ppermute | solution.py:290
  90.4 8.6 %collective-permute-start.13 = (bf16[64,1024]{1,0:T(8,128)(2,1)}, bf16[64,1024]{1,0:T(8,128)(2,1)S(1)}, u32[]{:S(2)}, u32[]{:S(2)}) collective-permute-start(bf16[64,1024]{1,0:T(8,128)(2,1)} %get-tuple-element.36), channel_id=1, source_target_pairs={{0,1},{1,2},{2,3},{3,0},{4,5},{5,6},{6,7},{7,4},{8,9},{9,10},{10,1... | collective-permute-start | bytes 393224 | tf_op jit(solution)/shard_map/ppermute | solution.py:292
  91.1 7.9 %collective-permute-start.14 = (bf16[64,1024]{1,0:T(8,128)(2,1)}, bf16[64,1024]{1,0:T(8,128)(2,1)S(1)}, u32[]{:S(2)}, u32[]{:S(2)}) collective-permute-start(bf16[64,1024]{1,0:T(8,128)(2,1)} %get-tuple-element.37), channel_id=1, source_target_pairs={{0,2},{1,3},{2,0},{3,1},{4,6},{5,7},{6,4},{7,5},{8,10},{9,11},{10,... | collective-permute-start | bytes 393224 | tf_op jit(solution)/shard_map/ppermute | solution.py:292
  91.9 7.2 %collective-permute-start.15 = (bf16[64,1024]{1,0:T(8,128)(2,1)}, bf16[64,1024]{1,0:T(8,128)(2,1)S(1)}, u32[]{:S(2)}, u32[]{:S(2)}) collective-permute-start(bf16[64,1024]{1,0:T(8,128)(2,1)} %get-tuple-element.38), channel_id=1, source_target_pairs={{0,3},{1,0},{2,1},{3,2},{4,7},{5,4},{6,5},{7,6},{8,11},{9,8},{10,9... | collective-permute-start | bytes 393224 | tf_op jit(solution)/shard_map/ppermute | solution.py:292
  94.0 9.1 %collective-permute-start.19 = (bf16[64,1024]{1,0:T(8,128)(2,1)S(1)}, bf16[64,1024]{1,0:T(8,128)(2,1)S(1)}, u32[]{:S(2)}, u32[]{:S(2)}) collective-permute-start(bf16[64,1024]{1,0:T(8,128)(2,1)S(1)} %add_convert_fusion.1), channel_id=1, source_target_pairs={{0,4},{1,5},{2,6},{3,7},{4,0},{5,1},{6,2},{7,3},{8,12},{9,13},{10,... | collective-permute-start | bytes 393224 | tf_op jit(solution)/shard_map/ppermute | solution.py:297
  (8 other events, 26.6 us)

commit v2 on v1

--- a/solution.py
+++ b/solution.py
@@ -15,7 +15,6 @@
 SCALE2 = LOG2E / math.sqrt(DH)
 F32 = jnp.float32
 BF16 = jnp.bfloat16
-VMEM_LIMIT = 56 << 20
 
 NX, NZ, NC = 4, 4, 2
 NH, NY = 2, 4
@@ -37,12 +36,12 @@
     ]
 
 
-def params():
-    return pltpu.CompilerParams(vmem_limit_bytes=VMEM_LIMIT)
-
-
-def cost(flops, nbytes, transcendentals=0):
-    return pl.CostEstimate(flops=flops, bytes_accessed=nbytes, transcendentals=transcendentals)
+def params(mib):
+    return pltpu.CompilerParams(vmem_limit_bytes=mib << 20)
+
+
+def cost(micros):
+    return pl.CostEstimate(flops=int(micros * 1.1e9), bytes_accessed=1 << 20, transcendentals=0)
 
 
 def heads_of(q):
@@ -99,9 +98,34 @@
             jax.ShapeDtypeStruct((rows, WIDTH), F32),
             jax.ShapeDtypeStruct((rows, DH), F32),
         ],
-        compiler_params=params(),
-        cost_estimate=cost(4 * rows * WIDTH * slots * SUB, 4 * rows * slots * DH),
+        compiler_params=params(12),
+        cost_estimate=cost(3.0),
     )(lengths, q, sk, sv)
+
+
+def stack_kernel(a_ref, b_ref, o_ref, sems):
+    rows = a_ref.shape[0]
+    copies = [
+        pltpu.make_async_copy(ref, o_ref.at[pl.ds(i * rows, rows)], sems.at[i])
+        for i, ref in enumerate((a_ref, b_ref))
+    ]
+    for copy in copies:
+        copy.start()
+    for copy in copies:
+        copy.wait()
+
+
+def stacked(a, b):
+    rows, width = a.shape
+    return pl.pallas_call(
+        stack_kernel,
+        in_specs=[pl.BlockSpec(memory_space=pl.ANY)] * 2,
+        out_specs=pl.BlockSpec(memory_space=pltpu.VMEM),
+        out_shape=jax.ShapeDtypeStruct((2 * rows, width), a.dtype),
+        scratch_shapes=[pltpu.SemaphoreType.DMA((2,))],
+        compiler_params=params(4),
+        cost_estimate=cost(0.8),
+    )(a, b)
 
 
 def prefix_kernel(groups, blocks, first, last, *refs):
@@ -187,8 +211,8 @@
     return pl.pallas_call(
         functools.partial(prefix_kernel, groups, tuple(kinds), state is None, last),
         out_shape=outs,
-        compiler_params=params(),
-        cost_estimate=cost(8 * all_rows * DH * keys, 4 * keys * DH, all_rows * keys),
+        compiler_params=params(16),
+        cost_estimate=cost(0.5 + 1.4e-6 * all_rows * keys),
     )(*queries, *arrays, *(state or ()))
 
 
@@ -232,7 +256,7 @@
 STEPS = 4
 
 
-def project(index, inputs, weight, merge):
+def project(index, first, inputs, weight, merge):
     rows = inputs[0].shape[0]
     depth, columns = weight.shape
     piece = columns // (NH * NY)
@@ -242,7 +266,7 @@
         return pl.BlockSpec(a.shape, lambda i, _: (0, 0))
 
     def block(k):
-        return pl.BlockSpec((depth, tile), lambda i, at: (0, at[k] * STEPS + i))
+        return pl.BlockSpec((depth, tile), lambda i, at: (0, at[first + k] * STEPS + i))
 
     out_shape = [jax.ShapeDtypeStruct((rows, piece), F32 if k == 0 else BF16) for k in range(NY)]
     out_specs = [pl.BlockSpec((rows, tile), lambda i, _: (0, i)) for _ in range(NY)]
@@ -258,37 +282,43 @@
             out_specs=out_specs,
         ),
         out_shape=out_shape,
-        compiler_params=params(),
-        cost_estimate=cost(2 * rows * depth * piece * NY, 2 * depth * piece * NY),
+        compiler_params=params(12),
+        cost_estimate=cost(3.0),
     )(index, *inputs, *([weight] * NY))
 
 
 def on_device(
     queries, prefix_keys, prefix_values, suffix_keys, suffix_values, suffix_lengths, out_weight
 ):
+    here = lax.axis_index("tensor").astype(jnp.int32)
+    step = jnp.arange(NH * NY, dtype=jnp.int32)
+    index = (here + NY * (1 - step // NY)) // NY % NH * NY + (here + step) % NY
+
     send = functools.partial(lax.ppermute, axis_name="blk")
-    both = jnp.concatenate([prefix_keys, prefix_values], axis=0)
+    group = [queries] + [send(queries, perm=blk_perm(dz=d)) for d in (1, 2, 3)]
+    both = stacked(prefix_keys, prefix_values)
+    near = [send(both, perm=blk_perm(dx=d)) for d in (1, 3)]
     peer = send(both, perm=blk_perm(dc=1))
-    near = [send(both, perm=blk_perm(dx=d)) for d in (1, 3)]
     far = send(both, perm=blk_perm(dx=2))
-    group = [queries] + [send(queries, perm=blk_perm(dz=d)) for d in (1, 2, 3)]
-
+
+    together = lax.optimization_barrier
     mixed, lse = suffix_partial(queries, suffix_keys, suffix_values, suffix_lengths)
-
+    peer, lse, index = together((peer, lse, index))
     state = prefix_partial(group, [(prefix_keys, prefix_values), peer], None, False)
+    near, state = together((near, state))
     near_peer = [send(b, perm=blk_perm(dc=1)) for b in near]
     state = prefix_partial(group, near, state, False)
+    far, state = together((far, state))
     far_peer = send(far, perm=blk_perm(dc=1))
-    parts = prefix_partial(group, near_peer + [far, far_peer], state, True)
+    state = prefix_partial(group, near_peer, state, False)
+    far_peer, state = together((far_peer, state))
+    parts = prefix_partial(group, [far, far_peer], state, True)
     parts = [parts[0]] + [send(parts[d], perm=blk_perm(dz=-d)) for d in (1, 2, 3)]
 
-    here = lax.axis_index("tensor")
-    half, line = here // NY, here % NY
-    lines = (line + jnp.arange(NY, dtype=jnp.int32)) % NY
     send = functools.partial(lax.ppermute, axis_name="tensor")
-    *away, attention = project((NH - 1 - half) * NY + lines, parts + [mixed, lse], out_weight, True)
+    *away, attention = project(index, 0, parts + [mixed, lse], out_weight, True)
     away = [away[0]] + [send(away[d], perm=tensor_perm(dy=d)) for d in (1, 2, 3)]
-    home = project(half * NY + lines, [attention], out_weight, False)
+    home = project(index, NY, [attention], out_weight, False)
     home = [home[0]] + [send(home[d], perm=tensor_perm(dy=d)) for d in (1, 2, 3)]
 
     def summed(pieces):

time: 105 us -> 82.6 us (0.79)
  the two profiles are of different devices: /device:TPU:2 before, /device:TPU:6 now
where the time goes in v2:
time: 82.6 us; the launch traced here: 82.4 us
  starting transfers between devices  28.1 us (34%)
  waiting for transfers between devices  24.9 us (30%)
  Pallas kernels  24 us (29%)
  local copies, waits for them, and re-layouts  4.33 us (5%)
    pallas_call x4, Pallas kernels, prefix_partial(): pl.pallas_call(functools.partial(prefix_kernel, groups, tuple(kinds), sta...  14.7 us
    ppermute x2, waiting for transfers between devices, on_device(): near = [send(both, perm=blk_perm(dx=d)) for d in (1, 3)]  11.8 us
    ppermute x3, waiting for transfers between devices, on_device(): send(parts[d], perm=blk_perm(dz=-d))  8.06 us
    pallas_call x2, Pallas kernels, project(): pl.pallas_call(functools.partial(project_kernel, len(inputs) - 2, merge),...  6.33 us
    ppermute x3, starting transfers between devices, on_device(): group = [queries] + [send(queries, perm=blk_perm(dz=d)) for d in (1, 2, 3)]  6.26 us
    ppermute x1, starting transfers between devices, on_device(): other = send(summed(away).astype(BF16), perm=tensor_perm(dh=1))  6.02 us
    ppermute x3, starting transfers between devices, on_device(): send(away[d], perm=tensor_perm(dy=d))  5.4 us
    unnamed x20, local copies, waits for them, and re-layouts  4.33 us
  transfers between devices with their start and end apart: 20, of which 6 were waited for; matrix products, arithmetic and copies ran while one was open for 0% of the time, Pallas kernels for 19%

profile of v2, /device:TPU:6, one launch (start us, length us, event | category | flops | bytes accessed | tf_op | source)
XLA Modules:
  0.0 82.4 jit_solution(144170811442898301)
XLA Ops:
  2.9 1.9 %collective-permute-start.1 = (bf16[64,512]{1,0:T(8,128)(2,1)S(1)}, bf16[64,512]{1,0:T(8,128)(2,1)S(1)}, u32[]{:S(2)}, u32[]{:S(2)}) collective-permute-start(bf16[64,512]{1,0:T(8,128)(2,1)S(1)} %copy-done.6), channel_id=1, source_target_pairs={{0,16},{8,24},{16,32},{24,40},{32,48},{40,56},{48,0},{56,8},{64,80... | collective-permute-start | bytes 196616 | tf_op jit(solution)/shard_map/ppermute | solution.py:298
  4.8 3.3 %collective-permute-start.2 = (bf16[64,512]{1,0:T(8,128)(2,1)S(1)}, bf16[64,512]{1,0:T(8,128)(2,1)S(1)}, u32[]{:S(2)}, u32[]{:S(2)}) collective-permute-start(bf16[64,512]{1,0:T(8,128)(2,1)S(1)} %copy-done.6), channel_id=1, source_target_pairs={{0,32},{8,40},{16,48},{24,56},{32,0},{40,8},{48,16},{56,24},{64,96... | collective-permute-start | bytes 196616 | tf_op jit(solution)/shard_map/ppermute | solution.py:298
  8.6 1.5 %collective-permute-start.6 = (bf16[2048,128]{1,0:T(8,128)(2,1)S(1)}, bf16[2048,128]{1,0:T(8,128)(2,1)S(1)}, u32[]{:S(2)}, u32[]{:S(2)}) collective-permute-start(bf16[2048,128]{1,0:T(8,128)(2,1)S(1)} %shard_map.73), channel_id=1, source_target_pairs={{0,192},{8,200},{16,208},{24,216},{32,224},{40,232},{48,240},{56,2... | collective-permute-start | bytes 1572872 | tf_op jit(solution)/shard_map/ppermute | solution.py:300
  10.1 1.6 %copy-done.1 = bf16[64,128,128]{2,1,0:T(8,128)(2,1)S(1)} copy-done((bf16[64,128,128]{2,1,0:T(8,128)(2,1)S(1)}, bf16[64,128,128]{2,1,0:T(8,128)(2,1)}, u32[]{:S(2)}) %copy-start.1) | copy-done | bytes 2097176
  11.7 2.9 %shard_map.74 = (f32[64,512]{1,0:T(8,128)S(1)}, f32[64,128]{1,0:T(8,128)S(1)}) custom-call(s32[64]{0:T(128)S(1)} %copy-done.7, bf16[64,512]{1,0:T(8,128)(2,1)S(1)} %copy-done.6, bf16[64,128,128]{2,1,0:T(8,128)(2,1)S(1)} %copy-done, bf16[64,128,128]{2,1,0:T(8,128)(2,1)S(1)} %copy-done.1), custom_call_target="tpu_custom_call" | custom-call | flops 3300000000 | bytes 1048576 | tf_op jit(solution)/shard_map/pallas_call | solution.py:82
  15.7 1.5 %collective-permute-start.4 = (bf16[2048,128]{1,0:T(8,128)(2,1)S(1)}, bf16[2048,128]{1,0:T(8,128)(2,1)S(1)}, u32[]{:S(2)}, u32[]{:S(2)}) collective-permute-start(bf16[2048,128]{1,0:T(8,128)(2,1)S(1)} %shard_map.73), channel_id=1, source_target_pairs={{0,128},{8,136},{16,144},{24,152},{32,160},{40,168},{48,176},{56,1... | collective-permute-start | bytes 1572872 | tf_op jit(solution)/shard_map/ppermute | solution.py:302
  17.2 1.7 %collective-permute-done.3.refs_3_ = bf16[64,512]{1,0:T(8,128)(2,1)S(1)} collective-permute-done((bf16[64,512]{1,0:T(8,128)(2,1)S(1)}, bf16[64,512]{1,0:T(8,128)(2,1)S(1)}, u32[]{:S(2)}, u32[]{:S(2)}) %collective-permute-start.3) | collective-permute-done | bytes 65568 | tf_op jit(solution)/shard_map/ppermute | solution.py:298
  19.0 3.0 %shard_map.75 = (f32[1024,128]{1,0:T(8,128)S(1)}, f32[1024,128]{1,0:T(8,128)S(1)}) custom-call(bf16[64,512]{1,0:T(8,128)(2,1)S(1)} %copy-done.6, bf16[64,512]{1,0:T(8,128)(2,1)S(1)} %collective-permute-done.1.refs_1_, bf16[64,512]{1,0:T(8,128)(2,1)S(1)} %collective-permute-done.2.refs_2_, bf16[64,512]{1,0:T(8,128)(2,1)S(1)} %collective-permute-done.3.refs_3_, ...), custom_call_target="tpu_custom_call" | custom-call | flops 3779614208 | bytes 1048576 | tf_op jit(solution)/shard_map/pallas_call | solution.py:211
  22.9 10.9 %collective-permute-done.6.refs_5_ = bf16[2048,128]{1,0:T(8,128)(2,1)S(1)} collective-permute-done((bf16[2048,128]{1,0:T(8,128)(2,1)S(1)}, bf16[2048,128]{1,0:T(8,128)(2,1)S(1)}, u32[]{:S(2)}, u32[]{:S(2)}) %collective-permute-start.6) | collective-permute-done | bytes 524320 | tf_op jit(solution)/shard_map/ppermute | solution.py:300
  34.3 3.4 %shard_map.76 = (f32[1024,128]{1,0:T(8,128)S(1)}, f32[1024,128]{1,0:T(8,128)S(1)}) custom-call(bf16[64,512]{1,0:T(8,128)(2,1)S(1)} %copy-done.6, bf16[64,512]{1,0:T(8,128)(2,1)S(1)} %collective-permute-done.1.refs_1_, bf16[64,512]{1,0:T(8,128)(2,1)S(1)} %collective-permute-done.2.refs_2_, bf16[64,512]{1,0:T(8,128)(2,1)S(1)} %collective-permute-done.3.refs_3_, ...), custom_call_target="tpu_custom_call" | custom-call | flops 3779614208 | bytes 1048576 | tf_op jit(solution)/shard_map/pallas_call | solution.py:211
  37.9 3.5 %shard_map.77 = (f32[1024,128]{1,0:T(8,128)S(1)}, f32[1024,128]{1,0:T(8,128)S(1)}) custom-call(bf16[64,512]{1,0:T(8,128)(2,1)S(1)} %copy-done.6, bf16[64,512]{1,0:T(8,128)(2,1)S(1)} %collective-permute-done.1.refs_1_, bf16[64,512]{1,0:T(8,128)(2,1)S(1)} %collective-permute-done.2.refs_2_, bf16[64,512]{1,0:T(8,128)(2,1)S(1)} %collective-permute-done.3.refs_3_, ...), custom_call_target="tpu_custom_call" | custom-call | flops 3779614208 | bytes 1048576 | tf_op jit(solution)/shard_map/pallas_call | solution.py:211
  41.5 4.7 %shard_map.78 = (bf16[64,640]{1,0:T(8,128)(2,1)S(1)}, bf16[64,640]{1,0:T(8,128)(2,1)S(1)}, bf16[64,640]{1,0:T(8,128)(2,1)S(1)}, bf16[64,640]{1,0:T(8,128)(2,1)S(1)}) custom-call(bf16[64,512]{1,0:T(8,128)(2,1)S(1)} %copy-done.6, bf16[64,512]{1,0:T(8,128)(2,1)S(1)} %collective-permute-done.1.refs_1_, bf16[64,512]{1,0:T(8,128)(2,1)S(1)} %collective-permute-done.2.refs_2_, ...), custom_call_target="tpu_custom_call" | custom-call | flops 3779614208 | bytes 1048576 | tf_op jit(solution)/shard_map/pallas_call | solution.py:211
  46.2 1.3 %collective-permute-start.10 = (bf16[64,640]{1,0:T(8,128)(2,1)S(1)}, bf16[64,640]{1,0:T(8,128)(2,1)S(1)}, u32[]{:S(2)}, u32[]{:S(2)}) collective-permute-start(bf16[64,640]{1,0:T(8,128)(2,1)S(1)} %get-tuple-element.59), channel_id=1, source_target_pairs={{0,48},{8,56},{16,0},{24,8},{32,16},{40,24},{48,32},{56,40},{64,11... | collective-permute-start | bytes 245768 | tf_op jit(solution)/shard_map/ppermute | solution.py:316
  47.5 1.4 %collective-permute-start.11 = (bf16[64,640]{1,0:T(8,128)(2,1)S(1)}, bf16[64,640]{1,0:T(8,128)(2,1)S(1)}, u32[]{:S(2)}, u32[]{:S(2)}) collective-permute-start(bf16[64,640]{1,0:T(8,128)(2,1)S(1)} %get-tuple-element.60), channel_id=1, source_target_pairs={{0,32},{8,40},{16,48},{24,56},{32,0},{40,8},{48,16},{56,24},{64,96... | collective-permute-start | bytes 245768 | tf_op jit(solution)/shard_map/ppermute | solution.py:316
  48.9 2.5 %collective-permute-done.10.refs_1_ = bf16[64,640]{1,0:T(8,128)(2,1)S(1)} collective-permute-done((bf16[64,640]{1,0:T(8,128)(2,1)S(1)}, bf16[64,640]{1,0:T(8,128)(2,1)S(1)}, u32[]{:S(2)}, u32[]{:S(2)}) %collective-permute-start.10) | collective-permute-done | bytes 81952 | tf_op jit(solution)/shard_map/ppermute | solution.py:316
  51.4 5.6 %collective-permute-done.11.refs_2_ = bf16[64,640]{1,0:T(8,128)(2,1)S(1)} collective-permute-done((bf16[64,640]{1,0:T(8,128)(2,1)S(1)}, bf16[64,640]{1,0:T(8,128)(2,1)S(1)}, u32[]{:S(2)}, u32[]{:S(2)}) %collective-permute-start.11) | collective-permute-done | bytes 81952 | tf_op jit(solution)/shard_map/ppermute | solution.py:316
  57.0 3.7 %shard_map.79 = (f32[64,1024]{1,0:T(8,128)S(1)}, bf16[64,1024]{1,0:T(8,128)(2,1)S(1)}, bf16[64,1024]{1,0:T(8,128)(2,1)S(1)}, bf16[64,1024]{1,0:T(8,128)(2,1)S(1)}, bf16[64,512]{1,0:T(8,128)(2,1)S(1)}) custom-call(s32[8]{0:T(128)S(1)} %fusion.index_ref, bf16[64,640]{1,0:T(8,128)(2,1)S(1)} %get-tuple-element.58.refs_0_, ...), custom_call_target="tpu_custom_call" | custom-call | flops 3300000000 | bytes 1048576 | tf_op jit(solution)/shard_map/pallas_call | solution.py:276
  60.7 1.2 %collective-permute-start.16 = (bf16[64,1024]{1,0:T(8,128)(2,1)S(1)}, bf16[64,1024]{1,0:T(8,128)(2,1)S(1)}, u32[]{:S(2)}, u32[]{:S(2)}) collective-permute-start(bf16[64,1024]{1,0:T(8,128)(2,1)S(1)} %get-tuple-element.70), channel_id=1, source_target_pairs={{0,1},{1,2},{2,3},{3,0},{4,5},{5,6},{6,7},{7,4},{8,9},{9,10},{10,1... | collective-permute-start | bytes 393224 | tf_op jit(solution)/shard_map/ppermute | solution.py:320
  61.9 2.9 %collective-permute-start.17 = (bf16[64,1024]{1,0:T(8,128)(2,1)S(1)}, bf16[64,1024]{1,0:T(8,128)(2,1)S(1)}, u32[]{:S(2)}, u32[]{:S(2)}) collective-permute-start(bf16[64,1024]{1,0:T(8,128)(2,1)S(1)} %get-tuple-element.71), channel_id=1, source_target_pairs={{0,2},{1,3},{2,0},{3,1},{4,6},{5,7},{6,4},{7,5},{8,10},{9,11},{10,... | collective-permute-start | bytes 393224 | tf_op jit(solution)/shard_map/ppermute | solution.py:320
  64.8 1.3 %collective-permute-start.18 = (bf16[64,1024]{1,0:T(8,128)(2,1)S(1)}, bf16[64,1024]{1,0:T(8,128)(2,1)S(1)}, u32[]{:S(2)}, u32[]{:S(2)}) collective-permute-start(bf16[64,1024]{1,0:T(8,128)(2,1)S(1)} %get-tuple-element.72), channel_id=1, source_target_pairs={{0,3},{1,0},{2,1},{3,2},{4,7},{5,4},{6,5},{7,6},{8,11},{9,8},{10,9... | collective-permute-start | bytes 393224 | tf_op jit(solution)/shard_map/ppermute | solution.py:320
  66.1 2.6 %shard_map.80 = (f32[64,1024]{1,0:T(8,128)S(1)}, bf16[64,1024]{1,0:T(8,128)(2,1)S(1)}, bf16[64,1024]{1,0:T(8,128)(2,1)S(1)}, bf16[64,1024]{1,0:T(8,128)(2,1)S(1)}) custom-call(s32[8]{0:T(128)S(1)} %fusion.index_ref, bf16[64,512]{1,0:T(8,128)(2,1)S(1)} %get-tuple-element.64.refs_0_, bf16[512,8192]{1,0:T(8,128)(2,1)S(1)} %bitcast.1, ...), custom_call_target="tpu_custom_call" | custom-call | flops 3300000000 | bytes 1048576 | tf_op jit(solution)/shard_map/pallas_call | solution.py:276
  70.3 2.0 %collective-permute-start.15 = (bf16[64,1024]{1,0:T(8,128)(2,1)S(1)}, bf16[64,1024]{1,0:T(8,128)(2,1)S(1)}, u32[]{:S(2)}, u32[]{:S(2)}) collective-permute-start(bf16[64,1024]{1,0:T(8,128)(2,1)S(1)} %get-tuple-element.68), channel_id=1, source_target_pairs={{0,3},{1,0},{2,1},{3,2},{4,7},{5,4},{6,5},{7,6},{8,11},{9,8},{10,9... | collective-permute-start | bytes 393224 | tf_op jit(solution)/shard_map/ppermute | solution.py:322
  72.4 6.0 %collective-permute-start.19 = (bf16[64,1024]{1,0:T(8,128)(2,1)S(1)}, bf16[64,1024]{1,0:T(8,128)(2,1)S(1)}, u32[]{:S(2)}, u32[]{:S(2)}) collective-permute-start(bf16[64,1024]{1,0:T(8,128)(2,1)S(1)} %add_convert_fusion.1), channel_id=1, source_target_pairs={{0,4},{1,5},{2,6},{3,7},{4,0},{5,1},{6,2},{7,3},{8,12},{9,13},{10,... | collective-permute-start | bytes 393224 | tf_op jit(solution)/shard_map/ppermute | solution.py:327
  78.4 3.3 %collective-permute-done.19 = bf16[64,1024]{1,0:T(8,128)(2,1)S(1)} collective-permute-done((bf16[64,1024]{1,0:T(8,128)(2,1)S(1)}, bf16[64,1024]{1,0:T(8,128)(2,1)S(1)}, u32[]{:S(2)}, u32[]{:S(2)}) %collective-permute-start.19) | collective-permute-done | bytes 131104 | tf_op jit(solution)/shard_map/ppermute | solution.py:327
  (48 shorter events, 8.4 us)
Async XLA Ops:
  2.1 16.9 %copy-start.3 = (bf16[1024,128]{1,0:T(8,128)(2,1)S(1)}, bf16[1024,128]{1,0:T(8,128)(2,1)}, u32[]{:S(2)}) copy-start(bf16[1024,128]{1,0:T(8,128)(2,1)} %refs_4_.2) | copy-start | bytes 786436
  2.1 16.9 %copy-start.5 = (bf16[1024,128]{1,0:T(8,128)(2,1)S(1)}, bf16[1024,128]{1,0:T(8,128)(2,1)}, u32[]{:S(2)}) copy-start(bf16[1024,128]{1,0:T(8,128)(2,1)} %refs_5_.1) | copy-start | bytes 786436
  2.1 12.5 %collective-permute-start = (bf16[2048,128]{1,0:T(8,128)(2,1)S(1)}, bf16[2048,128]{1,0:T(8,128)(2,1)S(1)}, u32[]{:S(2)}, u32[]{:S(2)}) collective-permute-start(bf16[2048,128]{1,0:T(8,128)(2,1)S(1)} %shard_map.73), channel_id=1, source_target_pairs={{0,8},{8,0},{16,24},{24,16},{32,40},{40,32},{48,56},{56,48},{64,72... | collective-permute-start | bytes 1572872 | tf_op jit(solution)/shard_map/ppermute | solution.py:301
  2.9 12.8 %collective-permute-start.1 = (bf16[64,512]{1,0:T(8,128)(2,1)S(1)}, bf16[64,512]{1,0:T(8,128)(2,1)S(1)}, u32[]{:S(2)}, u32[]{:S(2)}) collective-permute-start(bf16[64,512]{1,0:T(8,128)(2,1)S(1)} %copy-done.6), channel_id=1, source_target_pairs={{0,16},{8,24},{16,32},{24,40},{32,48},{40,56},{48,0},{56,8},{64,80... | collective-permute-start | bytes 196616 | tf_op jit(solution)/shard_map/ppermute | solution.py:298
  4.8 12.4 %collective-permute-start.2 = (bf16[64,512]{1,0:T(8,128)(2,1)S(1)}, bf16[64,512]{1,0:T(8,128)(2,1)S(1)}, u32[]{:S(2)}, u32[]{:S(2)}) collective-permute-start(bf16[64,512]{1,0:T(8,128)(2,1)S(1)} %copy-done.6), channel_id=1, source_target_pairs={{0,32},{8,40},{16,48},{24,56},{32,0},{40,8},{48,16},{56,24},{64,96... | collective-permute-start | bytes 196616 | tf_op jit(solution)/shard_map/ppermute | solution.py:298
  8.1 14.9 %collective-permute-start.5 = (bf16[2048,128]{1,0:T(8,128)(2,1)S(1)}, bf16[2048,128]{1,0:T(8,128)(2,1)S(1)}, u32[]{:S(2)}, u32[]{:S(2)}) collective-permute-start(bf16[2048,128]{1,0:T(8,128)(2,1)S(1)} %shard_map.73), channel_id=1, source_target_pairs={{0,64},{8,72},{16,80},{24,88},{32,96},{40,104},{48,112},{56,120},{... | collective-permute-start | bytes 1572872 | tf_op jit(solution)/shard_map/ppermute | solution.py:300
  8.6 25.3 %collective-permute-start.6 = (bf16[2048,128]{1,0:T(8,128)(2,1)S(1)}, bf16[2048,128]{1,0:T(8,128)(2,1)S(1)}, u32[]{:S(2)}, u32[]{:S(2)}) collective-permute-start(bf16[2048,128]{1,0:T(8,128)(2,1)S(1)} %shard_map.73), channel_id=1, source_target_pairs={{0,192},{8,200},{16,208},{24,216},{32,224},{40,232},{48,240},{56,2... | collective-permute-start | bytes 1572872 | tf_op jit(solution)/shard_map/ppermute | solution.py:300
  14.6 4.3 %collective-permute-start.3 = (bf16[64,512]{1,0:T(8,128)(2,1)S(1)}, bf16[64,512]{1,0:T(8,128)(2,1)S(1)}, u32[]{:S(2)}, u32[]{:S(2)}) collective-permute-start(bf16[64,512]{1,0:T(8,128)(2,1)S(1)} %copy-done.6), channel_id=1, source_target_pairs={{0,48},{8,56},{16,0},{24,8},{32,16},{40,24},{48,32},{56,40},{64,11... | collective-permute-start | bytes 196616 | tf_op jit(solution)/shard_map/ppermute | solution.py:298
  15.7 22.1 %collective-permute-start.4 = (bf16[2048,128]{1,0:T(8,128)(2,1)S(1)}, bf16[2048,128]{1,0:T(8,128)(2,1)S(1)}, u32[]{:S(2)}, u32[]{:S(2)}) collective-permute-start(bf16[2048,128]{1,0:T(8,128)(2,1)S(1)} %shard_map.73), channel_id=1, source_target_pairs={{0,128},{8,136},{16,144},{24,152},{32,160},{40,168},{48,176},{56,1... | collective-permute-start | bytes 1572872 | tf_op jit(solution)/shard_map/ppermute | solution.py:302
  33.8 4.1 %collective-permute-start.8 = (bf16[2048,128]{1,0:T(8,128)(2,1)S(1)}, bf16[2048,128]{1,0:T(8,128)(2,1)S(1)}, u32[]{:S(2)}, u32[]{:S(2)}) collective-permute-start(bf16[2048,128]{1,0:T(8,128)(2,1)S(1)} %collective-permute-done.5.refs_4_), channel_id=1, source_target_pairs={{0,8},{8,0},{16,24},{24,16},{32,40},{40,32},{48,56},{56,48},{64,72... | collective-permute-start | bytes 1572872 | tf_op jit(solution)/shard_map/ppermute | solution.py:309
  33.8 4.1 %collective-permute-start.9 = (bf16[2048,128]{1,0:T(8,128)(2,1)S(1)}, bf16[2048,128]{1,0:T(8,128)(2,1)S(1)}, u32[]{:S(2)}, u32[]{:S(2)}) collective-permute-start(bf16[2048,128]{1,0:T(8,128)(2,1)S(1)} %collective-permute-done.6.refs_5_), channel_id=1, source_target_pairs={{0,8},{8,0},{16,24},{24,16},{32,40},{40,32},{48,56},{56,48},{64,72... | collective-permute-start | bytes 1572872 | tf_op jit(solution)/shard_map/ppermute | solution.py:309
  37.8 3.6 %collective-permute-start.7 = (bf16[2048,128]{1,0:T(8,128)(2,1)S(1)}, bf16[2048,128]{1,0:T(8,128)(2,1)S(1)}, u32[]{:S(2)}, u32[]{:S(2)}) collective-permute-start(bf16[2048,128]{1,0:T(8,128)(2,1)S(1)} %collective-permute-done.4.refs_4_), channel_id=1, source_target_pairs={{0,8},{8,0},{16,24},{24,16},{32,40},{40,32},{48,56},{56,48},{64,72... | collective-permute-start | bytes 1572872 | tf_op jit(solution)/shard_map/ppermute | solution.py:312
  37.9 19.0 %slice-start = ((s8[8388608]{0:T(1024)(128)(4,1)}), s8[4194304]{0:T(1024)(128)(4,1)S(1)}, s32[]{:S(2)}) async-start(s8[8388608]{0:T(1024)(128)(4,1)} %bitcast), calls=%async_computation | async-start | bytes 8388608
  41.4 15.5 %slice-start.1 = ((s8[8388608]{0:T(1024)(128)(4,1)}), s8[4194304]{0:T(1024)(128)(4,1)S(1)}, s32[]{:S(2)}) async-start(s8[8388608]{0:T(1024)(128)(4,1)} %bitcast), calls=%async_computation.1 | async-start | bytes 8388608
  46.2 5.2 %collective-permute-start.10 = (bf16[64,640]{1,0:T(8,128)(2,1)S(1)}, bf16[64,640]{1,0:T(8,128)(2,1)S(1)}, u32[]{:S(2)}, u32[]{:S(2)}) collective-permute-start(bf16[64,640]{1,0:T(8,128)(2,1)S(1)} %get-tuple-element.59), channel_id=1, source_target_pairs={{0,48},{8,56},{16,0},{24,8},{32,16},{40,24},{48,32},{56,40},{64,11... | collective-permute-start | bytes 245768 | tf_op jit(solution)/shard_map/ppermute | solution.py:316
  47.5 9.5 %collective-permute-start.11 = (bf16[64,640]{1,0:T(8,128)(2,1)S(1)}, bf16[64,640]{1,0:T(8,128)(2,1)S(1)}, u32[]{:S(2)}, u32[]{:S(2)}) collective-permute-start(bf16[64,640]{1,0:T(8,128)(2,1)S(1)} %get-tuple-element.60), channel_id=1, source_target_pairs={{0,32},{8,40},{16,48},{24,56},{32,0},{40,8},{48,16},{56,24},{64,96... | collective-permute-start | bytes 245768 | tf_op jit(solution)/shard_map/ppermute | solution.py:316
  48.9 8.1 %collective-permute-start.12 = (bf16[64,640]{1,0:T(8,128)(2,1)S(1)}, bf16[64,640]{1,0:T(8,128)(2,1)S(1)}, u32[]{:S(2)}, u32[]{:S(2)}) collective-permute-start(bf16[64,640]{1,0:T(8,128)(2,1)S(1)} %get-tuple-element.61), channel_id=1, source_target_pairs={{0,16},{8,24},{16,32},{24,40},{32,48},{40,56},{48,0},{56,8},{64,80... | collective-permute-start | bytes 245768 | tf_op jit(solution)/shard_map/ppermute | solution.py:316
  60.7 9.6 %collective-permute-start.16 = (bf16[64,1024]{1,0:T(8,128)(2,1)S(1)}, bf16[64,1024]{1,0:T(8,128)(2,1)S(1)}, u32[]{:S(2)}, u32[]{:S(2)}) collective-permute-start(bf16[64,1024]{1,0:T(8,128)(2,1)S(1)} %get-tuple-element.70), channel_id=1, source_target_pairs={{0,1},{1,2},{2,3},{3,0},{4,5},{5,6},{6,7},{7,4},{8,9},{9,10},{10,1... | collective-permute-start | bytes 393224 | tf_op jit(solution)/shard_map/ppermute | solution.py:320
  61.9 10.4 %collective-permute-start.17 = (bf16[64,1024]{1,0:T(8,128)(2,1)S(1)}, bf16[64,1024]{1,0:T(8,128)(2,1)S(1)}, u32[]{:S(2)}, u32[]{:S(2)}) collective-permute-start(bf16[64,1024]{1,0:T(8,128)(2,1)S(1)} %get-tuple-element.71), channel_id=1, source_target_pairs={{0,2},{1,3},{2,0},{3,1},{4,6},{5,7},{6,4},{7,5},{8,10},{9,11},{10,... | collective-permute-start | bytes 393224 | tf_op jit(solution)/shard_map/ppermute | solution.py:320
  64.8 7.5 %collective-permute-start.18 = (bf16[64,1024]{1,0:T(8,128)(2,1)S(1)}, bf16[64,1024]{1,0:T(8,128)(2,1)S(1)}, u32[]{:S(2)}, u32[]{:S(2)}) collective-permute-start(bf16[64,1024]{1,0:T(8,128)(2,1)S(1)} %get-tuple-element.72), channel_id=1, source_target_pairs={{0,3},{1,0},{2,1},{3,2},{4,7},{5,4},{6,5},{7,6},{8,11},{9,8},{10,9... | collective-permute-start | bytes 393224 | tf_op jit(solution)/shard_map/ppermute | solution.py:320
  68.7 9.7 %collective-permute-start.13 = (bf16[64,1024]{1,0:T(8,128)(2,1)S(1)}, bf16[64,1024]{1,0:T(8,128)(2,1)S(1)}, u32[]{:S(2)}, u32[]{:S(2)}) collective-permute-start(bf16[64,1024]{1,0:T(8,128)(2,1)S(1)} %get-tuple-element.66), channel_id=1, source_target_pairs={{0,1},{1,2},{2,3},{3,0},{4,5},{5,6},{6,7},{7,4},{8,9},{9,10},{10,1... | collective-permute-start | bytes 393224 | tf_op jit(solution)/shard_map/ppermute | solution.py:322
  69.5 8.9 %collective-permute-start.14 = (bf16[64,1024]{1,0:T(8,128)(2,1)S(1)}, bf16[64,1024]{1,0:T(8,128)(2,1)S(1)}, u32[]{:S(2)}, u32[]{:S(2)}) collective-permute-start(bf16[64,1024]{1,0:T(8,128)(2,1)S(1)} %get-tuple-element.67), channel_id=1, source_target_pairs={{0,2},{1,3},{2,0},{3,1},{4,6},{5,7},{6,4},{7,5},{8,10},{9,11},{10,... | collective-permute-start | bytes 393224 | tf_op jit(solution)/shard_map/ppermute | solution.py:322
  70.3 8.1 %collective-permute-start.15 = (bf16[64,1024]{1,0:T(8,128)(2,1)S(1)}, bf16[64,1024]{1,0:T(8,128)(2,1)S(1)}, u32[]{:S(2)}, u32[]{:S(2)}) collective-permute-start(bf16[64,1024]{1,0:T(8,128)(2,1)S(1)} %get-tuple-element.68), channel_id=1, source_target_pairs={{0,3},{1,0},{2,1},{3,2},{4,7},{5,4},{6,5},{7,6},{8,11},{9,8},{10,9... | collective-permute-start | bytes 393224 | tf_op jit(solution)/shard_map/ppermute | solution.py:322
  72.4 9.3 %collective-permute-start.19 = (bf16[64,1024]{1,0:T(8,128)(2,1)S(1)}, bf16[64,1024]{1,0:T(8,128)(2,1)S(1)}, u32[]{:S(2)}, u32[]{:S(2)}) collective-permute-start(bf16[64,1024]{1,0:T(8,128)(2,1)S(1)} %add_convert_fusion.1), channel_id=1, source_target_pairs={{0,4},{1,5},{2,6},{3,7},{4,0},{5,1},{6,2},{7,3},{8,12},{9,13},{10,... | collective-permute-start | bytes 393224 | tf_op jit(solution)/shard_map/ppermute | solution.py:327
  (6 other events, 22.7 us)

commit v3 on v2

v3 whole, which is shorter than its diff:
```python
import functools
import math

import jax
import jax.numpy as jnp
from jax import lax
from jax.experimental import pallas as pl
from jax.experimental.pallas import tpu as pltpu
from jax.sharding import PartitionSpec as P

DH = 128
GROUP = 4
WIDTH = GROUP * DH
LOG2E = math.log2(math.e)
SCALE2 = LOG2E / math.sqrt(DH)
F32 = jnp.float32
BF16 = jnp.bfloat16

NX, NZ, NC = 4, 4, 2
NH, NY = 2, 4


def blk_perm(dx=0, dz=0, dc=0):
    pairs = []
    for x in range(NX):
        for z in range(NZ):
            for c in range(NC):
                there = ((x + dx) % NX * NZ + (z + dz) % NZ) * NC + (c + dc) % NC
                pairs.append(((x * NZ + z) * NC + c, there))
    return pairs


def tensor_perm(dh=0, dy=0):
    return [
        (h * NY + y, (h + dh) % NH * NY + (y + dy) % NY) for h in range(NH) for y in range(NY)
    ]


def params(mib):
    return pltpu.CompilerParams(vmem_limit_bytes=mib << 20)


def cost(micros):
    return pl.CostEstimate(flops=int(micros * 1.1e9), bytes_accessed=1 << 20, transcendentals=0)


def heads_of(q):
    return jnp.concatenate([q[:, h * DH : (h + 1) * DH] for h in range(GROUP)], axis=0)


SUB = 16


def suffix_kernel(len_ref, q_ref, k_ref, v_ref, o_ref, lse_ref):
    rows, slots, _ = k_ref.shape
    row = lax.broadcasted_iota(jnp.int32, (SUB, slots), 0)
    col = lax.broadcasted_iota(jnp.int32, (SUB, slots), 1)
    lane = lax.broadcasted_iota(jnp.int32, (SUB, DH), 1)
    for first in range(0, rows, SUB):
        here = slice(first, first + SUB)
        q = heads_of(q_ref[here, :])
        k = k_ref[here].reshape(SUB * slots, DH)
        v = v_ref[here].reshape(SUB * slots, DH)
        s = lax.dot_general(q, k, (((1,), (1,)), ((), ())), preferred_element_type=F32)
        tiles = [(row == j) & (col < len_ref[first + j]) for j in range(SUB)]
        live = jnp.concatenate(tiles, axis=1)
        live = jnp.concatenate([live] * GROUP, axis=0)
        s = jnp.where(live, s * SCALE2, -jnp.inf)
        peak = jnp.max(s, axis=1, keepdims=True)
        p = jnp.exp2(s - peak)
        total = jnp.sum(p, axis=1, keepdims=True)
        mixed = jnp.dot(p.astype(BF16), v, preferred_element_type=F32) / total
        lse = peak + jnp.log2(total)
        stat = jnp.zeros((SUB, DH), F32)
        for h in range(GROUP):
            o_ref[here, h * DH : (h + 1) * DH] = mixed[h * SUB : (h + 1) * SUB]
            stat = jnp.where(lane == h, lse[h * SUB : (h + 1) * SUB], stat)
        lse_ref[here, :] = stat


def in_vmem(n):
    return [pl.BlockSpec(memory_space=pltpu.VMEM)] * n


def suffix_partial(q, sk, sv, lengths):
    rows = q.shape[0]
    return pl.pallas_call(
        suffix_kernel,
        in_specs=[pl.BlockSpec(memory_space=pltpu.SMEM)] + in_vmem(3),
        out_specs=in_vmem(2),
        out_shape=[
            jax.ShapeDtypeStruct((rows, WIDTH), F32),
            jax.ShapeDtypeStruct((rows, DH), F32),
        ],
        compiler_params=params(12),
        cost_estimate=cost(3.0),
    )(lengths, q, sk, sv)


def stack_kernel(a_ref, b_ref, o_ref, sems):
    rows = a_ref.shape[0]
    copies = [
        pltpu.make_async_copy(ref, o_ref.at[pl.ds(i * rows, rows)], sems.at[i])
        for i, ref in enumerate((a_ref, b_ref))
    ]
    for copy in copies:
        copy.start()
    for copy in copies:
        copy.wait()


def stacked(a, b):
    rows, width = a.shape
    return pl.pallas_call(
        stack_kernel,
        in_specs=[pl.BlockSpec(memory_space=pl.ANY)] * 2,
        out_specs=pl.BlockSpec(memory_space=pltpu.VMEM),
        out_shape=jax.ShapeDtypeStruct((2 * rows, width), a.dtype),
        scratch_shapes=[pltpu.SemaphoreType.DMA((2,))],
        compiler_params=params(4),
        cost_estimate=cost(0.8),
    )(a, b)


def prefix_kernel(groups, half, kinds, old, joined, packed, skip, *refs):
    refs = list(refs)
    qs = [refs.pop(0) for _ in range(groups)]
    kvs = []
    for kind in kinds:
        if kind == "pair":
            kvs.append((refs.pop(0), 0, refs.pop(0), 0))
        else:
            both = refs.pop(0)
            kvs.append((both, 0, both, both.shape[0] // 2))
    if old:
        acc_in, stat_in = refs.pop(0), refs.pop(0)
    if joined:
        part_ref = refs.pop(0)
    rows = qs[0].shape[0] // 2
    total_rows = GROUP * rows
    lane = lax.broadcasted_iota(jnp.int32, (total_rows, DH), 1)
    for g in range(groups):
        q = heads_of(qs[g][half * rows : (half + 1) * rows, :])
        peak = None
        if old:
            span = slice((skip + g) * total_rows, (skip + g + 1) * total_rows)
            acc = acc_in[span, :]
            peak = stat_in[span, 0:1]
            total = stat_in[span, DH // 2 : DH // 2 + 1]
        for k_ref, k_at, v_ref, v_at in kvs:
            size = v_ref.shape[0] - v_at
            k = k_ref[k_at : k_at + size, :]
            v = v_ref[v_at : v_at + size, :]
            s = lax.dot_general(q, k, (((1,), (1,)), ((), ())), preferred_element_type=F32)
            top = jnp.max(s, axis=1, keepdims=True) * SCALE2
            new = top if peak is None else jnp.maximum(peak, top)
            p = jnp.exp2(s * SCALE2 - new).astype(BF16)
            both = jnp.dot(
                p,
                jnp.concatenate([v, jnp.ones_like(v)], axis=1),
                preferred_element_type=F32,
            )
            if peak is None:
                acc, total = both[:, :DH], both[:, DH : DH + 1]
            else:
                fade = jnp.exp2(peak - new)
                acc = acc * fade + both[:, :DH]
                total = total * fade + both[:, DH : DH + 1]
            peak = new
        if joined:
            part = part_ref[(skip + g) * rows : (skip + g + 1) * rows, :]
            logs = jnp.concatenate(logs_of(part), axis=0)
            new = jnp.maximum(peak, logs)
            fade, weight = jnp.exp2(peak - new), jnp.exp2(logs - new)
            acc = acc * fade + heads_of(part).astype(F32) * weight
            total = total * fade + weight
            peak = new
        if packed:
            o_ref, top_row = (refs[0], g * rows) if packed == "one" else (refs[g], 0)
            out = slice(top_row, top_row + rows)
            mixed = (acc / total).astype(BF16)
            lse = peak + jnp.log2(total)
            stat = jnp.zeros((rows, DH), F32)
            for h in range(GROUP):
                part = slice(h * rows, (h + 1) * rows)
                o_ref[out, h * DH : (h + 1) * DH] = mixed[part]
                rest = lse[part]
                for j in range(3):
                    piece = rest.astype(BF16).astype(F32)
                    rest = rest - piece
                    stat = jnp.where(lane[:rows] == 3 * h + j, piece, stat)
            o_ref[out, WIDTH:] = stat.astype(BF16)
        else:
            span = slice(g * total_rows, (g + 1) * total_rows)
            refs[0][span, :] = acc
            refs[1][span, :] = jnp.where(lane < DH // 2, peak, total)


def logs_of(part):
    stat = part[:, WIDTH:].astype(F32)
    logs = []
    for h in range(GROUP):
        at = 3 * h
        logs.append(stat[:, at : at + 1] + stat[:, at + 1 : at + 2] + stat[:, at + 2 : at + 3])
    return logs


def prefix_partial(queries, half, blocks, state=None, part=None, packed=None, skip=0):
    rows = queries[0].shape[0] // 2
    groups = len(queries)
    all_rows = groups * GROUP * rows
    kinds, arrays, keys = [], [], 0
    for block in blocks:
        if isinstance(block, tuple):
            kinds.append("pair")
            arrays += list(block)
            keys += block[0].shape[0]
        else:
            kinds.append("both")
            arrays.append(block)
            keys += block.shape[0] // 2
    arrays = list(queries) + arrays
    if state is not None:
        arrays += list(state)
    if part is not None:
        arrays.append(part)
    if packed == "one":
        outs = [jax.ShapeDtypeStruct((groups * rows, WIDTH + DH), BF16)]
    elif packed:
        outs = [jax.ShapeDtypeStruct((rows, WIDTH + DH), BF16)] * groups
    else:
        outs = [jax.ShapeDtypeStruct((all_rows, DH), F32)] * 2
    kernel = functools.partial(
        prefix_kernel,
        groups,
        half,
        tuple(kinds),
        state is not None,
        part is not None,
        packed,
        skip,
    )
    return pl.pallas_call(
        kernel,
        in_specs=in_vmem(len(arrays)),
        out_specs=in_vmem(len(outs)),
        out_shape=outs,
        compiler_params=params(16),
        cost_estimate=cost(0.5 + 1.4e-6 * all_rows * keys),
    )(*arrays)


def merged(parts, mixed, lse):
    columns = []
    for h in range(GROUP):
        span = slice(h * DH, (h + 1) * DH)
        logs, values = [lse[:, h : h + 1]], [mixed[:, span]]
        for part in parts:
            logs.append(logs_of(part)[h])
            values.append(part[:, span].astype(F32))
        peak = functools.reduce(jnp.maximum, logs)
        weights = [jnp.exp2(log - peak) for log in logs]
        total = functools.reduce(jnp.add, weights)
        value = functools.reduce(jnp.add, [w * o for w, o in zip(weights, values)])
        columns.append((value / total).astype(BF16))
    return jnp.concatenate(columns, axis=1)


def project_kernel(first, merge, index_ref, weight_ref, *refs):
    refs = list(refs)
    piece = weight_ref.shape[1] // (NH * NY)
    if merge:
        *parts, mixed, lse = refs[: NZ + 2]
        *outs, att_ref = refs[NZ + 2 :]
        att = merged([p[...] for p in parts], mixed[...], lse[...])
        att_ref[...] = att
    else:
        att = refs[0][...]
        outs = refs[1:]
    for k, o in enumerate(outs):
        at = pl.multiple_of(index_ref[first + k] * piece, piece)
        w = weight_ref[:, pl.ds(at, piece)]
        o[...] = jnp.dot(att, w, preferred_element_type=F32).astype(o.dtype)


def project(index, first, inputs, weight, merge):
    rows = inputs[0].shape[0]
    depth, columns = weight.shape
    piece = columns // (NH * NY)
    outs = [jax.ShapeDtypeStruct((rows, piece), F32 if k == 0 else BF16) for k in range(NY)]
    if merge:
        outs.append(jax.ShapeDtypeStruct((rows, depth), BF16))
    return pl.pallas_call(
        functools.partial(project_kernel, first, merge),
        in_specs=[pl.BlockSpec(memory_space=pltpu.SMEM)] + in_vmem(1 + len(inputs)),
        out_specs=in_vmem(len(outs)),
        out_shape=outs,
        compiler_params=params(16),
        cost_estimate=cost(3.0),
    )(index, weight, *inputs)


def on_device(
    queries, prefix_keys, prefix_values, suffix_keys, suffix_values, suffix_lengths, out_weight
):
    here = lax.axis_index("tensor").astype(jnp.int32)
    step = jnp.arange(NH * NY, dtype=jnp.int32)
    index = (here + NY * (1 - step // NY)) // NY % NH * NY + (here + step) % NY

    send = functools.partial(lax.ppermute, axis_name="blk")
    far_queries = send(queries, perm=blk_perm(dx=2))
    both = stacked(prefix_keys, prefix_values)
    peer = send(both, perm=blk_perm(dc=1))
    near = [send(both, perm=blk_perm(dx=d)) for d in (1, 3)]
    pair = stacked(queries, far_queries)
    group = [pair] + [send(pair, perm=blk_perm(dz=d)) for d in (1, 2, 3)]

    together = lax.optimization_barrier
    peer, index = together((peer, index))
    mine = [(prefix_keys, prefix_values), peer]
    (far_part,) = prefix_partial(group, 1, mine, packed="one")
    near, far_part = together((near, far_part))
    far_part = send(far_part, perm=blk_perm(dx=2))
    near_peer = [send(b, perm=blk_perm(dc=1)) for b in near]
    state = prefix_partial(group, 0, mine)
    state = prefix_partial(group, 0, near, state)
    near_peer, state = together((near_peer, state))
    away = prefix_partial(group[1:], 0, near_peer, state, far_part, "each", 1)

    suffix_lengths, state, away = together((suffix_lengths, state, away))
    away = [send(part, perm=blk_perm(dz=-d)) for d, part in enumerate(away, 1)]
    home = prefix_partial(group[:1], 0, near_peer, state, far_part, "each")
    mixed, lse = suffix_partial(queries, suffix_keys, suffix_values, suffix_lengths)
    parts = list(home) + away

    send = functools.partial(lax.ppermute, axis_name="tensor")
    *away, attention = project(index, 0, parts + [mixed, lse], out_weight, True)
    away = [away[0]] + [send(away[d], perm=tensor_perm(dy=d)) for d in (1, 2, 3)]
    home = project(index, NY, [attention], out_weight, False)
    home = [home[0]] + [send(home[d], perm=tensor_perm(dy=d)) for d in (1, 2, 3)]

    def summed(pieces):
        return functools.reduce(jnp.add, [p.astype(F32) for p in pieces])

    other = send(summed(away).astype(BF16), perm=tensor_perm(dh=1))
    return summed(home + [other]).astype(BF16)


def solution(mesh):
    in_specs = (
        P("blk", "tensor"),
        P("blk", "tensor"),
        P("blk", "tensor"),
        P("blk", None, "tensor"),
        P("blk", None, "tensor"),
        P("blk"),
        P("tensor", None),
    )
    out_specs = P("blk", "tensor")
    return jax.shard_map(
        on_device, mesh=mesh, in_specs=in_specs, out_specs=out_specs, check_vma=False
    )
```

time: 82.6 us -> 77.2 us (0.935)
  the two profiles are of different devices: /device:TPU:6 before, /device:TPU:2 now
where the time goes in v3:
time: 77.2 us; the launch traced here: 75.8 us
  starting transfers between devices  31.3 us (41%)
  Pallas kernels  21.1 us (27%)
  waiting for transfers between devices  19.8 us (26%)
  local copies, waits for them, and re-layouts  2.59 us (3%)
  other arithmetic  0.83 us (1%)
    pallas_call x5, Pallas kernels, prefix_partial(): pl.pallas_call(kernel, in_specs=in_vmem(len(arrays)), out_specs=in_vmem(l...  15 us
    ppermute x3, waiting for transfers between devices, on_device(): group = [pair] + [send(pair, perm=blk_perm(dz=d)) for d in (1, 2, 3)]  9.42 us
    ppermute x3, starting transfers between devices, on_device(): send(away[d], perm=tensor_perm(dy=d))  5.9 us
    ppermute x3, starting transfers between devices, on_device(): group = [pair] + [send(pair, perm=blk_perm(dz=d)) for d in (1, 2, 3)]  5.65 us
    ppermute x1, waiting for transfers between devices, on_device(): other = send(summed(away).astype(BF16), perm=tensor_perm(dh=1))  5.34 us
    ppermute x1, starting transfers between devices, on_device(): other = send(summed(away).astype(BF16), perm=tensor_perm(dh=1))  5.02 us
    ppermute x3, starting transfers between devices, on_device(): away = [send(part, perm=blk_perm(dz=-d)) for d, part in enumerate(away, 1)]  4.29 us
    ppermute x3, starting transfers between devices, on_device(): send(home[d], perm=tensor_perm(dy=d))  3.53 us
  transfers between devices with their start and end apart: 20, of which 7 were waited for; matrix products, arithmetic and copies ran while one was open for 0% of the time, Pallas kernels for 20%

profile of v3, /device:TPU:2, one launch (start us, length us, event | category | flops | bytes accessed | tf_op | source)
XLA Modules:
  0.0 75.8 jit_solution(1723044236558446726)
XLA Ops:
  2.7 2.1 %collective-permute-start.1 = (bf16[64,512]{1,0:T(8,128)(2,1)S(1)}, bf16[64,512]{1,0:T(8,128)(2,1)S(1)}, u32[]{:S(2)}, u32[]{:S(2)}) collective-permute-start(bf16[64,512]{1,0:T(8,128)(2,1)S(1)} %copy-done.6), channel_id=1, source_target_pairs={{0,128},{8,136},{16,144},{24,152},{32,160},{40,168},{48,176},{56,1... | collective-permute-start | bytes 196616 | tf_op jit(solution)/shard_map/ppermute | solution.py:311
  4.9 1.4 %collective-permute-start.3 = (bf16[2048,128]{1,0:T(8,128)(2,1)S(1)}, bf16[2048,128]{1,0:T(8,128)(2,1)S(1)}, u32[]{:S(2)}, u32[]{:S(2)}) collective-permute-start(bf16[2048,128]{1,0:T(8,128)(2,1)S(1)} %shard_map.73), channel_id=1, source_target_pairs={{0,192},{8,200},{16,208},{24,216},{32,224},{40,232},{48,240},{56,2... | collective-permute-start | bytes 1572872 | tf_op jit(solution)/shard_map/ppermute | solution.py:314
  6.9 2.1 %collective-permute-done.1.b_ref = bf16[64,512]{1,0:T(8,128)(2,1)S(1)} collective-permute-done((bf16[64,512]{1,0:T(8,128)(2,1)S(1)}, bf16[64,512]{1,0:T(8,128)(2,1)S(1)}, u32[]{:S(2)}, u32[]{:S(2)}) %collective-permute-start.1) | collective-permute-done | bytes 65568 | tf_op jit(solution)/shard_map/ppermute | solution.py:311
  9.1 5.0 %collective-permute-start.6 = (bf16[128,512]{1,0:T(8,128)(2,1)S(1)}, bf16[128,512]{1,0:T(8,128)(2,1)S(1)}, u32[]{:S(2)}, u32[]{:S(2)}) collective-permute-start(bf16[128,512]{1,0:T(8,128)(2,1)S(1)} %shard_map.74.refs_0_), channel_id=1, source_target_pairs={{0,48},{8,56},{16,0},{24,8},{32,16},{40,24},{48,32},{56,40},{64,11... | collective-permute-start | bytes 393224 | tf_op jit(solution)/shard_map/ppermute | solution.py:316
  14.8 3.1 %collective-permute-done.6.refs_3_.refs_2_ = bf16[128,512]{1,0:T(8,128)(2,1)S(1)} collective-permute-done((bf16[128,512]{1,0:T(8,128)(2,1)S(1)}, bf16[128,512]{1,0:T(8,128)(2,1)S(1)}, u32[]{:S(2)}, u32[]{:S(2)}) %collective-permute-start.6) | collective-permute-done | bytes 131104 | tf_op jit(solution)/shard_map/ppermute | solution.py:316
  17.9 6.3 %collective-permute-done.5.refs_2_.refs_1_ = bf16[128,512]{1,0:T(8,128)(2,1)S(1)} collective-permute-done((bf16[128,512]{1,0:T(8,128)(2,1)S(1)}, bf16[128,512]{1,0:T(8,128)(2,1)S(1)}, u32[]{:S(2)}, u32[]{:S(2)}) %collective-permute-start.5) | collective-permute-done | bytes 131104 | tf_op jit(solution)/shard_map/ppermute | solution.py:316
  24.2 3.1 %shard_map.75 = bf16[256,640]{1,0:T(8,128)(2,1)S(1)} custom-call(bf16[128,512]{1,0:T(8,128)(2,1)S(1)} %shard_map.74.refs_0_, bf16[128,512]{1,0:T(8,128)(2,1)S(1)} %collective-permute-done.4.refs_1_.refs_0_, bf16[128,512]{1,0:T(8,128)(2,1)S(1)} %collective-permute-done.5.refs_2_.refs_1_, bf16[128,512]{1,0:T(8,128)(2,1)S(1)} %collective-permute-done.6.refs_3_.refs_2_, ...), custom_call_target="tpu_custom_call" | custom-call | flops 3779614208 | bytes 1048576 | tf_op jit(solution)/shard_map/pallas_call | solution.py:243
  27.4 2.2 %collective-permute-start.9 = (bf16[256,640]{1,0:T(8,128)(2,1)S(1)}, bf16[256,640]{1,0:T(8,128)(2,1)S(1)}, u32[]{:S(2)}, u32[]{:S(2)}) collective-permute-start(bf16[256,640]{1,0:T(8,128)(2,1)S(1)} %shard_map.75), channel_id=1, source_target_pairs={{0,128},{8,136},{16,144},{24,152},{32,160},{40,168},{48,176},{56,1... | collective-permute-start | bytes 983048 | tf_op jit(solution)/shard_map/ppermute | solution.py:323
  30.1 3.0 %shard_map.76 = (f32[1024,128]{1,0:T(8,128)S(1)}, f32[1024,128]{1,0:T(8,128)S(1)}) custom-call(bf16[128,512]{1,0:T(8,128)(2,1)S(1)} %shard_map.74.refs_0_, bf16[128,512]{1,0:T(8,128)(2,1)S(1)} %collective-permute-done.4.refs_1_.refs_0_, bf16[128,512]{1,0:T(8,128)(2,1)S(1)} %collective-permute-done.5.refs_2_.refs_1_, ...), custom_call_target="tpu_custom_call" | custom-call | flops 3779614208 | bytes 1048576 | tf_op jit(solution)/shard_map/pallas_call | solution.py:243
  33.1 3.4 %shard_map.77 = (f32[1024,128]{1,0:T(8,128)S(1)}, f32[1024,128]{1,0:T(8,128)S(1)}) custom-call(bf16[128,512]{1,0:T(8,128)(2,1)S(1)} %shard_map.74.refs_0_, bf16[128,512]{1,0:T(8,128)(2,1)S(1)} %collective-permute-done.4.refs_1_.refs_0_, bf16[128,512]{1,0:T(8,128)(2,1)S(1)} %collective-permute-done.5.refs_2_.refs_1_, ...), custom_call_target="tpu_custom_call" | custom-call | flops 3779614208 | bytes 1048576 | tf_op jit(solution)/shard_map/pallas_call | solution.py:243
  37.4 3.9 %shard_map.78 = (bf16[64,640]{1,0:T(8,128)(2,1)S(1)}, bf16[64,640]{1,0:T(8,128)(2,1)S(1)}, bf16[64,640]{1,0:T(8,128)(2,1)S(1)}) custom-call(bf16[128,512]{1,0:T(8,128)(2,1)S(1)} %collective-permute-done.4.refs_1_.refs_0_, bf16[128,512]{1,0:T(8,128)(2,1)S(1)} %collective-permute-done.5.refs_2_.refs_1_, ...), custom_call_target="tpu_custom_call" | custom-call | flops 2972210688 | bytes 1048576 | tf_op jit(solution)/shard_map/pallas_call | solution.py:243
  41.5 2.1 %collective-permute-start.11 = (bf16[64,640]{1,0:T(8,128)(2,1)S(1)}, bf16[64,640]{1,0:T(8,128)(2,1)S(1)}, u32[]{:S(2)}, u32[]{:S(2)}) collective-permute-start(bf16[64,640]{1,0:T(8,128)(2,1)S(1)} %get-tuple-element.57), channel_id=1, source_target_pairs={{0,32},{8,40},{16,48},{24,56},{32,0},{40,8},{48,16},{56,24},{64,96... | collective-permute-start | bytes 245768 | tf_op jit(solution)/shard_map/ppermute | solution.py:331
  43.7 1.9 %collective-permute-start.12 = (bf16[64,640]{1,0:T(8,128)(2,1)S(1)}, bf16[64,640]{1,0:T(8,128)(2,1)S(1)}, u32[]{:S(2)}, u32[]{:S(2)}) collective-permute-start(bf16[64,640]{1,0:T(8,128)(2,1)S(1)} %get-tuple-element.58), channel_id=1, source_target_pairs={{0,16},{8,24},{16,32},{24,40},{32,48},{40,56},{48,0},{56,8},{64,80... | collective-permute-start | bytes 245768 | tf_op jit(solution)/shard_map/ppermute | solution.py:331
  45.6 2.5 %shard_map.80 = (f32[64,512]{1,0:T(8,128)S(1)}, f32[64,128]{1,0:T(8,128)S(1)}) custom-call(s32[64]{0:T(128)S(1)} %copy-done.7, bf16[64,512]{1,0:T(8,128)(2,1)S(1)} %copy-done.6, bf16[64,128,128]{2,1,0:T(8,128)(2,1)S(1)} %copy-done, bf16[64,128,128]{2,1,0:T(8,128)(2,1)S(1)} %copy-done.1), custom_call_target="tpu_custom_call" | custom-call | flops 3300000000 | bytes 1048576 | tf_op jit(solution)/shard_map/pallas_call | solution.py:87
  48.1 1.5 %shard_map.79.refs_0_ = bf16[64,640]{1,0:T(8,128)(2,1)S(1)} custom-call(bf16[128,512]{1,0:T(8,128)(2,1)S(1)} %shard_map.74.refs_0_, bf16[2048,128]{1,0:T(8,128)(2,1)S(1)} %collective-permute-done.7.refs_3_.refs_1_, bf16[2048,128]{1,0:T(8,128)(2,1)S(1)} %collective-permute-done.8.refs_4_.refs_2_, f32[1024,128]{1,0:T(8,128)S(1)} %get-tuple-element.54.refs_5_.refs_3_, ...), custom_call_target="tpu_custom_call" | custom-call | flops 1357403520 | bytes 1048576 | tf_op jit(solution)/shard_map/pallas_call | solution.py:243
  49.6 1.3 %collective-permute-done.11.refs_2_ = bf16[64,640]{1,0:T(8,128)(2,1)S(1)} collective-permute-done((bf16[64,640]{1,0:T(8,128)(2,1)S(1)}, bf16[64,640]{1,0:T(8,128)(2,1)S(1)}, u32[]{:S(2)}, u32[]{:S(2)}) %collective-permute-start.11) | collective-permute-done | bytes 81952 | tf_op jit(solution)/shard_map/ppermute | solution.py:331
  50.9 2.0 %shard_map.81 = (f32[64,1024]{1,0:T(8,128)S(1)}, bf16[64,1024]{1,0:T(8,128)(2,1)S(1)}, bf16[64,1024]{1,0:T(8,128)(2,1)S(1)}, bf16[64,1024]{1,0:T(8,128)(2,1)S(1)}, bf16[64,512]{1,0:T(8,128)(2,1)S(1)}) custom-call(s32[8]{0:T(128)S(1)} %fusion.index_ref, bf16[512,8192]{1,0:T(8,128)(2,1)S(1)} %bitcast.1, bf16[64,640]{1,0:T(8,128)(2,1)S(1)} %shard_map.79.refs_0_, ...), custom_call_target="tpu_custom_call" | custom-call | flops 3300000000 | bytes 1048576 | tf_op jit(solution)/shard_map/pallas_call | solution.py:293
  53.0 1.6 %collective-permute-start.16 = (bf16[64,1024]{1,0:T(8,128)(2,1)S(1)}, bf16[64,1024]{1,0:T(8,128)(2,1)S(1)}, u32[]{:S(2)}, u32[]{:S(2)}) collective-permute-start(bf16[64,1024]{1,0:T(8,128)(2,1)S(1)} %get-tuple-element.68), channel_id=1, source_target_pairs={{0,1},{1,2},{2,3},{3,0},{4,5},{5,6},{6,7},{7,4},{8,9},{9,10},{10,1... | collective-permute-start | bytes 393224 | tf_op jit(solution)/shard_map/ppermute | solution.py:338
  54.6 2.9 %collective-permute-start.17 = (bf16[64,1024]{1,0:T(8,128)(2,1)S(1)}, bf16[64,1024]{1,0:T(8,128)(2,1)S(1)}, u32[]{:S(2)}, u32[]{:S(2)}) collective-permute-start(bf16[64,1024]{1,0:T(8,128)(2,1)S(1)} %get-tuple-element.69), channel_id=1, source_target_pairs={{0,2},{1,3},{2,0},{3,1},{4,6},{5,7},{6,4},{7,5},{8,10},{9,11},{10,... | collective-permute-start | bytes 393224 | tf_op jit(solution)/shard_map/ppermute | solution.py:338
  57.5 1.3 %collective-permute-start.18 = (bf16[64,1024]{1,0:T(8,128)(2,1)S(1)}, bf16[64,1024]{1,0:T(8,128)(2,1)S(1)}, u32[]{:S(2)}, u32[]{:S(2)}) collective-permute-start(bf16[64,1024]{1,0:T(8,128)(2,1)S(1)} %get-tuple-element.70), channel_id=1, source_target_pairs={{0,3},{1,0},{2,1},{3,2},{4,7},{5,4},{6,5},{7,6},{8,11},{9,8},{10,9... | collective-permute-start | bytes 393224 | tf_op jit(solution)/shard_map/ppermute | solution.py:338
  58.9 1.4 %shard_map.82 = (f32[64,1024]{1,0:T(8,128)S(1)}, bf16[64,1024]{1,0:T(8,128)(2,1)S(1)}, bf16[64,1024]{1,0:T(8,128)(2,1)S(1)}, bf16[64,1024]{1,0:T(8,128)(2,1)S(1)}) custom-call(s32[8]{0:T(128)S(1)} %fusion.index_ref, bf16[512,8192]{1,0:T(8,128)(2,1)S(1)} %bitcast.1, bf16[64,512]{1,0:T(8,128)(2,1)S(1)} %get-tuple-element.62.refs_0_), custom_call_target="tpu_custom_call" | custom-call | flops 3300000000 | bytes 1048576 | tf_op jit(solution)/shard_map/pallas_call | solution.py:293
  61.8 2.0 %collective-permute-start.15 = (bf16[64,1024]{1,0:T(8,128)(2,1)S(1)}, bf16[64,1024]{1,0:T(8,128)(2,1)S(1)}, u32[]{:S(2)}, u32[]{:S(2)}) collective-permute-start(bf16[64,1024]{1,0:T(8,128)(2,1)S(1)} %get-tuple-element.66), channel_id=1, source_target_pairs={{0,3},{1,0},{2,1},{3,2},{4,7},{5,4},{6,5},{7,6},{8,11},{9,8},{10,9... | collective-permute-start | bytes 393224 | tf_op jit(solution)/shard_map/ppermute | solution.py:340
  64.7 5.0 %collective-permute-start.19 = (bf16[64,1024]{1,0:T(8,128)(2,1)S(1)}, bf16[64,1024]{1,0:T(8,128)(2,1)S(1)}, u32[]{:S(2)}, u32[]{:S(2)}) collective-permute-start(bf16[64,1024]{1,0:T(8,128)(2,1)S(1)} %add_convert_fusion.1), channel_id=1, source_target_pairs={{0,4},{1,5},{2,6},{3,7},{4,0},{5,1},{6,2},{7,3},{8,12},{9,13},{10,... | collective-permute-start | bytes 393224 | tf_op jit(solution)/shard_map/ppermute | solution.py:345
  69.8 5.3 %collective-permute-done.19 = bf16[64,1024]{1,0:T(8,128)(2,1)S(1)} collective-permute-done((bf16[64,1024]{1,0:T(8,128)(2,1)S(1)}, bf16[64,1024]{1,0:T(8,128)(2,1)S(1)}, u32[]{:S(2)}, u32[]{:S(2)}) %collective-permute-start.19) | collective-permute-done | bytes 131104 | tf_op jit(solution)/shard_map/ppermute | solution.py:345
  (50 shorter events, 8.9 us)
Async XLA Ops:
  2.0 22.2 %copy-start.3 = (bf16[1024,128]{1,0:T(8,128)(2,1)S(1)}, bf16[1024,128]{1,0:T(8,128)(2,1)}, u32[]{:S(2)}) copy-start(bf16[1024,128]{1,0:T(8,128)(2,1)} %refs_4_.3) | copy-start | bytes 786436
  2.0 22.2 %copy-start.5 = (bf16[1024,128]{1,0:T(8,128)(2,1)S(1)}, bf16[1024,128]{1,0:T(8,128)(2,1)}, u32[]{:S(2)}) copy-start(bf16[1024,128]{1,0:T(8,128)(2,1)} %refs_5_.3) | copy-start | bytes 786436
  2.0 12.1 %collective-permute-start = (bf16[2048,128]{1,0:T(8,128)(2,1)S(1)}, bf16[2048,128]{1,0:T(8,128)(2,1)S(1)}, u32[]{:S(2)}, u32[]{:S(2)}) collective-permute-start(bf16[2048,128]{1,0:T(8,128)(2,1)S(1)} %shard_map.73), channel_id=1, source_target_pairs={{0,8},{8,0},{16,24},{24,16},{32,40},{40,32},{48,56},{56,48},{64,72... | collective-permute-start | bytes 1572872 | tf_op jit(solution)/shard_map/ppermute | solution.py:313
  2.7 6.2 %collective-permute-start.1 = (bf16[64,512]{1,0:T(8,128)(2,1)S(1)}, bf16[64,512]{1,0:T(8,128)(2,1)S(1)}, u32[]{:S(2)}, u32[]{:S(2)}) collective-permute-start(bf16[64,512]{1,0:T(8,128)(2,1)S(1)} %copy-done.6), channel_id=1, source_target_pairs={{0,128},{8,136},{16,144},{24,152},{32,160},{40,168},{48,176},{56,1... | collective-permute-start | bytes 196616 | tf_op jit(solution)/shard_map/ppermute | solution.py:311
  4.9 22.5 %collective-permute-start.3 = (bf16[2048,128]{1,0:T(8,128)(2,1)S(1)}, bf16[2048,128]{1,0:T(8,128)(2,1)S(1)}, u32[]{:S(2)}, u32[]{:S(2)}) collective-permute-start(bf16[2048,128]{1,0:T(8,128)(2,1)S(1)} %shard_map.73), channel_id=1, source_target_pairs={{0,192},{8,200},{16,208},{24,216},{32,224},{40,232},{48,240},{56,2... | collective-permute-start | bytes 1572872 | tf_op jit(solution)/shard_map/ppermute | solution.py:314
  6.3 21.1 %collective-permute-start.2 = (bf16[2048,128]{1,0:T(8,128)(2,1)S(1)}, bf16[2048,128]{1,0:T(8,128)(2,1)S(1)}, u32[]{:S(2)}, u32[]{:S(2)}) collective-permute-start(bf16[2048,128]{1,0:T(8,128)(2,1)S(1)} %shard_map.73), channel_id=1, source_target_pairs={{0,64},{8,72},{16,80},{24,88},{32,96},{40,104},{48,112},{56,120},{... | collective-permute-start | bytes 1572872 | tf_op jit(solution)/shard_map/ppermute | solution.py:314
  9.1 8.8 %collective-permute-start.6 = (bf16[128,512]{1,0:T(8,128)(2,1)S(1)}, bf16[128,512]{1,0:T(8,128)(2,1)S(1)}, u32[]{:S(2)}, u32[]{:S(2)}) collective-permute-start(bf16[128,512]{1,0:T(8,128)(2,1)S(1)} %shard_map.74.refs_0_), channel_id=1, source_target_pairs={{0,48},{8,56},{16,0},{24,8},{32,16},{40,24},{48,32},{56,40},{64,11... | collective-permute-start | bytes 393224 | tf_op jit(solution)/shard_map/ppermute | solution.py:316
  14.1 10.1 %collective-permute-start.5 = (bf16[128,512]{1,0:T(8,128)(2,1)S(1)}, bf16[128,512]{1,0:T(8,128)(2,1)S(1)}, u32[]{:S(2)}, u32[]{:S(2)}) collective-permute-start(bf16[128,512]{1,0:T(8,128)(2,1)S(1)} %shard_map.74.refs_0_), channel_id=1, source_target_pairs={{0,32},{8,40},{16,48},{24,56},{32,0},{40,8},{48,16},{56,24},{64,96... | collective-permute-start | bytes 393224 | tf_op jit(solution)/shard_map/ppermute | solution.py:316
  14.1 10.1 %collective-permute-start.4 = (bf16[128,512]{1,0:T(8,128)(2,1)S(1)}, bf16[128,512]{1,0:T(8,128)(2,1)S(1)}, u32[]{:S(2)}, u32[]{:S(2)}) collective-permute-start(bf16[128,512]{1,0:T(8,128)(2,1)S(1)} %shard_map.74.refs_0_), channel_id=1, source_target_pairs={{0,16},{8,24},{16,32},{24,40},{32,48},{40,56},{48,0},{56,8},{64,80... | collective-permute-start | bytes 393224 | tf_op jit(solution)/shard_map/ppermute | solution.py:316
  27.4 10.0 %collective-permute-start.9 = (bf16[256,640]{1,0:T(8,128)(2,1)S(1)}, bf16[256,640]{1,0:T(8,128)(2,1)S(1)}, u32[]{:S(2)}, u32[]{:S(2)}) collective-permute-start(bf16[256,640]{1,0:T(8,128)(2,1)S(1)} %shard_map.75), channel_id=1, source_target_pairs={{0,128},{8,136},{16,144},{24,152},{32,160},{40,168},{48,176},{56,1... | collective-permute-start | bytes 983048 | tf_op jit(solution)/shard_map/ppermute | solution.py:323
  29.6 7.0 %collective-permute-start.7 = (bf16[2048,128]{1,0:T(8,128)(2,1)S(1)}, bf16[2048,128]{1,0:T(8,128)(2,1)S(1)}, u32[]{:S(2)}, u32[]{:S(2)}) collective-permute-start(bf16[2048,128]{1,0:T(8,128)(2,1)S(1)} %collective-permute-done.2.refs_4_), channel_id=1, source_target_pairs={{0,8},{8,0},{16,24},{24,16},{32,40},{40,32},{48,56},{56,48},{64,72... | collective-permute-start | bytes 1572872 | tf_op jit(solution)/shard_map/ppermute | solution.py:324
  29.6 7.0 %collective-permute-start.8 = (bf16[2048,128]{1,0:T(8,128)(2,1)S(1)}, bf16[2048,128]{1,0:T(8,128)(2,1)S(1)}, u32[]{:S(2)}, u32[]{:S(2)}) collective-permute-start(bf16[2048,128]{1,0:T(8,128)(2,1)S(1)} %collective-permute-done.3.refs_5_), channel_id=1, source_target_pairs={{0,8},{8,0},{16,24},{24,16},{32,40},{40,32},{48,56},{56,48},{64,72... | collective-permute-start | bytes 1572872 | tf_op jit(solution)/shard_map/ppermute | solution.py:324
  37.4 13.5 %slice-start = ((s8[8388608]{0:T(1024)(128)(4,1)}), s8[4194304]{0:T(1024)(128)(4,1)S(1)}, s32[]{:S(2)}) async-start(s8[8388608]{0:T(1024)(128)(4,1)} %bitcast), calls=%async_computation | async-start | bytes 8388608
  41.3 9.6 %slice-start.1 = ((s8[8388608]{0:T(1024)(128)(4,1)}), s8[4194304]{0:T(1024)(128)(4,1)S(1)}, s32[]{:S(2)}) async-start(s8[8388608]{0:T(1024)(128)(4,1)} %bitcast), calls=%async_computation.1 | async-start | bytes 8388608
  41.3 8.3 %collective-permute-start.10 = (bf16[64,640]{1,0:T(8,128)(2,1)S(1)}, bf16[64,640]{1,0:T(8,128)(2,1)S(1)}, u32[]{:S(2)}, u32[]{:S(2)}) collective-permute-start(bf16[64,640]{1,0:T(8,128)(2,1)S(1)} %get-tuple-element.56), channel_id=1, source_target_pairs={{0,48},{8,56},{16,0},{24,8},{32,16},{40,24},{48,32},{56,40},{64,11... | collective-permute-start | bytes 245768 | tf_op jit(solution)/shard_map/ppermute | solution.py:331
  41.5 9.4 %collective-permute-start.11 = (bf16[64,640]{1,0:T(8,128)(2,1)S(1)}, bf16[64,640]{1,0:T(8,128)(2,1)S(1)}, u32[]{:S(2)}, u32[]{:S(2)}) collective-permute-start(bf16[64,640]{1,0:T(8,128)(2,1)S(1)} %get-tuple-element.57), channel_id=1, source_target_pairs={{0,32},{8,40},{16,48},{24,56},{32,0},{40,8},{48,16},{56,24},{64,96... | collective-permute-start | bytes 245768 | tf_op jit(solution)/shard_map/ppermute | solution.py:331
  43.7 7.2 %collective-permute-start.12 = (bf16[64,640]{1,0:T(8,128)(2,1)S(1)}, bf16[64,640]{1,0:T(8,128)(2,1)S(1)}, u32[]{:S(2)}, u32[]{:S(2)}) collective-permute-start(bf16[64,640]{1,0:T(8,128)(2,1)S(1)} %get-tuple-element.58), channel_id=1, source_target_pairs={{0,16},{8,24},{16,32},{24,40},{32,48},{40,56},{48,0},{56,8},{64,80... | collective-permute-start | bytes 245768 | tf_op jit(solution)/shard_map/ppermute | solution.py:331
  53.0 8.8 %collective-permute-start.16 = (bf16[64,1024]{1,0:T(8,128)(2,1)S(1)}, bf16[64,1024]{1,0:T(8,128)(2,1)S(1)}, u32[]{:S(2)}, u32[]{:S(2)}) collective-permute-start(bf16[64,1024]{1,0:T(8,128)(2,1)S(1)} %get-tuple-element.68), channel_id=1, source_target_pairs={{0,1},{1,2},{2,3},{3,0},{4,5},{5,6},{6,7},{7,4},{8,9},{9,10},{10,1... | collective-permute-start | bytes 393224 | tf_op jit(solution)/shard_map/ppermute | solution.py:338
  54.6 10.0 %collective-permute-start.17 = (bf16[64,1024]{1,0:T(8,128)(2,1)S(1)}, bf16[64,1024]{1,0:T(8,128)(2,1)S(1)}, u32[]{:S(2)}, u32[]{:S(2)}) collective-permute-start(bf16[64,1024]{1,0:T(8,128)(2,1)S(1)} %get-tuple-element.69), channel_id=1, source_target_pairs={{0,2},{1,3},{2,0},{3,1},{4,6},{5,7},{6,4},{7,5},{8,10},{9,11},{10,... | collective-permute-start | bytes 393224 | tf_op jit(solution)/shard_map/ppermute | solution.py:338
  57.5 7.1 %collective-permute-start.18 = (bf16[64,1024]{1,0:T(8,128)(2,1)S(1)}, bf16[64,1024]{1,0:T(8,128)(2,1)S(1)}, u32[]{:S(2)}, u32[]{:S(2)}) collective-permute-start(bf16[64,1024]{1,0:T(8,128)(2,1)S(1)} %get-tuple-element.70), channel_id=1, source_target_pairs={{0,3},{1,0},{2,1},{3,2},{4,7},{5,4},{6,5},{7,6},{8,11},{9,8},{10,9... | collective-permute-start | bytes 393224 | tf_op jit(solution)/shard_map/ppermute | solution.py:338
  60.3 9.5 %collective-permute-start.13 = (bf16[64,1024]{1,0:T(8,128)(2,1)S(1)}, bf16[64,1024]{1,0:T(8,128)(2,1)S(1)}, u32[]{:S(2)}, u32[]{:S(2)}) collective-permute-start(bf16[64,1024]{1,0:T(8,128)(2,1)S(1)} %get-tuple-element.64), channel_id=1, source_target_pairs={{0,1},{1,2},{2,3},{3,0},{4,5},{5,6},{6,7},{7,4},{8,9},{9,10},{10,1... | collective-permute-start | bytes 393224 | tf_op jit(solution)/shard_map/ppermute | solution.py:340
  61.0 8.7 %collective-permute-start.14 = (bf16[64,1024]{1,0:T(8,128)(2,1)S(1)}, bf16[64,1024]{1,0:T(8,128)(2,1)S(1)}, u32[]{:S(2)}, u32[]{:S(2)}) collective-permute-start(bf16[64,1024]{1,0:T(8,128)(2,1)S(1)} %get-tuple-element.65), channel_id=1, source_target_pairs={{0,2},{1,3},{2,0},{3,1},{4,6},{5,7},{6,4},{7,5},{8,10},{9,11},{10,... | collective-permute-start | bytes 393224 | tf_op jit(solution)/shard_map/ppermute | solution.py:340
  61.8 8.0 %collective-permute-start.15 = (bf16[64,1024]{1,0:T(8,128)(2,1)S(1)}, bf16[64,1024]{1,0:T(8,128)(2,1)S(1)}, u32[]{:S(2)}, u32[]{:S(2)}) collective-permute-start(bf16[64,1024]{1,0:T(8,128)(2,1)S(1)} %get-tuple-element.66), channel_id=1, source_target_pairs={{0,3},{1,0},{2,1},{3,2},{4,7},{5,4},{6,5},{7,6},{8,11},{9,8},{10,9... | collective-permute-start | bytes 393224 | tf_op jit(solution)/shard_map/ppermute | solution.py:340
  64.7 10.4 %collective-permute-start.19 = (bf16[64,1024]{1,0:T(8,128)(2,1)S(1)}, bf16[64,1024]{1,0:T(8,128)(2,1)S(1)}, u32[]{:S(2)}, u32[]{:S(2)}) collective-permute-start(bf16[64,1024]{1,0:T(8,128)(2,1)S(1)} %add_convert_fusion.1), channel_id=1, source_target_pairs={{0,4},{1,5},{2,6},{3,7},{4,0},{5,1},{6,2},{7,3},{8,12},{9,13},{10,... | collective-permute-start | bytes 393224 | tf_op jit(solution)/shard_map/ppermute | solution.py:345
  (6 other events, 29.8 us)

commit v4 on v3

v4 whole, which is shorter than its diff:
```python
import functools
import math

import jax
import jax.numpy as jnp
from jax import lax
from jax.experimental import pallas as pl
from jax.experimental.pallas import tpu as pltpu
from jax.sharding import PartitionSpec as P

DH = 128
GROUP = 4
WIDTH = GROUP * DH
LOG2E = math.log2(math.e)
SCALE2 = LOG2E / math.sqrt(DH)
F32 = jnp.float32
BF16 = jnp.bfloat16

NX, NZ, NC = 4, 4, 2
NH, NY = 2, 4


def blk_perm(dx=0, dz=0, dc=0):
    pairs = []
    for x in range(NX):
        for z in range(NZ):
            for c in range(NC):
                there = ((x + dx) % NX * NZ + (z + dz) % NZ) * NC + (c + dc) % NC
                pairs.append(((x * NZ + z) * NC + c, there))
    return pairs


def tensor_perm(dh=0, dy=0):
    return [
        (h * NY + y, (h + dh) % NH * NY + (y + dy) % NY) for h in range(NH) for y in range(NY)
    ]


def params(mib):
    return pltpu.CompilerParams(vmem_limit_bytes=mib << 20)


def cost(micros):
    return pl.CostEstimate(flops=int(micros * 1.1e9), bytes_accessed=1 << 20, transcendentals=0)


def heads_of(q):
    return jnp.concatenate([q[:, h * DH : (h + 1) * DH] for h in range(GROUP)], axis=0)


SUB = 16


def suffix_kernel(len_ref, q_ref, k_ref, v_ref, o_ref, lse_ref):
    rows, slots, _ = k_ref.shape
    row = lax.broadcasted_iota(jnp.int32, (SUB, slots), 0)
    col = lax.broadcasted_iota(jnp.int32, (SUB, slots), 1)
    for first in range(0, rows, SUB):
        here = slice(first, first + SUB)
        q = heads_of(q_ref[here, :])
        k = k_ref[here].reshape(SUB * slots, DH)
        v = v_ref[here].reshape(SUB * slots, DH)
        s = lax.dot_general(q, k, (((1,), (1,)), ((), ())), preferred_element_type=F32)
        tiles = [(row == j) & (col < len_ref[first + j]) for j in range(SUB)]
        live = jnp.concatenate(tiles, axis=1)
        live = jnp.concatenate([live] * GROUP, axis=0)
        s = jnp.where(live, s * SCALE2, -jnp.inf)
        peak = jnp.max(s, axis=1, keepdims=True)
        p = jnp.exp2(s - peak)
        total = jnp.sum(p, axis=1, keepdims=True)
        mixed = jnp.dot(p.astype(BF16), v, preferred_element_type=F32) / total
        lse = peak + jnp.log2(total)
        for h in range(GROUP):
            part = slice(h * SUB, (h + 1) * SUB)
            o_ref[here, h * DH : (h + 1) * DH] = mixed[part]
            lse_ref[here, h * DH : (h + 1) * DH] = jnp.broadcast_to(lse[part], (SUB, DH))


def in_vmem(n):
    return [pl.BlockSpec(memory_space=pltpu.VMEM)] * n


def suffix_partial(q, sk, sv, lengths):
    rows = q.shape[0]
    return pl.pallas_call(
        suffix_kernel,
        in_specs=[pl.BlockSpec(memory_space=pltpu.SMEM)] + in_vmem(3),
        out_specs=in_vmem(2),
        out_shape=[jax.ShapeDtypeStruct((rows, WIDTH), F32)] * 2,
        compiler_params=params(12),
        cost_estimate=cost(3.0),
    )(lengths, q, sk, sv)


def stack_kernel(pieces, a_ref, b_ref, o_ref, sems):
    rows = a_ref.shape[0]
    step = rows // pieces
    copies = []
    for i, ref in enumerate((a_ref, b_ref)):
        for j in range(pieces):
            n = i * pieces + j
            copies.append(
                pltpu.make_async_copy(
                    ref.at[pl.ds(j * step, step)], o_ref.at[pl.ds(n * step, step)], sems.at[n]
                )
            )
    for copy in copies:
        copy.start()
    for copy in copies:
        copy.wait()


def stacked(a, b, pieces, mib):
    rows, width = a.shape
    return pl.pallas_call(
        functools.partial(stack_kernel, pieces),
        in_specs=[pl.BlockSpec(memory_space=pl.ANY)] * 2,
        out_specs=pl.BlockSpec(memory_space=pltpu.VMEM),
        out_shape=jax.ShapeDtypeStruct((2 * rows, width), a.dtype),
        scratch_shapes=[pltpu.SemaphoreType.DMA((2 * pieces,))],
        compiler_params=params(mib),
        cost_estimate=cost(0.8),
    )(a, b)


def spread(part):
    row = lax.broadcasted_iota(jnp.int32, (DH, WIDTH), 0)
    col = lax.broadcasted_iota(jnp.int32, (DH, WIDTH), 1)
    chosen = jnp.zeros((DH, WIDTH), F32)
    for h in range(GROUP):
        mine = (row >= 3 * h) & (row < 3 * h + 3) & (col >= h * DH) & (col < (h + 1) * DH)
        chosen = jnp.where(mine, 1.0, chosen)
    return jnp.dot(part[:, WIDTH:], chosen.astype(BF16), preferred_element_type=F32)


def pack(o_ref, out, values, logs):
    rows = values.shape[0] // GROUP
    lane = lax.broadcasted_iota(jnp.int32, (rows, DH), 1)
    stat = jnp.zeros((rows, DH), F32)
    for h in range(GROUP):
        span = slice(h * rows, (h + 1) * rows)
        o_ref[out, h * DH : (h + 1) * DH] = values[span].astype(BF16)
        rest = logs[span]
        for j in range(3):
            piece = rest.astype(BF16).astype(F32)
            rest = rest - piece
            stat = jnp.where(lane == 3 * h + j, piece, stat)
    o_ref[out, WIDTH:] = stat.astype(BF16)


def locate(counts, at):
    for i, count in enumerate(counts):
        if at < count:
            return i, at
        at -= count


def prefix_kernel(groups, half, blocks, olds, joins, packed, skip, *refs):
    refs = list(refs)

    def take(n):
        return [refs.pop(0) for _ in range(n)]

    qs, kvs = take(groups), take(blocks)
    old_refs, part_refs = take(2 * len(olds)), take(len(joins))
    rows = qs[0].shape[0] // 2
    size = kvs[0].shape[0] // 2
    many = GROUP * rows

    def scores(g, b):
        q = heads_of(qs[g][half * rows : (half + 1) * rows, :])
        return lax.dot_general(
            q, kvs[b][:size, :], (((1,), (1,)), ((), ())), preferred_element_type=F32
        )

    units = [(g, b) for g in range(groups) for b in range(blocks)]
    ahead = scores(*units[0])
    for at, (g, b) in enumerate(units):
        s = ahead
        if at + 1 < len(units):
            ahead = scores(*units[at + 1])
        if b == 0:
            peak = None
            if olds:
                i, n = locate(olds, skip + g)
                span = slice(n * many, (n + 1) * many)
                both = old_refs[2 * i][span, :]
                peak = old_refs[2 * i + 1][span, 0:1]
        top = jnp.max(s, axis=1, keepdims=True) * SCALE2
        new = top if peak is None else jnp.maximum(peak, top)
        p = jnp.exp2(s * SCALE2 - new).astype(BF16)
        v = kvs[b][size:, :]
        added = jnp.dot(
            p, jnp.concatenate([v, jnp.ones_like(v)], axis=1), preferred_element_type=F32
        )
        both = added if peak is None else both * jnp.exp2(peak - new) + added
        peak = new
        if b < blocks - 1:
            continue
        level = jnp.broadcast_to(peak, (many, DH))
        if not packed:
            span = slice(g * many, (g + 1) * many)
            refs[0][span, :] = both
            refs[1][span, :] = level
            continue
        acc, total = both[:, :DH], both[:, DH:]
        if joins:
            i, n = locate(joins, skip + g)
            part = part_refs[i][n * rows : (n + 1) * rows, :]
            logs = heads_of(spread(part))
            new = jnp.maximum(level, logs)
            fade, weight = jnp.exp2(level - new), jnp.exp2(logs - new)
            acc = acc * fade + heads_of(part).astype(F32) * weight
            total = total * fade + weight
            level = new
        o_ref, first = (refs[0], g * rows) if packed == "one" else (refs[g], 0)
        pack(o_ref, slice(first, first + rows), acc / total, level + jnp.log2(total))


def prefix_partial(queries, half, blocks, olds=(), joins=(), packed=None, skip=0):
    rows = queries[0].shape[0] // 2
    groups = len(queries)
    many = GROUP * rows
    keys = sum(b.shape[0] // 2 for b in blocks)
    arrays = [*queries, *blocks, *(a for old in olds for a in old), *joins]
    if packed == "one":
        outs = [jax.ShapeDtypeStruct((groups * rows, WIDTH + DH), BF16)]
    elif packed:
        outs = [jax.ShapeDtypeStruct((rows, WIDTH + DH), BF16)] * groups
    else:
        outs = [jax.ShapeDtypeStruct((groups * many, n * DH), F32) for n in (2, 1)]
    kernel = functools.partial(
        prefix_kernel,
        groups,
        half,
        len(blocks),
        [old[0].shape[0] // many for old in olds],
        [part.shape[0] // rows for part in joins],
        packed,
        skip,
    )
    return pl.pallas_call(
        kernel,
        in_specs=in_vmem(len(arrays)),
        out_specs=in_vmem(len(outs)),
        out_shape=outs,
        compiler_params=params(16),
        cost_estimate=cost(0.5 + 1.4e-6 * groups * many * keys),
    )(*arrays)


def merged(parts, mixed, lse):
    logs = [lse] + [spread(part) for part in parts]
    values = [mixed] + [part[:, :WIDTH].astype(F32) for part in parts]
    peak = functools.reduce(jnp.maximum, logs)
    weights = [jnp.exp2(log - peak) for log in logs]
    total = functools.reduce(jnp.add, weights)
    value = functools.reduce(jnp.add, [w * o for w, o in zip(weights, values)])
    return (value / total).astype(BF16)


def project_kernel(first, merge, index_ref, weight_ref, *refs):
    refs = list(refs)
    piece = weight_ref.shape[1] // (NH * NY)
    if merge:
        *parts, mixed, lse = refs[: NZ + 2]
        *outs, att_ref = refs[NZ + 2 :]
        att = merged([p[...] for p in parts], mixed[...], lse[...])
        att_ref[...] = att
    else:
        att = refs[0][...]
        outs = refs[1:]
    for k, o in enumerate(outs):
        at = pl.multiple_of(index_ref[first + k] * piece, piece)
        w = weight_ref[:, pl.ds(at, piece)]
        o[...] = jnp.dot(att, w, preferred_element_type=F32).astype(o.dtype)


def project(index, first, inputs, weight, merge):
    rows = inputs[0].shape[0]
    depth, columns = weight.shape
    piece = columns // (NH * NY)
    outs = [jax.ShapeDtypeStruct((rows, piece), F32 if k == 0 else BF16) for k in range(NY)]
    if merge:
        outs.append(jax.ShapeDtypeStruct((rows, depth), BF16))
    return pl.pallas_call(
        functools.partial(project_kernel, first, merge),
        in_specs=[pl.BlockSpec(memory_space=pltpu.SMEM)] + in_vmem(1 + len(inputs)),
        out_specs=in_vmem(len(outs)),
        out_shape=outs,
        compiler_params=params(16),
        cost_estimate=cost(3.0),
    )(index, weight, *inputs)


def on_device(
    queries, prefix_keys, prefix_values, suffix_keys, suffix_values, suffix_lengths, out_weight
):
    here = lax.axis_index("tensor").astype(jnp.int32)
    step = jnp.arange(NH * NY, dtype=jnp.int32)
    index = (here + NY * (1 - step // NY)) // NY % NH * NY + (here + step) % NY

    send = functools.partial(lax.ppermute, axis_name="blk")
    far_queries = send(queries, perm=blk_perm(dx=2))
    own = stacked(prefix_keys, prefix_values, 4, 56)
    peer = send(own, perm=blk_perm(dc=1))
    near = [send(own, perm=blk_perm(dx=d)) for d in (1, 3)]
    pair = stacked(queries, far_queries, 1, 4)
    shifts = (0, 3, 1, 2)
    group = [pair] + [send(pair, perm=blk_perm(dz=d)) for d in shifts[1:]]

    together = lax.optimization_barrier
    mixed, lse = suffix_partial(queries, suffix_keys, suffix_values, suffix_lengths)
    peer, index, lse = together((peer, index, lse))
    chip = [own, peer]
    (part_a,) = prefix_partial(group[:2], 1, chip, packed="one")
    part_a = send(part_a, perm=blk_perm(dx=2))
    state_a = prefix_partial(group[:2], 0, chip)
    rest, state_a = together((group[2:], state_a))
    group = group[:2] + rest
    (part_b,) = prefix_partial(rest, 1, chip, packed="one")
    near, part_b = together((near, part_b))
    part_b = send(part_b, perm=blk_perm(dx=2))
    near_peer = [send(b, perm=blk_perm(dc=1)) for b in near]
    state_b = prefix_partial(rest, 0, chip)
    state = prefix_partial(group, 0, near, [state_a, state_b])
    near_peer, state = together((near_peer, state))
    joins = [part_a, part_b]
    (third,) = prefix_partial(group[3:], 0, near_peer, [state], joins, "each", 3)
    state, third = together((state, third))
    away = prefix_partial(group[1:3], 0, near_peer, [state], joins, "each", 1)
    state, away = together((state, away))
    away = [send(part, perm=blk_perm(dz=-d)) for d, part in zip(shifts[1:], [*away, third])]
    home = prefix_partial(group[:1], 0, near_peer, [state], joins, "each")
    parts = [*home, *away]

    send = functools.partial(lax.ppermute, axis_name="tensor")
    *away, attention = project(index, 0, parts + [mixed, lse], out_weight, True)
    away = [away[0]] + [send(away[d], perm=tensor_perm(dy=d)) for d in (1, 2, 3)]
    home = project(index, NY, [attention], out_weight, False)
    home = [home[0]] + [send(home[d], perm=tensor_perm(dy=d)) for d in (1, 2, 3)]

    def summed(pieces):
        return functools.reduce(jnp.add, [p.astype(F32) for p in pieces])

    other = send(summed(away).astype(BF16), perm=tensor_perm(dh=1))
    return summed(home + [other]).astype(BF16)


def solution(mesh):
    in_specs = (
        P("blk", "tensor"),
        P("blk", "tensor"),
        P("blk", "tensor"),
        P("blk", None, "tensor"),
        P("blk", None, "tensor"),
        P("blk"),
        P("tensor", None),
    )
    out_specs = P("blk", "tensor")
    return jax.shard_map(
        on_device, mesh=mesh, in_specs=in_specs, out_specs=out_specs, check_vma=False
    )
```

time: 77.2 us -> 71.6 us (0.927)
  waiting for transfers between devices: 19.8 us -> 13 us
  starting transfers between devices: 31.3 us -> 35.3 us
  local copies, waits for them, and re-layouts: 2.59 us -> 0.04 us
    ppermute x10 -> x11, starting transfers between devices: 14.2 us -> 17.8 us  [the longest x3 5.45 us: on_device(): group = [pair] + [send(pair, perm=blk_perm(dz=d)) for d in shifts[1:]]]
    ppermute x10 -> x11, waiting for transfers between devices: 11.5 us -> 8.53 us  [the longest x3 5.57 us: on_device(): send(part, perm=blk_perm(dz=-d))]
    unnamed x20 -> x14, local copies, waits for them, and re-layouts: 2.59 us -> 0.04 us
    ppermute x1, waiting for transfers between devices: 2.05 us -> 0.01 us  [on_device(): far_queries = send(queries, perm=blk_perm(dx=2))]
    pallas_call x2, Pallas kernels: 0.22 us -> 2.25 us  [stacked(): pl.pallas_call(functools.partial(stack_kernel, pieces), in_specs=[pl.Bloc...]
    pallas_call x5 -> x8, Pallas kernels: 15 us -> 13.2 us  [prefix_partial(): pl.pallas_call(kernel, in_specs=in_vmem(len(arrays)), out_specs=in_vmem(l...]
    ppermute x1, waiting for transfers between devices: 5.34 us -> 3.49 us  [on_device(): other = send(summed(away).astype(BF16), perm=tensor_perm(dh=1))]
  transfers between devices with their start and end apart: 20 -> 21, of which waited for: 7 -> 6; matrix products, arithmetic and copies ran while one was open for 0% -> 0% of each run, Pallas kernels for 20% -> 23%
where the time goes in v4:
time: 71.6 us; the launch traced here: 70.4 us
  starting transfers between devices  35.3 us (49%)
  Pallas kernels  21 us (29%)
  waiting for transfers between devices  13 us (18%)
  other arithmetic  0.83 us (1%)
    pallas_call x8, Pallas kernels, prefix_partial(): pl.pallas_call(kernel, in_specs=in_vmem(len(arrays)), out_specs=in_vmem(l...  13.2 us
    ppermute x3, starting transfers between devices, on_device(): send(away[d], perm=tensor_perm(dy=d))  5.9 us
    ppermute x3, waiting for transfers between devices, on_device(): send(part, perm=blk_perm(dz=-d))  5.57 us
    ppermute x1, starting transfers between devices, on_device(): other = send(summed(away).astype(BF16), perm=tensor_perm(dh=1))  5.46 us
    ppermute x3, starting transfers between devices, on_device(): group = [pair] + [send(pair, perm=blk_perm(dz=d)) for d in shifts[1:]]  5.45 us
    ppermute x3, starting transfers between devices, on_device(): send(part, perm=blk_perm(dz=-d))  4.74 us
    ppermute x3, starting transfers between devices, on_device(): send(home[d], perm=tensor_perm(dy=d))  3.53 us
    ppermute x1, waiting for transfers between devices, on_device(): other = send(summed(away).astype(BF16), perm=tensor_perm(dh=1))  3.49 us
  transfers between devices with their start and end apart: 21, of which 6 were waited for; matrix products, arithmetic and copies ran while one was open for 0% of the time, Pallas kernels for 23%

profile of v4, /device:TPU:2, one launch (start us, length us, event | category | flops | bytes accessed | tf_op | source)
XLA Modules:
  0.0 70.4 jit_solution(14514548739563887243)
XLA Ops:
  0.0 2.1 %collective-permute-start.1 = (bf16[64,512]{1,0:T(8,128)(2,1)}, bf16[64,512]{1,0:T(8,128)(2,1)S(1)}, u32[]{:S(2)}, u32[]{:S(2)}) collective-permute-start(bf16[64,512]{1,0:T(8,128)(2,1)} %a_ref.3), channel_id=1, source_target_pairs={{0,128},{8,136},{16,144},{24,152},{32,160},{40,168},{48,176},{56,1... | collective-permute-start | bytes 196616 | tf_op jit(solution)/shard_map/ppermute | solution.py:304
  2.1 2.1 %shard_map.73.refs_2_ = bf16[2048,128]{1,0:T(8,128)(2,1)} custom-call(bf16[1024,128]{1,0:T(8,128)(2,1)} %a_ref.2, bf16[1024,128]{1,0:T(8,128)(2,1)} %b_ref.1), custom_call_target="tpu_custom_call" | custom-call | flops 880000000 | bytes 1048576 | tf_op jit(solution)/shard_map/pallas_call | solution.py:115
  4.3 1.5 %collective-permute-start.3 = (bf16[2048,128]{1,0:T(8,128)(2,1)}, bf16[2048,128]{1,0:T(8,128)(2,1)S(1)}, u32[]{:S(2)}, u32[]{:S(2)}) collective-permute-start(bf16[2048,128]{1,0:T(8,128)(2,1)} %shard_map.73.refs_2_), channel_id=1, source_target_pairs={{0,192},{8,200},{16,208},{24,216},{32,224},{40,232},{48,240},{56,2... | collective-permute-start | bytes 1572872 | tf_op jit(solution)/shard_map/ppermute | solution.py:307
  6.6 4.7 %collective-permute-start.6 = (bf16[128,512]{1,0:T(8,128)(2,1)S(1)}, bf16[128,512]{1,0:T(8,128)(2,1)S(1)}, u32[]{:S(2)}, u32[]{:S(2)}) collective-permute-start(bf16[128,512]{1,0:T(8,128)(2,1)S(1)} %shard_map.75.refs_0_), channel_id=1, source_target_pairs={{0,48},{8,56},{16,0},{24,8},{32,16},{40,24},{48,32},{56,40},{64,11... | collective-permute-start | bytes 393224 | tf_op jit(solution)/shard_map/ppermute | solution.py:310
  11.4 2.5 %shard_map.74 = (f32[64,512]{1,0:T(8,128)S(1)}, f32[64,512]{1,0:T(8,128)S(1)}) custom-call(s32[64]{0:T(128)S(1)} %copy-done.4, bf16[64,512]{1,0:T(8,128)(2,1)S(1)} %copy-done.3, bf16[64,128,128]{2,1,0:T(8,128)(2,1)S(1)} %copy-done, bf16[64,128,128]{2,1,0:T(8,128)(2,1)S(1)} %copy-done.1), custom_call_target="tpu_custom_call" | custom-call | flops 3300000000 | bytes 1048576 | tf_op jit(solution)/shard_map/pallas_call | solution.py:85
  14.7 1.5 %shard_map.80 = bf16[128,640]{1,0:T(8,128)(2,1)S(1)} custom-call(bf16[128,512]{1,0:T(8,128)(2,1)S(1)} %shard_map.75.refs_0_, bf16[128,512]{1,0:T(8,128)(2,1)S(1)} %collective-permute-done.6.refs_1_.refs_0_, bf16[2048,128]{1,0:T(8,128)(2,1)S(1)} %copy-done.2, bf16[2048,128]{1,0:T(8,128)(2,1)S(1)} %collective-permute-done.refs_3_), custom_call_target="tpu_custom_call" | custom-call | flops 2164807168 | bytes 1048576 | tf_op jit(solution)/shard_map/pallas_call | solution.py:242
  16.2 2.7 %collective-permute-start.9 = (bf16[128,640]{1,0:T(8,128)(2,1)S(1)}, bf16[128,640]{1,0:T(8,128)(2,1)S(1)}, u32[]{:S(2)}, u32[]{:S(2)}) collective-permute-start(bf16[128,640]{1,0:T(8,128)(2,1)S(1)} %shard_map.80), channel_id=1, source_target_pairs={{0,128},{8,136},{16,144},{24,152},{32,160},{40,168},{48,176},{56,1... | collective-permute-start | bytes 491528 | tf_op jit(solution)/shard_map/ppermute | solution.py:317
  18.9 1.5 %shard_map.76 = (f32[512,256]{1,0:T(8,128)S(1)}, f32[512,128]{1,0:T(8,128)S(1)}) custom-call(bf16[128,512]{1,0:T(8,128)(2,1)S(1)} %shard_map.75.refs_0_, bf16[128,512]{1,0:T(8,128)(2,1)S(1)} %collective-permute-done.6.refs_1_.refs_0_, bf16[2048,128]{1,0:T(8,128)(2,1)S(1)} %copy-done.2, bf16[2048,128]{1,0:T(8,128)(2,1)S(1)} %collective-permute-done.refs_3_), custom_call_target="tpu_custom_call" | custom-call | flops 2164807168 | bytes 1048576 | tf_op jit(solution)/shard_map/pallas_call | solution.py:242
  20.4 2.9 %collective-permute-done.5.refs_1_.refs_3_.refs_0_ = bf16[128,512]{1,0:T(8,128)(2,1)S(1)} collective-permute-done((bf16[128,512]{1,0:T(8,128)(2,1)S(1)}, bf16[128,512]{1,0:T(8,128)(2,1)S(1)}, u32[]{:S(2)}, u32[]{:S(2)}) %collective-permute-start.5) | collective-permute-done | bytes 131104 | tf_op jit(solution)/shard_map/ppermute | solution.py:310
  23.3 1.5 %shard_map.77 = bf16[128,640]{1,0:T(8,128)(2,1)S(1)} custom-call(bf16[128,512]{1,0:T(8,128)(2,1)S(1)} %collective-permute-done.4.refs_0_.refs_2_.refs_1_, bf16[128,512]{1,0:T(8,128)(2,1)S(1)} %collective-permute-done.5.refs_1_.refs_3_.refs_0_, bf16[2048,128]{1,0:T(8,128)(2,1)S(1)} %copy-done.2, bf16[2048,128]{1,0:T(8,128)(2,1)S(1)} %collective-permute-done.refs_3_), custom_call_target="tpu_custom_call" | custom-call | flops 2164807168 | bytes 1048576 | tf_op jit(solution)/shard_map/pallas_call | solution.py:242
  24.9 2.7 %collective-permute-start.10 = (bf16[128,640]{1,0:T(8,128)(2,1)S(1)}, bf16[128,640]{1,0:T(8,128)(2,1)S(1)}, u32[]{:S(2)}, u32[]{:S(2)}) collective-permute-start(bf16[128,640]{1,0:T(8,128)(2,1)S(1)} %shard_map.77), channel_id=1, source_target_pairs={{0,128},{8,136},{16,144},{24,152},{32,160},{40,168},{48,176},{56,1... | collective-permute-start | bytes 491528 | tf_op jit(solution)/shard_map/ppermute | solution.py:323
  28.1 1.5 %shard_map.78 = (f32[512,256]{1,0:T(8,128)S(1)}, f32[512,128]{1,0:T(8,128)S(1)}) custom-call(bf16[128,512]{1,0:T(8,128)(2,1)S(1)} %collective-permute-done.4.refs_0_.refs_2_.refs_1_, bf16[128,512]{1,0:T(8,128)(2,1)S(1)} %collective-permute-done.5.refs_1_.refs_3_.refs_0_, bf16[2048,128]{1,0:T(8,128)(2,1)S(1)} %copy-done.2, ...), custom_call_target="tpu_custom_call" | custom-call | flops 2164807168 | bytes 1048576 | tf_op jit(solution)/shard_map/pallas_call | solution.py:242
  29.5 3.1 %shard_map.79 = (f32[1024,256]{1,0:T(8,128)S(1)}, f32[1024,128]{1,0:T(8,128)S(1)}) custom-call(bf16[128,512]{1,0:T(8,128)(2,1)S(1)} %shard_map.75.refs_0_, bf16[128,512]{1,0:T(8,128)(2,1)S(1)} %collective-permute-done.6.refs_1_.refs_0_, bf16[128,512]{1,0:T(8,128)(2,1)S(1)} %collective-permute-done.4.refs_0_.refs_2_.refs_1_, ...), custom_call_target="tpu_custom_call" | custom-call | flops 3779614208 | bytes 1048576 | tf_op jit(solution)/shard_map/pallas_call | solution.py:242
  33.9 1.8 %shard_map.82 = (bf16[64,640]{1,0:T(8,128)(2,1)S(1)}, bf16[64,640]{1,0:T(8,128)(2,1)S(1)}) custom-call(bf16[128,512]{1,0:T(8,128)(2,1)S(1)} %collective-permute-done.6.refs_1_.refs_0_, bf16[128,512]{1,0:T(8,128)(2,1)S(1)} %collective-permute-done.4.refs_0_.refs_2_.refs_1_, bf16[2048,128]{1,0:T(8,128)(2,1)S(1)} %collective-permute-done.7.refs_1_.refs_2_, ...), custom_call_target="tpu_custom_call" | custom-call | flops 2164807168 | bytes 1048576 | tf_op jit(solution)/shard_map/pallas_call | solution.py:242
  36.5 3.1 %collective-permute-start.12 = (bf16[64,640]{1,0:T(8,128)(2,1)S(1)}, bf16[64,640]{1,0:T(8,128)(2,1)S(1)}, u32[]{:S(2)}, u32[]{:S(2)}) collective-permute-start(bf16[64,640]{1,0:T(8,128)(2,1)S(1)} %get-tuple-element.72), channel_id=1, source_target_pairs={{0,48},{8,56},{16,0},{24,8},{32,16},{40,24},{48,32},{56,40},{64,11... | collective-permute-start | bytes 245768 | tf_op jit(solution)/shard_map/ppermute | solution.py:333
  43.0 4.1 %collective-permute-done.13.refs_3_ = bf16[64,640]{1,0:T(8,128)(2,1)S(1)} collective-permute-done((bf16[64,640]{1,0:T(8,128)(2,1)S(1)}, bf16[64,640]{1,0:T(8,128)(2,1)S(1)}, u32[]{:S(2)}, u32[]{:S(2)}) %collective-permute-start.13) | collective-permute-done | bytes 81952 | tf_op jit(solution)/shard_map/ppermute | solution.py:333
  47.2 1.7 %shard_map.84 = (f32[64,1024]{1,0:T(8,128)S(1)}, bf16[64,1024]{1,0:T(8,128)(2,1)S(1)}, bf16[64,1024]{1,0:T(8,128)(2,1)S(1)}, bf16[64,1024]{1,0:T(8,128)(2,1)S(1)}, bf16[64,512]{1,0:T(8,128)(2,1)S(1)}) custom-call(s32[8]{0:T(128)S(1)} %fusion.index_ref, bf16[512,8192]{1,0:T(8,128)(2,1)S(1)} %bitcast.1, bf16[64,640]{1,0:T(8,128)(2,1)S(1)} %shard_map.83.refs_0_, ...), custom_call_target="tpu_custom_call" | custom-call | flops 3300000000 | bytes 1048576 | tf_op jit(solution)/shard_map/pallas_call | solution.py:286
  48.8 1.6 %collective-permute-start.17 = (bf16[64,1024]{1,0:T(8,128)(2,1)S(1)}, bf16[64,1024]{1,0:T(8,128)(2,1)S(1)}, u32[]{:S(2)}, u32[]{:S(2)}) collective-permute-start(bf16[64,1024]{1,0:T(8,128)(2,1)S(1)} %get-tuple-element.82), channel_id=1, source_target_pairs={{0,1},{1,2},{2,3},{3,0},{4,5},{5,6},{6,7},{7,4},{8,9},{9,10},{10,1... | collective-permute-start | bytes 393224 | tf_op jit(solution)/shard_map/ppermute | solution.py:339
  50.5 2.9 %collective-permute-start.18 = (bf16[64,1024]{1,0:T(8,128)(2,1)S(1)}, bf16[64,1024]{1,0:T(8,128)(2,1)S(1)}, u32[]{:S(2)}, u32[]{:S(2)}) collective-permute-start(bf16[64,1024]{1,0:T(8,128)(2,1)S(1)} %get-tuple-element.83), channel_id=1, source_target_pairs={{0,2},{1,3},{2,0},{3,1},{4,6},{5,7},{6,4},{7,5},{8,10},{9,11},{10,... | collective-permute-start | bytes 393224 | tf_op jit(solution)/shard_map/ppermute | solution.py:339
  53.4 1.3 %collective-permute-start.19 = (bf16[64,1024]{1,0:T(8,128)(2,1)S(1)}, bf16[64,1024]{1,0:T(8,128)(2,1)S(1)}, u32[]{:S(2)}, u32[]{:S(2)}) collective-permute-start(bf16[64,1024]{1,0:T(8,128)(2,1)S(1)} %get-tuple-element.84), channel_id=1, source_target_pairs={{0,3},{1,0},{2,1},{3,2},{4,7},{5,4},{6,5},{7,6},{8,11},{9,8},{10,9... | collective-permute-start | bytes 393224 | tf_op jit(solution)/shard_map/ppermute | solution.py:339
  54.7 1.4 %shard_map.85 = (f32[64,1024]{1,0:T(8,128)S(1)}, bf16[64,1024]{1,0:T(8,128)(2,1)S(1)}, bf16[64,1024]{1,0:T(8,128)(2,1)S(1)}, bf16[64,1024]{1,0:T(8,128)(2,1)S(1)}) custom-call(s32[8]{0:T(128)S(1)} %fusion.index_ref, bf16[512,8192]{1,0:T(8,128)(2,1)S(1)} %bitcast.1, bf16[64,512]{1,0:T(8,128)(2,1)S(1)} %get-tuple-element.76.refs_0_), custom_call_target="tpu_custom_call" | custom-call | flops 3300000000 | bytes 1048576 | tf_op jit(solution)/shard_map/pallas_call | solution.py:286
  57.7 2.0 %collective-permute-start.16 = (bf16[64,1024]{1,0:T(8,128)(2,1)S(1)}, bf16[64,1024]{1,0:T(8,128)(2,1)S(1)}, u32[]{:S(2)}, u32[]{:S(2)}) collective-permute-start(bf16[64,1024]{1,0:T(8,128)(2,1)S(1)} %get-tuple-element.80), channel_id=1, source_target_pairs={{0,3},{1,0},{2,1},{3,2},{4,7},{5,4},{6,5},{7,6},{8,11},{9,8},{10,9... | collective-permute-start | bytes 393224 | tf_op jit(solution)/shard_map/ppermute | solution.py:341
  60.7 5.5 %collective-permute-start.20 = (bf16[64,1024]{1,0:T(8,128)(2,1)S(1)}, bf16[64,1024]{1,0:T(8,128)(2,1)S(1)}, u32[]{:S(2)}, u32[]{:S(2)}) collective-permute-start(bf16[64,1024]{1,0:T(8,128)(2,1)S(1)} %add_convert_fusion.1), channel_id=1, source_target_pairs={{0,4},{1,5},{2,6},{3,7},{4,0},{5,1},{6,2},{7,3},{8,12},{9,13},{10,... | collective-permute-start | bytes 393224 | tf_op jit(solution)/shard_map/ppermute | solution.py:346
  66.2 3.5 %collective-permute-done.20 = bf16[64,1024]{1,0:T(8,128)(2,1)S(1)} collective-permute-done((bf16[64,1024]{1,0:T(8,128)(2,1)S(1)}, bf16[64,1024]{1,0:T(8,128)(2,1)S(1)}, u32[]{:S(2)}, u32[]{:S(2)}) %collective-permute-start.20) | collective-permute-done | bytes 131104 | tf_op jit(solution)/shard_map/ppermute | solution.py:346
  (49 shorter events, 11.0 us)
Async XLA Ops:
  0.0 6.4 %collective-permute-start.1 = (bf16[64,512]{1,0:T(8,128)(2,1)}, bf16[64,512]{1,0:T(8,128)(2,1)S(1)}, u32[]{:S(2)}, u32[]{:S(2)}) collective-permute-start(bf16[64,512]{1,0:T(8,128)(2,1)} %a_ref.3), channel_id=1, source_target_pairs={{0,128},{8,136},{16,144},{24,152},{32,160},{40,168},{48,176},{56,1... | collective-permute-start | bytes 196616 | tf_op jit(solution)/shard_map/ppermute | solution.py:304
  2.1 9.2 %copy-start.1 = (bf16[64,128,128]{2,1,0:T(8,128)(2,1)S(1)}, bf16[64,128,128]{2,1,0:T(8,128)(2,1)}, u32[]{:S(2)}) copy-start(bf16[64,128,128]{2,1,0:T(8,128)(2,1)} %v_ref.1) | copy-start | bytes 6291460
  4.2 9.8 %collective-permute-start = (bf16[2048,128]{1,0:T(8,128)(2,1)}, bf16[2048,128]{1,0:T(8,128)(2,1)S(1)}, u32[]{:S(2)}, u32[]{:S(2)}) collective-permute-start(bf16[2048,128]{1,0:T(8,128)(2,1)} %shard_map.73.refs_2_), channel_id=1, source_target_pairs={{0,8},{8,0},{16,24},{24,16},{32,40},{40,32},{48,56},{56,48},{64,72... | collective-permute-start | bytes 1572872 | tf_op jit(solution)/shard_map/ppermute | solution.py:306
  4.3 20.5 %collective-permute-start.3 = (bf16[2048,128]{1,0:T(8,128)(2,1)}, bf16[2048,128]{1,0:T(8,128)(2,1)S(1)}, u32[]{:S(2)}, u32[]{:S(2)}) collective-permute-start(bf16[2048,128]{1,0:T(8,128)(2,1)} %shard_map.73.refs_2_), channel_id=1, source_target_pairs={{0,192},{8,200},{16,208},{24,216},{32,224},{40,232},{48,240},{56,2... | collective-permute-start | bytes 1572872 | tf_op jit(solution)/shard_map/ppermute | solution.py:307
  5.8 19.0 %collective-permute-start.2 = (bf16[2048,128]{1,0:T(8,128)(2,1)}, bf16[2048,128]{1,0:T(8,128)(2,1)S(1)}, u32[]{:S(2)}, u32[]{:S(2)}) collective-permute-start(bf16[2048,128]{1,0:T(8,128)(2,1)} %shard_map.73.refs_2_), channel_id=1, source_target_pairs={{0,64},{8,72},{16,80},{24,88},{32,96},{40,104},{48,112},{56,120},{... | collective-permute-start | bytes 1572872 | tf_op jit(solution)/shard_map/ppermute | solution.py:307
  6.6 8.0 %collective-permute-start.6 = (bf16[128,512]{1,0:T(8,128)(2,1)S(1)}, bf16[128,512]{1,0:T(8,128)(2,1)S(1)}, u32[]{:S(2)}, u32[]{:S(2)}) collective-permute-start(bf16[128,512]{1,0:T(8,128)(2,1)S(1)} %shard_map.75.refs_0_), channel_id=1, source_target_pairs={{0,48},{8,56},{16,0},{24,8},{32,16},{40,24},{48,32},{56,40},{64,11... | collective-permute-start | bytes 393224 | tf_op jit(solution)/shard_map/ppermute | solution.py:310
  13.9 9.4 %collective-permute-start.5 = (bf16[128,512]{1,0:T(8,128)(2,1)S(1)}, bf16[128,512]{1,0:T(8,128)(2,1)S(1)}, u32[]{:S(2)}, u32[]{:S(2)}) collective-permute-start(bf16[128,512]{1,0:T(8,128)(2,1)S(1)} %shard_map.75.refs_0_), channel_id=1, source_target_pairs={{0,32},{8,40},{16,48},{24,56},{32,0},{40,8},{48,16},{56,24},{64,96... | collective-permute-start | bytes 393224 | tf_op jit(solution)/shard_map/ppermute | solution.py:310
  14.0 9.3 %collective-permute-start.4 = (bf16[128,512]{1,0:T(8,128)(2,1)S(1)}, bf16[128,512]{1,0:T(8,128)(2,1)S(1)}, u32[]{:S(2)}, u32[]{:S(2)}) collective-permute-start(bf16[128,512]{1,0:T(8,128)(2,1)S(1)} %shard_map.75.refs_0_), channel_id=1, source_target_pairs={{0,16},{8,24},{16,32},{24,40},{32,48},{40,56},{48,0},{56,8},{64,80... | collective-permute-start | bytes 393224 | tf_op jit(solution)/shard_map/ppermute | solution.py:310
  16.2 16.4 %collective-permute-start.9 = (bf16[128,640]{1,0:T(8,128)(2,1)S(1)}, bf16[128,640]{1,0:T(8,128)(2,1)S(1)}, u32[]{:S(2)}, u32[]{:S(2)}) collective-permute-start(bf16[128,640]{1,0:T(8,128)(2,1)S(1)} %shard_map.80), channel_id=1, source_target_pairs={{0,128},{8,136},{16,144},{24,152},{32,160},{40,168},{48,176},{56,1... | collective-permute-start | bytes 491528 | tf_op jit(solution)/shard_map/ppermute | solution.py:317
  24.9 7.8 %collective-permute-start.10 = (bf16[128,640]{1,0:T(8,128)(2,1)S(1)}, bf16[128,640]{1,0:T(8,128)(2,1)S(1)}, u32[]{:S(2)}, u32[]{:S(2)}) collective-permute-start(bf16[128,640]{1,0:T(8,128)(2,1)S(1)} %shard_map.77), channel_id=1, source_target_pairs={{0,128},{8,136},{16,144},{24,152},{32,160},{40,168},{48,176},{56,1... | collective-permute-start | bytes 491528 | tf_op jit(solution)/shard_map/ppermute | solution.py:323
  27.6 5.0 %collective-permute-start.7 = (bf16[2048,128]{1,0:T(8,128)(2,1)S(1)}, bf16[2048,128]{1,0:T(8,128)(2,1)S(1)}, u32[]{:S(2)}, u32[]{:S(2)}) collective-permute-start(bf16[2048,128]{1,0:T(8,128)(2,1)S(1)} %collective-permute-done.2.refs_4_), channel_id=1, source_target_pairs={{0,8},{8,0},{16,24},{24,16},{32,40},{40,32},{48,56},{56,48},{64,72... | collective-permute-start | bytes 1572872 | tf_op jit(solution)/shard_map/ppermute | solution.py:324
  27.6 5.1 %collective-permute-start.8 = (bf16[2048,128]{1,0:T(8,128)(2,1)S(1)}, bf16[2048,128]{1,0:T(8,128)(2,1)S(1)}, u32[]{:S(2)}, u32[]{:S(2)}) collective-permute-start(bf16[2048,128]{1,0:T(8,128)(2,1)S(1)} %collective-permute-done.3.refs_5_), channel_id=1, source_target_pairs={{0,8},{8,0},{16,24},{24,16},{32,40},{40,32},{48,56},{56,48},{64,72... | collective-permute-start | bytes 1572872 | tf_op jit(solution)/shard_map/ppermute | solution.py:324
  32.6 14.5 %slice-start = ((s8[8388608]{0:T(1024)(128)(4,1)}), s8[4194304]{0:T(1024)(128)(4,1)S(1)}, s32[]{:S(2)}) async-start(s8[8388608]{0:T(1024)(128)(4,1)} %bitcast), calls=%async_computation | async-start | bytes 8388608
  33.8 13.3 %slice-start.1 = ((s8[8388608]{0:T(1024)(128)(4,1)}), s8[4194304]{0:T(1024)(128)(4,1)S(1)}, s32[]{:S(2)}) async-start(s8[8388608]{0:T(1024)(128)(4,1)} %bitcast), calls=%async_computation.1 | async-start | bytes 8388608
  35.7 7.2 %collective-permute-start.11 = (bf16[64,640]{1,0:T(8,128)(2,1)S(1)}, bf16[64,640]{1,0:T(8,128)(2,1)S(1)}, u32[]{:S(2)}, u32[]{:S(2)}) collective-permute-start(bf16[64,640]{1,0:T(8,128)(2,1)S(1)} %get-tuple-element.71), channel_id=1, source_target_pairs={{0,16},{8,24},{16,32},{24,40},{32,48},{40,56},{48,0},{56,8},{64,80... | collective-permute-start | bytes 245768 | tf_op jit(solution)/shard_map/ppermute | solution.py:333
  36.5 6.6 %collective-permute-start.12 = (bf16[64,640]{1,0:T(8,128)(2,1)S(1)}, bf16[64,640]{1,0:T(8,128)(2,1)S(1)}, u32[]{:S(2)}, u32[]{:S(2)}) collective-permute-start(bf16[64,640]{1,0:T(8,128)(2,1)S(1)} %get-tuple-element.72), channel_id=1, source_target_pairs={{0,48},{8,56},{16,0},{24,8},{32,16},{40,24},{48,32},{56,40},{64,11... | collective-permute-start | bytes 245768 | tf_op jit(solution)/shard_map/ppermute | solution.py:333
  39.6 7.6 %collective-permute-start.13 = (bf16[64,640]{1,0:T(8,128)(2,1)S(1)}, bf16[64,640]{1,0:T(8,128)(2,1)S(1)}, u32[]{:S(2)}, u32[]{:S(2)}) collective-permute-start(bf16[64,640]{1,0:T(8,128)(2,1)S(1)} %shard_map.81), channel_id=1, source_target_pairs={{0,32},{8,40},{16,48},{24,56},{32,0},{40,8},{48,16},{56,24},{64,96... | collective-permute-start | bytes 245768 | tf_op jit(solution)/shard_map/ppermute | solution.py:333
  48.8 8.8 %collective-permute-start.17 = (bf16[64,1024]{1,0:T(8,128)(2,1)S(1)}, bf16[64,1024]{1,0:T(8,128)(2,1)S(1)}, u32[]{:S(2)}, u32[]{:S(2)}) collective-permute-start(bf16[64,1024]{1,0:T(8,128)(2,1)S(1)} %get-tuple-element.82), channel_id=1, source_target_pairs={{0,1},{1,2},{2,3},{3,0},{4,5},{5,6},{6,7},{7,4},{8,9},{9,10},{10,1... | collective-permute-start | bytes 393224 | tf_op jit(solution)/shard_map/ppermute | solution.py:339
  50.5 10.1 %collective-permute-start.18 = (bf16[64,1024]{1,0:T(8,128)(2,1)S(1)}, bf16[64,1024]{1,0:T(8,128)(2,1)S(1)}, u32[]{:S(2)}, u32[]{:S(2)}) collective-permute-start(bf16[64,1024]{1,0:T(8,128)(2,1)S(1)} %get-tuple-element.83), channel_id=1, source_target_pairs={{0,2},{1,3},{2,0},{3,1},{4,6},{5,7},{6,4},{7,5},{8,10},{9,11},{10,... | collective-permute-start | bytes 393224 | tf_op jit(solution)/shard_map/ppermute | solution.py:339
  53.4 7.2 %collective-permute-start.19 = (bf16[64,1024]{1,0:T(8,128)(2,1)S(1)}, bf16[64,1024]{1,0:T(8,128)(2,1)S(1)}, u32[]{:S(2)}, u32[]{:S(2)}) collective-permute-start(bf16[64,1024]{1,0:T(8,128)(2,1)S(1)} %get-tuple-element.84), channel_id=1, source_target_pairs={{0,3},{1,0},{2,1},{3,2},{4,7},{5,4},{6,5},{7,6},{8,11},{9,8},{10,9... | collective-permute-start | bytes 393224 | tf_op jit(solution)/shard_map/ppermute | solution.py:339
  56.1 10.0 %collective-permute-start.14 = (bf16[64,1024]{1,0:T(8,128)(2,1)S(1)}, bf16[64,1024]{1,0:T(8,128)(2,1)S(1)}, u32[]{:S(2)}, u32[]{:S(2)}) collective-permute-start(bf16[64,1024]{1,0:T(8,128)(2,1)S(1)} %get-tuple-element.78), channel_id=1, source_target_pairs={{0,1},{1,2},{2,3},{3,0},{4,5},{5,6},{6,7},{7,4},{8,9},{9,10},{10,1... | collective-permute-start | bytes 393224 | tf_op jit(solution)/shard_map/ppermute | solution.py:341
  56.9 9.3 %collective-permute-start.15 = (bf16[64,1024]{1,0:T(8,128)(2,1)S(1)}, bf16[64,1024]{1,0:T(8,128)(2,1)S(1)}, u32[]{:S(2)}, u32[]{:S(2)}) collective-permute-start(bf16[64,1024]{1,0:T(8,128)(2,1)S(1)} %get-tuple-element.79), channel_id=1, source_target_pairs={{0,2},{1,3},{2,0},{3,1},{4,6},{5,7},{6,4},{7,5},{8,10},{9,11},{10,... | collective-permute-start | bytes 393224 | tf_op jit(solution)/shard_map/ppermute | solution.py:341
  57.7 8.5 %collective-permute-start.16 = (bf16[64,1024]{1,0:T(8,128)(2,1)S(1)}, bf16[64,1024]{1,0:T(8,128)(2,1)S(1)}, u32[]{:S(2)}, u32[]{:S(2)}) collective-permute-start(bf16[64,1024]{1,0:T(8,128)(2,1)S(1)} %get-tuple-element.80), channel_id=1, source_target_pairs={{0,3},{1,0},{2,1},{3,2},{4,7},{5,4},{6,5},{7,6},{8,11},{9,8},{10,9... | collective-permute-start | bytes 393224 | tf_op jit(solution)/shard_map/ppermute | solution.py:341
  60.7 9.0 %collective-permute-start.20 = (bf16[64,1024]{1,0:T(8,128)(2,1)S(1)}, bf16[64,1024]{1,0:T(8,128)(2,1)S(1)}, u32[]{:S(2)}, u32[]{:S(2)}) collective-permute-start(bf16[64,1024]{1,0:T(8,128)(2,1)S(1)} %add_convert_fusion.1), channel_id=1, source_target_pairs={{0,4},{1,5},{2,6},{3,7},{4,0},{5,1},{6,2},{7,3},{8,12},{9,13},{10,... | collective-permute-start | bytes 393224 | tf_op jit(solution)/shard_map/ppermute | solution.py:346
  (4 other events, 28.8 us)

commit v5 on v4

--- a/solution.py
+++ b/solution.py
@@ -72,8 +72,9 @@
         lse = peak + jnp.log2(total)
         for h in range(GROUP):
             part = slice(h * SUB, (h + 1) * SUB)
-            o_ref[here, h * DH : (h + 1) * DH] = mixed[part]
-            lse_ref[here, h * DH : (h + 1) * DH] = jnp.broadcast_to(lse[part], (SUB, DH))
+            there = slice(h * rows + first, h * rows + first + SUB)
+            o_ref[there, :] = mixed[part]
+            lse_ref[there, :] = jnp.broadcast_to(lse[part], (SUB, DH))
 
 
 def in_vmem(n):
@@ -86,7 +87,7 @@
         suffix_kernel,
         in_specs=[pl.BlockSpec(memory_space=pltpu.SMEM)] + in_vmem(3),
         out_specs=in_vmem(2),
-        out_shape=[jax.ShapeDtypeStruct((rows, WIDTH), F32)] * 2,
+        out_shape=[jax.ShapeDtypeStruct((GROUP * rows, DH), F32)] * 2,
         compiler_params=params(12),
         cost_estimate=cost(3.0),
     )(lengths, q, sk, sv)
@@ -123,29 +124,36 @@
     )(a, b)
 
 
+TILE = 16
+
+
 def spread(part):
-    row = lax.broadcasted_iota(jnp.int32, (DH, WIDTH), 0)
-    col = lax.broadcasted_iota(jnp.int32, (DH, WIDTH), 1)
-    chosen = jnp.zeros((DH, WIDTH), F32)
-    for h in range(GROUP):
-        mine = (row >= 3 * h) & (row < 3 * h + 3) & (col >= h * DH) & (col < (h + 1) * DH)
-        chosen = jnp.where(mine, 1.0, chosen)
-    return jnp.dot(part[:, WIDTH:], chosen.astype(BF16), preferred_element_type=F32)
-
-
-def pack(o_ref, out, values, logs):
-    rows = values.shape[0] // GROUP
-    lane = lax.broadcasted_iota(jnp.int32, (rows, DH), 1)
-    stat = jnp.zeros((rows, DH), F32)
-    for h in range(GROUP):
-        span = slice(h * rows, (h + 1) * rows)
-        o_ref[out, h * DH : (h + 1) * DH] = values[span].astype(BF16)
-        rest = logs[span]
-        for j in range(3):
-            piece = rest.astype(BF16).astype(F32)
-            rest = rest - piece
-            stat = jnp.where(lane == 3 * h + j, piece, stat)
-    o_ref[out, WIDTH:] = stat.astype(BF16)
+    rows = (part.shape[0] - TILE) // GROUP
+    count = GROUP * rows // TILE
+    row = lax.broadcasted_iota(jnp.int32, (DH, count * DH), 0)
+    first = 3 * lax.shift_right_logical(
+        lax.broadcasted_iota(jnp.int32, (DH, count * DH), 1), DH.bit_length() - 1
+    )
+    chosen = jnp.where((row >= first) & (row < first + 3), 1.0, 0.0).astype(BF16)
+    logs = jnp.dot(part[GROUP * rows :, :], chosen, preferred_element_type=F32)
+    order = [n * GROUP + h for h in range(GROUP) for n in range(rows // TILE)]
+    return jnp.concatenate([logs[:, n * DH : (n + 1) * DH] for n in order], axis=0)
+
+
+def pack(o_ref, first, values, logs):
+    many = values.shape[0]
+    rows = many // GROUP
+    o_ref[first : first + many, :] = values.astype(BF16)
+    lane = lax.broadcasted_iota(jnp.int32, (TILE, DH), 1)
+    strip = jnp.zeros((TILE, DH), F32)
+    for n in range(rows // TILE):
+        for h in range(GROUP):
+            rest = logs[h * rows + n * TILE : h * rows + (n + 1) * TILE]
+            for j in range(3):
+                piece = rest.astype(BF16).astype(F32)
+                rest = rest - piece
+                strip = jnp.where(lane == 3 * (n * GROUP + h) + j, piece, strip)
+    o_ref[first + many : first + many + TILE, :] = strip.astype(BF16)
 
 
 def locate(counts, at):
@@ -206,15 +214,15 @@
         acc, total = both[:, :DH], both[:, DH:]
         if joins:
             i, n = locate(joins, skip + g)
-            part = part_refs[i][n * rows : (n + 1) * rows, :]
-            logs = heads_of(spread(part))
+            part = part_refs[i][n * (many + TILE) : (n + 1) * (many + TILE), :]
+            logs = spread(part)
             new = jnp.maximum(level, logs)
             fade, weight = jnp.exp2(level - new), jnp.exp2(logs - new)
-            acc = acc * fade + heads_of(part).astype(F32) * weight
+            acc = acc * fade + part[:many, :].astype(F32) * weight
             total = total * fade + weight
             level = new
-        o_ref, first = (refs[0], g * rows) if packed == "one" else (refs[g], 0)
-        pack(o_ref, slice(first, first + rows), acc / total, level + jnp.log2(total))
+        o_ref, first = (refs[0], g * (many + TILE)) if packed == "one" else (refs[g], 0)
+        pack(o_ref, first, acc / total, level + jnp.log2(total))
 
 
 def prefix_partial(queries, half, blocks, olds=(), joins=(), packed=None, skip=0):
@@ -224,9 +232,9 @@
     keys = sum(b.shape[0] // 2 for b in blocks)
     arrays = [*queries, *blocks, *(a for old in olds for a in old), *joins]
     if packed == "one":
-        outs = [jax.ShapeDtypeStruct((groups * rows, WIDTH + DH), BF16)]
+        outs = [jax.ShapeDtypeStruct((groups * (many + TILE), DH), BF16)]
     elif packed:
-        outs = [jax.ShapeDtypeStruct((rows, WIDTH + DH), BF16)] * groups
+        outs = [jax.ShapeDtypeStruct((many + TILE, DH), BF16)] * groups
     else:
         outs = [jax.ShapeDtypeStruct((groups * many, n * DH), F32) for n in (2, 1)]
     kernel = functools.partial(
@@ -235,7 +243,7 @@
         half,
         len(blocks),
         [old[0].shape[0] // many for old in olds],
-        [part.shape[0] // rows for part in joins],
+        [part.shape[0] // (many + TILE) for part in joins],
         packed,
         skip,
     )
@@ -251,12 +259,15 @@
 
 def merged(parts, mixed, lse):
     logs = [lse] + [spread(part) for part in parts]
-    values = [mixed] + [part[:, :WIDTH].astype(F32) for part in parts]
+    many = mixed.shape[0]
+    rows = many // GROUP
+    values = [mixed] + [part[:many, :].astype(F32) for part in parts]
     peak = functools.reduce(jnp.maximum, logs)
     weights = [jnp.exp2(log - peak) for log in logs]
     total = functools.reduce(jnp.add, weights)
     value = functools.reduce(jnp.add, [w * o for w, o in zip(weights, values)])
-    return (value / total).astype(BF16)
+    value = (value / total).astype(BF16)
+    return jnp.concatenate([value[h * rows : (h + 1) * rows] for h in range(GROUP)], axis=1)
 
 
 def project_kernel(first, merge, index_ref, weight_ref, *refs):
@@ -276,8 +287,7 @@
         o[...] = jnp.dot(att, w, preferred_element_type=F32).astype(o.dtype)
 
 
-def project(index, first, inputs, weight, merge):
-    rows = inputs[0].shape[0]
+def project(rows, index, first, inputs, weight, merge):
     depth, columns = weight.shape
     piece = columns // (NH * NY)
     outs = [jax.ShapeDtypeStruct((rows, piece), F32 if k == 0 else BF16) for k in range(NY)]
@@ -335,9 +345,9 @@
     parts = [*home, *away]
 
     send = functools.partial(lax.ppermute, axis_name="tensor")
-    *away, attention = project(index, 0, parts + [mixed, lse], out_weight, True)
+    *away, attention = project(queries.shape[0], index, 0, parts + [mixed, lse], out_weight, True)
     away = [away[0]] + [send(away[d], perm=tensor_perm(dy=d)) for d in (1, 2, 3)]
-    home = project(index, NY, [attention], out_weight, False)
+    home = project(queries.shape[0], index, NY, [attention], out_weight, False)
     home = [home[0]] + [send(home[d], perm=tensor_perm(dy=d)) for d in (1, 2, 3)]
 
     def summed(pieces):

time: 71.6 us -> 70.4 us (0.983); the launches traced: 70.4 us -> 70.3 us
  Pallas kernels: 21 us -> 22.1 us
    ppermute x3, waiting for transfers between devices: 5.57 us -> 4.32 us  [on_device(): send(part, perm=blk_perm(dz=-d))]
    pallas_call x8, Pallas kernels: 13.2 us -> 14 us  [prefix_partial(): pl.pallas_call(kernel, in_specs=in_vmem(len(arrays)), out_specs=in_vmem(l...]
  transfers between devices with their start and end apart: 21 -> 21, of which waited for: 6 -> 5; matrix products, arithmetic and copies ran while one was open for 0% -> 0% of each run, Pallas kernels for 23% -> 24%
where the time goes in v5:
time: 70.4 us; the launch traced here: 70.3 us
  starting transfers between devices  34.6 us (49%)
  Pallas kernels  22.1 us (31%)
  waiting for transfers between devices  12.4 us (18%)
  other arithmetic  0.83 us (1%)
    pallas_call x8, Pallas kernels, prefix_partial(): pl.pallas_call(kernel, in_specs=in_vmem(len(arrays)), out_specs=in_vmem(l...  14 us
    ppermute x3, starting transfers between devices, on_device(): send(away[d], perm=tensor_perm(dy=d))  5.89 us
    ppermute x3, starting transfers between devices, on_device(): group = [pair] + [send(pair, perm=blk_perm(dz=d)) for d in shifts[1:]]  5.45 us
    ppermute x1, starting transfers between devices, on_device(): other = send(summed(away).astype(BF16), perm=tensor_perm(dh=1))  4.8 us
    ppermute x3, starting transfers between devices, on_device(): send(part, perm=blk_perm(dz=-d))  4.74 us
    ppermute x3, waiting for transfers between devices, on_device(): send(part, perm=blk_perm(dz=-d))  4.32 us
    ppermute x1, waiting for transfers between devices, on_device(): other = send(summed(away).astype(BF16), perm=tensor_perm(dh=1))  4.15 us
    ppermute x3, starting transfers between devices, on_device(): send(home[d], perm=tensor_perm(dy=d))  3.53 us
  transfers between devices with their start and end apart: 21, of which 5 were waited for; matrix products, arithmetic and copies ran while one was open for 0% of the time, Pallas kernels for 24%

profile of v5, /device:TPU:2, one launch (start us, length us, event | category | flops | bytes accessed | tf_op | source)
XLA Modules:
  0.0 70.3 jit_solution(7417270000154527481)
XLA Ops:
  0.0 2.1 %collective-permute-start.1 = (bf16[64,512]{1,0:T(8,128)(2,1)}, bf16[64,512]{1,0:T(8,128)(2,1)S(1)}, u32[]{:S(2)}, u32[]{:S(2)}) collective-permute-start(bf16[64,512]{1,0:T(8,128)(2,1)} %a_ref.3), channel_id=1, source_target_pairs={{0,128},{8,136},{16,144},{24,152},{32,160},{40,168},{48,176},{56,1... | collective-permute-start | bytes 196616 | tf_op jit(solution)/shard_map/ppermute | solution.py:314
  2.1 2.1 %shard_map.73.refs_2_ = bf16[2048,128]{1,0:T(8,128)(2,1)} custom-call(bf16[1024,128]{1,0:T(8,128)(2,1)} %a_ref.2, bf16[1024,128]{1,0:T(8,128)(2,1)} %b_ref.1), custom_call_target="tpu_custom_call" | custom-call | flops 880000000 | bytes 1048576 | tf_op jit(solution)/shard_map/pallas_call | solution.py:116
  4.3 1.5 %collective-permute-start.3 = (bf16[2048,128]{1,0:T(8,128)(2,1)}, bf16[2048,128]{1,0:T(8,128)(2,1)S(1)}, u32[]{:S(2)}, u32[]{:S(2)}) collective-permute-start(bf16[2048,128]{1,0:T(8,128)(2,1)} %shard_map.73.refs_2_), channel_id=1, source_target_pairs={{0,192},{8,200},{16,208},{24,216},{32,224},{40,232},{48,240},{56,2... | collective-permute-start | bytes 1572872 | tf_op jit(solution)/shard_map/ppermute | solution.py:317
  6.6 4.7 %collective-permute-start.6 = (bf16[128,512]{1,0:T(8,128)(2,1)S(1)}, bf16[128,512]{1,0:T(8,128)(2,1)S(1)}, u32[]{:S(2)}, u32[]{:S(2)}) collective-permute-start(bf16[128,512]{1,0:T(8,128)(2,1)S(1)} %shard_map.75.refs_0_), channel_id=1, source_target_pairs={{0,48},{8,56},{16,0},{24,8},{32,16},{40,24},{48,32},{56,40},{64,11... | collective-permute-start | bytes 393224 | tf_op jit(solution)/shard_map/ppermute | solution.py:320
  11.4 2.5 %shard_map.74 = (f32[256,128]{1,0:T(8,128)S(1)}, f32[256,128]{1,0:T(8,128)S(1)}) custom-call(s32[64]{0:T(128)S(1)} %copy-done.4, bf16[64,512]{1,0:T(8,128)(2,1)S(1)} %copy-done.3, bf16[64,128,128]{2,1,0:T(8,128)(2,1)S(1)} %copy-done, bf16[64,128,128]{2,1,0:T(8,128)(2,1)S(1)} %copy-done.1), custom_call_target="tpu_custom_call" | custom-call | flops 3300000000 | bytes 1048576 | tf_op jit(solution)/shard_map/pallas_call | solution.py:86
  14.7 1.5 %shard_map.80 = bf16[544,128]{1,0:T(8,128)(2,1)S(1)} custom-call(bf16[128,512]{1,0:T(8,128)(2,1)S(1)} %shard_map.75.refs_0_, bf16[128,512]{1,0:T(8,128)(2,1)S(1)} %collective-permute-done.6.refs_1_.refs_0_, bf16[2048,128]{1,0:T(8,128)(2,1)S(1)} %copy-done.2, bf16[2048,128]{1,0:T(8,128)(2,1)S(1)} %collective-permute-done.refs_3_), custom_call_target="tpu_custom_call" | custom-call | flops 2164807168 | bytes 1048576 | tf_op jit(solution)/shard_map/pallas_call | solution.py:250
  16.2 2.7 %collective-permute-start.9 = (bf16[544,128]{1,0:T(8,128)(2,1)S(1)}, bf16[544,128]{1,0:T(8,128)(2,1)S(1)}, u32[]{:S(2)}, u32[]{:S(2)}) collective-permute-start(bf16[544,128]{1,0:T(8,128)(2,1)S(1)} %shard_map.80), channel_id=1, source_target_pairs={{0,128},{8,136},{16,144},{24,152},{32,160},{40,168},{48,176},{56,1... | collective-permute-start | bytes 417800 | tf_op jit(solution)/shard_map/ppermute | solution.py:327
  18.9 1.5 %shard_map.76 = (f32[512,256]{1,0:T(8,128)S(1)}, f32[512,128]{1,0:T(8,128)S(1)}) custom-call(bf16[128,512]{1,0:T(8,128)(2,1)S(1)} %shard_map.75.refs_0_, bf16[128,512]{1,0:T(8,128)(2,1)S(1)} %collective-permute-done.6.refs_1_.refs_0_, bf16[2048,128]{1,0:T(8,128)(2,1)S(1)} %copy-done.2, bf16[2048,128]{1,0:T(8,128)(2,1)S(1)} %collective-permute-done.refs_3_), custom_call_target="tpu_custom_call" | custom-call | flops 2164807168 | bytes 1048576 | tf_op jit(solution)/shard_map/pallas_call | solution.py:250
  20.4 2.9 %collective-permute-done.5.refs_1_.refs_3_.refs_0_ = bf16[128,512]{1,0:T(8,128)(2,1)S(1)} collective-permute-done((bf16[128,512]{1,0:T(8,128)(2,1)S(1)}, bf16[128,512]{1,0:T(8,128)(2,1)S(1)}, u32[]{:S(2)}, u32[]{:S(2)}) %collective-permute-start.5) | collective-permute-done | bytes 131104 | tf_op jit(solution)/shard_map/ppermute | solution.py:320
  23.3 1.5 %shard_map.77 = bf16[544,128]{1,0:T(8,128)(2,1)S(1)} custom-call(bf16[128,512]{1,0:T(8,128)(2,1)S(1)} %collective-permute-done.4.refs_0_.refs_2_.refs_1_, bf16[128,512]{1,0:T(8,128)(2,1)S(1)} %collective-permute-done.5.refs_1_.refs_3_.refs_0_, bf16[2048,128]{1,0:T(8,128)(2,1)S(1)} %copy-done.2, bf16[2048,128]{1,0:T(8,128)(2,1)S(1)} %collective-permute-done.refs_3_), custom_call_target="tpu_custom_call" | custom-call | flops 2164807168 | bytes 1048576 | tf_op jit(solution)/shard_map/pallas_call | solution.py:250
  24.9 2.7 %collective-permute-start.10 = (bf16[544,128]{1,0:T(8,128)(2,1)S(1)}, bf16[544,128]{1,0:T(8,128)(2,1)S(1)}, u32[]{:S(2)}, u32[]{:S(2)}) collective-permute-start(bf16[544,128]{1,0:T(8,128)(2,1)S(1)} %shard_map.77), channel_id=1, source_target_pairs={{0,128},{8,136},{16,144},{24,152},{32,160},{40,168},{48,176},{56,1... | collective-permute-start | bytes 417800 | tf_op jit(solution)/shard_map/ppermute | solution.py:333
  28.1 1.5 %shard_map.78 = (f32[512,256]{1,0:T(8,128)S(1)}, f32[512,128]{1,0:T(8,128)S(1)}) custom-call(bf16[128,512]{1,0:T(8,128)(2,1)S(1)} %collective-permute-done.4.refs_0_.refs_2_.refs_1_, bf16[128,512]{1,0:T(8,128)(2,1)S(1)} %collective-permute-done.5.refs_1_.refs_3_.refs_0_, bf16[2048,128]{1,0:T(8,128)(2,1)S(1)} %copy-done.2, ...), custom_call_target="tpu_custom_call" | custom-call | flops 2164807168 | bytes 1048576 | tf_op jit(solution)/shard_map/pallas_call | solution.py:250
  29.6 3.1 %shard_map.79 = (f32[1024,256]{1,0:T(8,128)S(1)}, f32[1024,128]{1,0:T(8,128)S(1)}) custom-call(bf16[128,512]{1,0:T(8,128)(2,1)S(1)} %shard_map.75.refs_0_, bf16[128,512]{1,0:T(8,128)(2,1)S(1)} %collective-permute-done.6.refs_1_.refs_0_, bf16[128,512]{1,0:T(8,128)(2,1)S(1)} %collective-permute-done.4.refs_0_.refs_2_.refs_1_, ...), custom_call_target="tpu_custom_call" | custom-call | flops 3779614208 | bytes 1048576 | tf_op jit(solution)/shard_map/pallas_call | solution.py:250
  32.7 1.4 %shard_map.81 = bf16[272,128]{1,0:T(8,128)(2,1)S(1)} custom-call(bf16[128,512]{1,0:T(8,128)(2,1)S(1)} %collective-permute-done.5.refs_1_.refs_3_.refs_0_, bf16[2048,128]{1,0:T(8,128)(2,1)S(1)} %collective-permute-done.7.refs_1_.refs_2_, bf16[2048,128]{1,0:T(8,128)(2,1)S(1)} %collective-permute-done.8.refs_2_.refs_3_, ...), custom_call_target="tpu_custom_call" | custom-call | flops 1357403520 | bytes 1048576 | tf_op jit(solution)/shard_map/pallas_call | solution.py:250
  34.1 2.2 %shard_map.82 = (bf16[272,128]{1,0:T(8,128)(2,1)S(1)}, bf16[272,128]{1,0:T(8,128)(2,1)S(1)}) custom-call(bf16[128,512]{1,0:T(8,128)(2,1)S(1)} %collective-permute-done.6.refs_1_.refs_0_, bf16[128,512]{1,0:T(8,128)(2,1)S(1)} %collective-permute-done.4.refs_0_.refs_2_.refs_1_, bf16[2048,128]{1,0:T(8,128)(2,1)S(1)} %collective-permute-done.7.refs_1_.refs_2_, ...), custom_call_target="tpu_custom_call" | custom-call | flops 2164807168 | bytes 1048576 | tf_op jit(solution)/shard_map/pallas_call | solution.py:250
  37.1 3.1 %collective-permute-start.12 = (bf16[272,128]{1,0:T(8,128)(2,1)S(1)}, bf16[272,128]{1,0:T(8,128)(2,1)S(1)}, u32[]{:S(2)}, u32[]{:S(2)}) collective-permute-start(bf16[272,128]{1,0:T(8,128)(2,1)S(1)} %get-tuple-element.72), channel_id=1, source_target_pairs={{0,48},{8,56},{16,0},{24,8},{32,16},{40,24},{48,32},{56,40},{64,11... | collective-permute-start | bytes 208904 | tf_op jit(solution)/shard_map/ppermute | solution.py:343
  43.3 3.5 %collective-permute-done.13.refs_3_ = bf16[272,128]{1,0:T(8,128)(2,1)S(1)} collective-permute-done((bf16[272,128]{1,0:T(8,128)(2,1)S(1)}, bf16[272,128]{1,0:T(8,128)(2,1)S(1)}, u32[]{:S(2)}, u32[]{:S(2)}) %collective-permute-start.13) | collective-permute-done | bytes 69664 | tf_op jit(solution)/shard_map/ppermute | solution.py:343
  46.7 2.0 %shard_map.84 = (f32[64,1024]{1,0:T(8,128)S(1)}, bf16[64,1024]{1,0:T(8,128)(2,1)S(1)}, bf16[64,1024]{1,0:T(8,128)(2,1)S(1)}, bf16[64,1024]{1,0:T(8,128)(2,1)S(1)}, bf16[64,512]{1,0:T(8,128)(2,1)S(1)}) custom-call(s32[8]{0:T(128)S(1)} %fusion.index_ref, bf16[512,8192]{1,0:T(8,128)(2,1)S(1)} %bitcast.1, bf16[272,128]{1,0:T(8,128)(2,1)S(1)} %shard_map.83.refs_0_, ...), custom_call_target="tpu_custom_call" | custom-call | flops 3300000000 | bytes 1048576 | tf_op jit(solution)/shard_map/pallas_call | solution.py:296
  48.7 1.7 %collective-permute-start.17 = (bf16[64,1024]{1,0:T(8,128)(2,1)S(1)}, bf16[64,1024]{1,0:T(8,128)(2,1)S(1)}, u32[]{:S(2)}, u32[]{:S(2)}) collective-permute-start(bf16[64,1024]{1,0:T(8,128)(2,1)S(1)} %get-tuple-element.82), channel_id=1, source_target_pairs={{0,1},{1,2},{2,3},{3,0},{4,5},{5,6},{6,7},{7,4},{8,9},{9,10},{10,1... | collective-permute-start | bytes 393224 | tf_op jit(solution)/shard_map/ppermute | solution.py:349
  50.4 2.9 %collective-permute-start.18 = (bf16[64,1024]{1,0:T(8,128)(2,1)S(1)}, bf16[64,1024]{1,0:T(8,128)(2,1)S(1)}, u32[]{:S(2)}, u32[]{:S(2)}) collective-permute-start(bf16[64,1024]{1,0:T(8,128)(2,1)S(1)} %get-tuple-element.83), channel_id=1, source_target_pairs={{0,2},{1,3},{2,0},{3,1},{4,6},{5,7},{6,4},{7,5},{8,10},{9,11},{10,... | collective-permute-start | bytes 393224 | tf_op jit(solution)/shard_map/ppermute | solution.py:349
  54.6 1.4 %shard_map.85 = (f32[64,1024]{1,0:T(8,128)S(1)}, bf16[64,1024]{1,0:T(8,128)(2,1)S(1)}, bf16[64,1024]{1,0:T(8,128)(2,1)S(1)}, bf16[64,1024]{1,0:T(8,128)(2,1)S(1)}) custom-call(s32[8]{0:T(128)S(1)} %fusion.index_ref, bf16[512,8192]{1,0:T(8,128)(2,1)S(1)} %bitcast.1, bf16[64,512]{1,0:T(8,128)(2,1)S(1)} %get-tuple-element.76.refs_0_), custom_call_target="tpu_custom_call" | custom-call | flops 3300000000 | bytes 1048576 | tf_op jit(solution)/shard_map/pallas_call | solution.py:296
  57.5 2.0 %collective-permute-start.16 = (bf16[64,1024]{1,0:T(8,128)(2,1)S(1)}, bf16[64,1024]{1,0:T(8,128)(2,1)S(1)}, u32[]{:S(2)}, u32[]{:S(2)}) collective-permute-start(bf16[64,1024]{1,0:T(8,128)(2,1)S(1)} %get-tuple-element.80), channel_id=1, source_target_pairs={{0,3},{1,0},{2,1},{3,2},{4,7},{5,4},{6,5},{7,6},{8,11},{9,8},{10,9... | collective-permute-start | bytes 393224 | tf_op jit(solution)/shard_map/ppermute | solution.py:351
  60.6 4.8 %collective-permute-start.20 = (bf16[64,1024]{1,0:T(8,128)(2,1)S(1)}, bf16[64,1024]{1,0:T(8,128)(2,1)S(1)}, u32[]{:S(2)}, u32[]{:S(2)}) collective-permute-start(bf16[64,1024]{1,0:T(8,128)(2,1)S(1)} %add_convert_fusion.1), channel_id=1, source_target_pairs={{0,4},{1,5},{2,6},{3,7},{4,0},{5,1},{6,2},{7,3},{8,12},{9,13},{10,... | collective-permute-start | bytes 393224 | tf_op jit(solution)/shard_map/ppermute | solution.py:356
  65.4 4.2 %collective-permute-done.20 = bf16[64,1024]{1,0:T(8,128)(2,1)S(1)} collective-permute-done((bf16[64,1024]{1,0:T(8,128)(2,1)S(1)}, bf16[64,1024]{1,0:T(8,128)(2,1)S(1)}, u32[]{:S(2)}, u32[]{:S(2)}) %collective-permute-start.20) | collective-permute-done | bytes 131104 | tf_op jit(solution)/shard_map/ppermute | solution.py:356
  (49 shorter events, 10.8 us)
Async XLA Ops:
  0.0 6.4 %collective-permute-start.1 = (bf16[64,512]{1,0:T(8,128)(2,1)}, bf16[64,512]{1,0:T(8,128)(2,1)S(1)}, u32[]{:S(2)}, u32[]{:S(2)}) collective-permute-start(bf16[64,512]{1,0:T(8,128)(2,1)} %a_ref.3), channel_id=1, source_target_pairs={{0,128},{8,136},{16,144},{24,152},{32,160},{40,168},{48,176},{56,1... | collective-permute-start | bytes 196616 | tf_op jit(solution)/shard_map/ppermute | solution.py:314
  2.1 9.2 %copy-start.1 = (bf16[64,128,128]{2,1,0:T(8,128)(2,1)S(1)}, bf16[64,128,128]{2,1,0:T(8,128)(2,1)}, u32[]{:S(2)}) copy-start(bf16[64,128,128]{2,1,0:T(8,128)(2,1)} %v_ref.1) | copy-start | bytes 6291460
  4.2 9.8 %collective-permute-start = (bf16[2048,128]{1,0:T(8,128)(2,1)}, bf16[2048,128]{1,0:T(8,128)(2,1)S(1)}, u32[]{:S(2)}, u32[]{:S(2)}) collective-permute-start(bf16[2048,128]{1,0:T(8,128)(2,1)} %shard_map.73.refs_2_), channel_id=1, source_target_pairs={{0,8},{8,0},{16,24},{24,16},{32,40},{40,32},{48,56},{56,48},{64,72... | collective-permute-start | bytes 1572872 | tf_op jit(solution)/shard_map/ppermute | solution.py:316
  4.3 20.5 %collective-permute-start.3 = (bf16[2048,128]{1,0:T(8,128)(2,1)}, bf16[2048,128]{1,0:T(8,128)(2,1)S(1)}, u32[]{:S(2)}, u32[]{:S(2)}) collective-permute-start(bf16[2048,128]{1,0:T(8,128)(2,1)} %shard_map.73.refs_2_), channel_id=1, source_target_pairs={{0,192},{8,200},{16,208},{24,216},{32,224},{40,232},{48,240},{56,2... | collective-permute-start | bytes 1572872 | tf_op jit(solution)/shard_map/ppermute | solution.py:317
  5.8 19.0 %collective-permute-start.2 = (bf16[2048,128]{1,0:T(8,128)(2,1)}, bf16[2048,128]{1,0:T(8,128)(2,1)S(1)}, u32[]{:S(2)}, u32[]{:S(2)}) collective-permute-start(bf16[2048,128]{1,0:T(8,128)(2,1)} %shard_map.73.refs_2_), channel_id=1, source_target_pairs={{0,64},{8,72},{16,80},{24,88},{32,96},{40,104},{48,112},{56,120},{... | collective-permute-start | bytes 1572872 | tf_op jit(solution)/shard_map/ppermute | solution.py:317
  6.6 8.0 %collective-permute-start.6 = (bf16[128,512]{1,0:T(8,128)(2,1)S(1)}, bf16[128,512]{1,0:T(8,128)(2,1)S(1)}, u32[]{:S(2)}, u32[]{:S(2)}) collective-permute-start(bf16[128,512]{1,0:T(8,128)(2,1)S(1)} %shard_map.75.refs_0_), channel_id=1, source_target_pairs={{0,48},{8,56},{16,0},{24,8},{32,16},{40,24},{48,32},{56,40},{64,11... | collective-permute-start | bytes 393224 | tf_op jit(solution)/shard_map/ppermute | solution.py:320
  13.9 9.4 %collective-permute-start.5 = (bf16[128,512]{1,0:T(8,128)(2,1)S(1)}, bf16[128,512]{1,0:T(8,128)(2,1)S(1)}, u32[]{:S(2)}, u32[]{:S(2)}) collective-permute-start(bf16[128,512]{1,0:T(8,128)(2,1)S(1)} %shard_map.75.refs_0_), channel_id=1, source_target_pairs={{0,32},{8,40},{16,48},{24,56},{32,0},{40,8},{48,16},{56,24},{64,96... | collective-permute-start | bytes 393224 | tf_op jit(solution)/shard_map/ppermute | solution.py:320
  14.0 9.3 %collective-permute-start.4 = (bf16[128,512]{1,0:T(8,128)(2,1)S(1)}, bf16[128,512]{1,0:T(8,128)(2,1)S(1)}, u32[]{:S(2)}, u32[]{:S(2)}) collective-permute-start(bf16[128,512]{1,0:T(8,128)(2,1)S(1)} %shard_map.75.refs_0_), channel_id=1, source_target_pairs={{0,16},{8,24},{16,32},{24,40},{32,48},{40,56},{48,0},{56,8},{64,80... | collective-permute-start | bytes 393224 | tf_op jit(solution)/shard_map/ppermute | solution.py:320
  16.2 16.4 %collective-permute-start.9 = (bf16[544,128]{1,0:T(8,128)(2,1)S(1)}, bf16[544,128]{1,0:T(8,128)(2,1)S(1)}, u32[]{:S(2)}, u32[]{:S(2)}) collective-permute-start(bf16[544,128]{1,0:T(8,128)(2,1)S(1)} %shard_map.80), channel_id=1, source_target_pairs={{0,128},{8,136},{16,144},{24,152},{32,160},{40,168},{48,176},{56,1... | collective-permute-start | bytes 417800 | tf_op jit(solution)/shard_map/ppermute | solution.py:327
  24.9 7.8 %collective-permute-start.10 = (bf16[544,128]{1,0:T(8,128)(2,1)S(1)}, bf16[544,128]{1,0:T(8,128)(2,1)S(1)}, u32[]{:S(2)}, u32[]{:S(2)}) collective-permute-start(bf16[544,128]{1,0:T(8,128)(2,1)S(1)} %shard_map.77), channel_id=1, source_target_pairs={{0,128},{8,136},{16,144},{24,152},{32,160},{40,168},{48,176},{56,1... | collective-permute-start | bytes 417800 | tf_op jit(solution)/shard_map/ppermute | solution.py:333
  27.6 5.0 %collective-permute-start.7 = (bf16[2048,128]{1,0:T(8,128)(2,1)S(1)}, bf16[2048,128]{1,0:T(8,128)(2,1)S(1)}, u32[]{:S(2)}, u32[]{:S(2)}) collective-permute-start(bf16[2048,128]{1,0:T(8,128)(2,1)S(1)} %collective-permute-done.2.refs_4_), channel_id=1, source_target_pairs={{0,8},{8,0},{16,24},{24,16},{32,40},{40,32},{48,56},{56,48},{64,72... | collective-permute-start | bytes 1572872 | tf_op jit(solution)/shard_map/ppermute | solution.py:334
  27.6 5.1 %collective-permute-start.8 = (bf16[2048,128]{1,0:T(8,128)(2,1)S(1)}, bf16[2048,128]{1,0:T(8,128)(2,1)S(1)}, u32[]{:S(2)}, u32[]{:S(2)}) collective-permute-start(bf16[2048,128]{1,0:T(8,128)(2,1)S(1)} %collective-permute-done.3.refs_5_), channel_id=1, source_target_pairs={{0,8},{8,0},{16,24},{24,16},{32,40},{40,32},{48,56},{56,48},{64,72... | collective-permute-start | bytes 1572872 | tf_op jit(solution)/shard_map/ppermute | solution.py:334
  32.7 14.1 %slice-start = ((s8[8388608]{0:T(1024)(128)(4,1)}), s8[4194304]{0:T(1024)(128)(4,1)S(1)}, s32[]{:S(2)}) async-start(s8[8388608]{0:T(1024)(128)(4,1)} %bitcast), calls=%async_computation | async-start | bytes 8388608
  34.1 12.7 %slice-start.1 = ((s8[8388608]{0:T(1024)(128)(4,1)}), s8[4194304]{0:T(1024)(128)(4,1)S(1)}, s32[]{:S(2)}) async-start(s8[8388608]{0:T(1024)(128)(4,1)} %bitcast), calls=%async_computation.1 | async-start | bytes 8388608
  36.3 7.0 %collective-permute-start.11 = (bf16[272,128]{1,0:T(8,128)(2,1)S(1)}, bf16[272,128]{1,0:T(8,128)(2,1)S(1)}, u32[]{:S(2)}, u32[]{:S(2)}) collective-permute-start(bf16[272,128]{1,0:T(8,128)(2,1)S(1)} %get-tuple-element.71), channel_id=1, source_target_pairs={{0,16},{8,24},{16,32},{24,40},{32,48},{40,56},{48,0},{56,8},{64,80... | collective-permute-start | bytes 208904 | tf_op jit(solution)/shard_map/ppermute | solution.py:343
  37.1 6.2 %collective-permute-start.12 = (bf16[272,128]{1,0:T(8,128)(2,1)S(1)}, bf16[272,128]{1,0:T(8,128)(2,1)S(1)}, u32[]{:S(2)}, u32[]{:S(2)}) collective-permute-start(bf16[272,128]{1,0:T(8,128)(2,1)S(1)} %get-tuple-element.72), channel_id=1, source_target_pairs={{0,48},{8,56},{16,0},{24,8},{32,16},{40,24},{48,32},{56,40},{64,11... | collective-permute-start | bytes 208904 | tf_op jit(solution)/shard_map/ppermute | solution.py:343
  40.2 6.5 %collective-permute-start.13 = (bf16[272,128]{1,0:T(8,128)(2,1)S(1)}, bf16[272,128]{1,0:T(8,128)(2,1)S(1)}, u32[]{:S(2)}, u32[]{:S(2)}) collective-permute-start(bf16[272,128]{1,0:T(8,128)(2,1)S(1)} %shard_map.81), channel_id=1, source_target_pairs={{0,32},{8,40},{16,48},{24,56},{32,0},{40,8},{48,16},{56,24},{64,96... | collective-permute-start | bytes 208904 | tf_op jit(solution)/shard_map/ppermute | solution.py:343
  48.7 8.8 %collective-permute-start.17 = (bf16[64,1024]{1,0:T(8,128)(2,1)S(1)}, bf16[64,1024]{1,0:T(8,128)(2,1)S(1)}, u32[]{:S(2)}, u32[]{:S(2)}) collective-permute-start(bf16[64,1024]{1,0:T(8,128)(2,1)S(1)} %get-tuple-element.82), channel_id=1, source_target_pairs={{0,1},{1,2},{2,3},{3,0},{4,5},{5,6},{6,7},{7,4},{8,9},{9,10},{10,1... | collective-permute-start | bytes 393224 | tf_op jit(solution)/shard_map/ppermute | solution.py:349
  50.4 10.2 %collective-permute-start.18 = (bf16[64,1024]{1,0:T(8,128)(2,1)S(1)}, bf16[64,1024]{1,0:T(8,128)(2,1)S(1)}, u32[]{:S(2)}, u32[]{:S(2)}) collective-permute-start(bf16[64,1024]{1,0:T(8,128)(2,1)S(1)} %get-tuple-element.83), channel_id=1, source_target_pairs={{0,2},{1,3},{2,0},{3,1},{4,6},{5,7},{6,4},{7,5},{8,10},{9,11},{10,... | collective-permute-start | bytes 393224 | tf_op jit(solution)/shard_map/ppermute | solution.py:349
  53.3 7.3 %collective-permute-start.19 = (bf16[64,1024]{1,0:T(8,128)(2,1)S(1)}, bf16[64,1024]{1,0:T(8,128)(2,1)S(1)}, u32[]{:S(2)}, u32[]{:S(2)}) collective-permute-start(bf16[64,1024]{1,0:T(8,128)(2,1)S(1)} %get-tuple-element.84), channel_id=1, source_target_pairs={{0,3},{1,0},{2,1},{3,2},{4,7},{5,4},{6,5},{7,6},{8,11},{9,8},{10,9... | collective-permute-start | bytes 393224 | tf_op jit(solution)/shard_map/ppermute | solution.py:349
  56.0 9.4 %collective-permute-start.14 = (bf16[64,1024]{1,0:T(8,128)(2,1)S(1)}, bf16[64,1024]{1,0:T(8,128)(2,1)S(1)}, u32[]{:S(2)}, u32[]{:S(2)}) collective-permute-start(bf16[64,1024]{1,0:T(8,128)(2,1)S(1)} %get-tuple-element.78), channel_id=1, source_target_pairs={{0,1},{1,2},{2,3},{3,0},{4,5},{5,6},{6,7},{7,4},{8,9},{9,10},{10,1... | collective-permute-start | bytes 393224 | tf_op jit(solution)/shard_map/ppermute | solution.py:351
  56.7 8.6 %collective-permute-start.15 = (bf16[64,1024]{1,0:T(8,128)(2,1)S(1)}, bf16[64,1024]{1,0:T(8,128)(2,1)S(1)}, u32[]{:S(2)}, u32[]{:S(2)}) collective-permute-start(bf16[64,1024]{1,0:T(8,128)(2,1)S(1)} %get-tuple-element.79), channel_id=1, source_target_pairs={{0,2},{1,3},{2,0},{3,1},{4,6},{5,7},{6,4},{7,5},{8,10},{9,11},{10,... | collective-permute-start | bytes 393224 | tf_op jit(solution)/shard_map/ppermute | solution.py:351
  57.5 7.9 %collective-permute-start.16 = (bf16[64,1024]{1,0:T(8,128)(2,1)S(1)}, bf16[64,1024]{1,0:T(8,128)(2,1)S(1)}, u32[]{:S(2)}, u32[]{:S(2)}) collective-permute-start(bf16[64,1024]{1,0:T(8,128)(2,1)S(1)} %get-tuple-element.80), channel_id=1, source_target_pairs={{0,3},{1,0},{2,1},{3,2},{4,7},{5,4},{6,5},{7,6},{8,11},{9,8},{10,9... | collective-permute-start | bytes 393224 | tf_op jit(solution)/shard_map/ppermute | solution.py:351
  60.6 9.0 %collective-permute-start.20 = (bf16[64,1024]{1,0:T(8,128)(2,1)S(1)}, bf16[64,1024]{1,0:T(8,128)(2,1)S(1)}, u32[]{:S(2)}, u32[]{:S(2)}) collective-permute-start(bf16[64,1024]{1,0:T(8,128)(2,1)S(1)} %add_convert_fusion.1), channel_id=1, source_target_pairs={{0,4},{1,5},{2,6},{3,7},{4,0},{5,1},{6,2},{7,3},{8,12},{9,13},{10,... | collective-permute-start | bytes 393224 | tf_op jit(solution)/shard_map/ppermute | solution.py:356
  (4 other events, 28.8 us)

commit v6 on v5

--- a/solution.py
+++ b/solution.py
@@ -129,15 +129,22 @@
 
 def spread(part):
     rows = (part.shape[0] - TILE) // GROUP
-    count = GROUP * rows // TILE
-    row = lax.broadcasted_iota(jnp.int32, (DH, count * DH), 0)
-    first = 3 * lax.shift_right_logical(
-        lax.broadcasted_iota(jnp.int32, (DH, count * DH), 1), DH.bit_length() - 1
+    strip = part[GROUP * rows :, :].astype(F32)
+    lane = lax.broadcasted_iota(jnp.int32, (TILE, DH), 1)
+    row = lax.broadcasted_iota(jnp.int32, (DH, WIDTH), 0)
+    head = lax.shift_right_logical(
+        lax.broadcasted_iota(jnp.int32, (DH, WIDTH), 1), DH.bit_length() - 1
     )
-    chosen = jnp.where((row >= first) & (row < first + 3), 1.0, 0.0).astype(BF16)
-    logs = jnp.dot(part[GROUP * rows :, :], chosen, preferred_element_type=F32)
-    order = [n * GROUP + h for h in range(GROUP) for n in range(rows // TILE)]
-    return jnp.concatenate([logs[:, n * DH : (n + 1) * DH] for n in order], axis=0)
+    chosen = jnp.zeros((DH, WIDTH), F32)
+    pieces = []
+    for n in range(rows // TILE):
+        first = 3 * GROUP * n
+        mine = (lane >= first) & (lane < first + 3 * GROUP)
+        pieces.append(jnp.where(mine, strip, 0.0))
+        at = first + 3 * head
+        chosen = jnp.where((row >= at) & (row < at + 3), 1.0, chosen)
+    pieces = jnp.concatenate(pieces, axis=0).astype(BF16)
+    return heads_of(jnp.dot(pieces, chosen.astype(BF16), preferred_element_type=F32))
 
 
 def pack(o_ref, first, values, logs):
@@ -340,7 +347,7 @@
     state, third = together((state, third))
     away = prefix_partial(group[1:3], 0, near_peer, [state], joins, "each", 1)
     state, away = together((state, away))
-    away = [send(part, perm=blk_perm(dz=-d)) for d, part in zip(shifts[1:], [*away, third])]
+    away = [send(part, perm=blk_perm(dz=-d)) for d, part in zip((2, 3, 1), [third, *away])]
     home = prefix_partial(group[:1], 0, near_peer, [state], joins, "each")
     parts = [*home, *away]
 

time: 70.4 us -> 70.2 us (level)
  no operation moved by 1% of the time
where the time goes in v6:
time: 70.2 us; the launch traced here: 70.1 us
  starting transfers between devices  34.9 us (50%)
  Pallas kernels  21.6 us (31%)
  waiting for transfers between devices  12.5 us (18%)
  other arithmetic  0.83 us (1%)
    pallas_call x8, Pallas kernels, prefix_partial(): pl.pallas_call(kernel, in_specs=in_vmem(len(arrays)), out_specs=in_vmem(l...  13.6 us
    ppermute x3, starting transfers between devices, on_device(): send(away[d], perm=tensor_perm(dy=d))  6.12 us
    ppermute x3, starting transfers between devices, on_device(): group = [pair] + [send(pair, perm=blk_perm(dz=d)) for d in shifts[1:]]  5.45 us
    ppermute x1, starting transfers between devices, on_device(): other = send(summed(away).astype(BF16), perm=tensor_perm(dh=1))  4.79 us
    ppermute x3, starting transfers between devices, on_device(): send(part, perm=blk_perm(dz=-d))  4.74 us
    ppermute x3, waiting for transfers between devices, on_device(): send(part, perm=blk_perm(dz=-d))  4.42 us
    ppermute x1, waiting for transfers between devices, on_device(): other = send(summed(away).astype(BF16), perm=tensor_perm(dh=1))  4.16 us
    ppermute x3, starting transfers between devices, on_device(): send(home[d], perm=tensor_perm(dy=d))  3.53 us
  transfers between devices with their start and end apart: 21, of which 5 were waited for; matrix products, arithmetic and copies ran while one was open for 0% of the time, Pallas kernels for 24%

profile of v6, /device:TPU:2, one launch (start us, length us, event | category | flops | bytes accessed | tf_op | source)
XLA Modules:
  0.0 70.1 jit_solution(15757706016613117196)
XLA Ops:
  0.0 2.1 %collective-permute-start.1 = (bf16[64,512]{1,0:T(8,128)(2,1)}, bf16[64,512]{1,0:T(8,128)(2,1)S(1)}, u32[]{:S(2)}, u32[]{:S(2)}) collective-permute-start(bf16[64,512]{1,0:T(8,128)(2,1)} %a_ref.3), channel_id=1, source_target_pairs={{0,128},{8,136},{16,144},{24,152},{32,160},{40,168},{48,176},{56,1... | collective-permute-start | bytes 196616 | tf_op jit(solution)/shard_map/ppermute | solution.py:321
  2.1 2.1 %shard_map.73.refs_2_ = bf16[2048,128]{1,0:T(8,128)(2,1)} custom-call(bf16[1024,128]{1,0:T(8,128)(2,1)} %a_ref.2, bf16[1024,128]{1,0:T(8,128)(2,1)} %b_ref.1), custom_call_target="tpu_custom_call" | custom-call | flops 880000000 | bytes 1048576 | tf_op jit(solution)/shard_map/pallas_call | solution.py:116
  4.3 1.5 %collective-permute-start.3 = (bf16[2048,128]{1,0:T(8,128)(2,1)}, bf16[2048,128]{1,0:T(8,128)(2,1)S(1)}, u32[]{:S(2)}, u32[]{:S(2)}) collective-permute-start(bf16[2048,128]{1,0:T(8,128)(2,1)} %shard_map.73.refs_2_), channel_id=1, source_target_pairs={{0,192},{8,200},{16,208},{24,216},{32,224},{40,232},{48,240},{56,2... | collective-permute-start | bytes 1572872 | tf_op jit(solution)/shard_map/ppermute | solution.py:324
  6.6 4.7 %collective-permute-start.6 = (bf16[128,512]{1,0:T(8,128)(2,1)S(1)}, bf16[128,512]{1,0:T(8,128)(2,1)S(1)}, u32[]{:S(2)}, u32[]{:S(2)}) collective-permute-start(bf16[128,512]{1,0:T(8,128)(2,1)S(1)} %shard_map.75.refs_0_), channel_id=1, source_target_pairs={{0,48},{8,56},{16,0},{24,8},{32,16},{40,24},{48,32},{56,40},{64,11... | collective-permute-start | bytes 393224 | tf_op jit(solution)/shard_map/ppermute | solution.py:327
  11.4 2.5 %shard_map.74 = (f32[256,128]{1,0:T(8,128)S(1)}, f32[256,128]{1,0:T(8,128)S(1)}) custom-call(s32[64]{0:T(128)S(1)} %copy-done.4, bf16[64,512]{1,0:T(8,128)(2,1)S(1)} %copy-done.3, bf16[64,128,128]{2,1,0:T(8,128)(2,1)S(1)} %copy-done, bf16[64,128,128]{2,1,0:T(8,128)(2,1)S(1)} %copy-done.1), custom_call_target="tpu_custom_call" | custom-call | flops 3300000000 | bytes 1048576 | tf_op jit(solution)/shard_map/pallas_call | solution.py:86
  14.7 1.5 %shard_map.80 = bf16[544,128]{1,0:T(8,128)(2,1)S(1)} custom-call(bf16[128,512]{1,0:T(8,128)(2,1)S(1)} %shard_map.75.refs_0_, bf16[128,512]{1,0:T(8,128)(2,1)S(1)} %collective-permute-done.6.refs_1_.refs_0_, bf16[2048,128]{1,0:T(8,128)(2,1)S(1)} %copy-done.2, bf16[2048,128]{1,0:T(8,128)(2,1)S(1)} %collective-permute-done.refs_3_), custom_call_target="tpu_custom_call" | custom-call | flops 2164807168 | bytes 1048576 | tf_op jit(solution)/shard_map/pallas_call | solution.py:257
  16.2 2.7 %collective-permute-start.9 = (bf16[544,128]{1,0:T(8,128)(2,1)S(1)}, bf16[544,128]{1,0:T(8,128)(2,1)S(1)}, u32[]{:S(2)}, u32[]{:S(2)}) collective-permute-start(bf16[544,128]{1,0:T(8,128)(2,1)S(1)} %shard_map.80), channel_id=1, source_target_pairs={{0,128},{8,136},{16,144},{24,152},{32,160},{40,168},{48,176},{56,1... | collective-permute-start | bytes 417800 | tf_op jit(solution)/shard_map/ppermute | solution.py:334
  18.9 1.5 %shard_map.76 = (f32[512,256]{1,0:T(8,128)S(1)}, f32[512,128]{1,0:T(8,128)S(1)}) custom-call(bf16[128,512]{1,0:T(8,128)(2,1)S(1)} %shard_map.75.refs_0_, bf16[128,512]{1,0:T(8,128)(2,1)S(1)} %collective-permute-done.6.refs_1_.refs_0_, bf16[2048,128]{1,0:T(8,128)(2,1)S(1)} %copy-done.2, bf16[2048,128]{1,0:T(8,128)(2,1)S(1)} %collective-permute-done.refs_3_), custom_call_target="tpu_custom_call" | custom-call | flops 2164807168 | bytes 1048576 | tf_op jit(solution)/shard_map/pallas_call | solution.py:257
  20.4 2.9 %collective-permute-done.5.refs_1_.refs_3_.refs_0_ = bf16[128,512]{1,0:T(8,128)(2,1)S(1)} collective-permute-done((bf16[128,512]{1,0:T(8,128)(2,1)S(1)}, bf16[128,512]{1,0:T(8,128)(2,1)S(1)}, u32[]{:S(2)}, u32[]{:S(2)}) %collective-permute-start.5) | collective-permute-done | bytes 131104 | tf_op jit(solution)/shard_map/ppermute | solution.py:327
  23.3 1.5 %shard_map.77 = bf16[544,128]{1,0:T(8,128)(2,1)S(1)} custom-call(bf16[128,512]{1,0:T(8,128)(2,1)S(1)} %collective-permute-done.4.refs_0_.refs_2_.refs_1_, bf16[128,512]{1,0:T(8,128)(2,1)S(1)} %collective-permute-done.5.refs_1_.refs_3_.refs_0_, bf16[2048,128]{1,0:T(8,128)(2,1)S(1)} %copy-done.2, bf16[2048,128]{1,0:T(8,128)(2,1)S(1)} %collective-permute-done.refs_3_), custom_call_target="tpu_custom_call" | custom-call | flops 2164807168 | bytes 1048576 | tf_op jit(solution)/shard_map/pallas_call | solution.py:257
  24.9 2.7 %collective-permute-start.10 = (bf16[544,128]{1,0:T(8,128)(2,1)S(1)}, bf16[544,128]{1,0:T(8,128)(2,1)S(1)}, u32[]{:S(2)}, u32[]{:S(2)}) collective-permute-start(bf16[544,128]{1,0:T(8,128)(2,1)S(1)} %shard_map.77), channel_id=1, source_target_pairs={{0,128},{8,136},{16,144},{24,152},{32,160},{40,168},{48,176},{56,1... | collective-permute-start | bytes 417800 | tf_op jit(solution)/shard_map/ppermute | solution.py:340
  28.1 1.5 %shard_map.78 = (f32[512,256]{1,0:T(8,128)S(1)}, f32[512,128]{1,0:T(8,128)S(1)}) custom-call(bf16[128,512]{1,0:T(8,128)(2,1)S(1)} %collective-permute-done.4.refs_0_.refs_2_.refs_1_, bf16[128,512]{1,0:T(8,128)(2,1)S(1)} %collective-permute-done.5.refs_1_.refs_3_.refs_0_, bf16[2048,128]{1,0:T(8,128)(2,1)S(1)} %copy-done.2, ...), custom_call_target="tpu_custom_call" | custom-call | flops 2164807168 | bytes 1048576 | tf_op jit(solution)/shard_map/pallas_call | solution.py:257
  29.6 3.1 %shard_map.79 = (f32[1024,256]{1,0:T(8,128)S(1)}, f32[1024,128]{1,0:T(8,128)S(1)}) custom-call(bf16[128,512]{1,0:T(8,128)(2,1)S(1)} %shard_map.75.refs_0_, bf16[128,512]{1,0:T(8,128)(2,1)S(1)} %collective-permute-done.6.refs_1_.refs_0_, bf16[128,512]{1,0:T(8,128)(2,1)S(1)} %collective-permute-done.4.refs_0_.refs_2_.refs_1_, ...), custom_call_target="tpu_custom_call" | custom-call | flops 3779614208 | bytes 1048576 | tf_op jit(solution)/shard_map/pallas_call | solution.py:257
  34.0 2.0 %shard_map.82 = (bf16[272,128]{1,0:T(8,128)(2,1)S(1)}, bf16[272,128]{1,0:T(8,128)(2,1)S(1)}) custom-call(bf16[128,512]{1,0:T(8,128)(2,1)S(1)} %collective-permute-done.6.refs_1_.refs_0_, bf16[128,512]{1,0:T(8,128)(2,1)S(1)} %collective-permute-done.4.refs_0_.refs_2_.refs_1_, bf16[2048,128]{1,0:T(8,128)(2,1)S(1)} %collective-permute-done.7.refs_1_.refs_2_, ...), custom_call_target="tpu_custom_call" | custom-call | flops 2164807168 | bytes 1048576 | tf_op jit(solution)/shard_map/pallas_call | solution.py:257
  36.8 3.1 %collective-permute-start.13 = (bf16[272,128]{1,0:T(8,128)(2,1)S(1)}, bf16[272,128]{1,0:T(8,128)(2,1)S(1)}, u32[]{:S(2)}, u32[]{:S(2)}) collective-permute-start(bf16[272,128]{1,0:T(8,128)(2,1)S(1)} %get-tuple-element.73), channel_id=1, source_target_pairs={{0,48},{8,56},{16,0},{24,8},{32,16},{40,24},{48,32},{56,40},{64,11... | collective-permute-start | bytes 208904 | tf_op jit(solution)/shard_map/ppermute | solution.py:350
  43.0 3.5 %collective-permute-done.11.refs_1_ = bf16[272,128]{1,0:T(8,128)(2,1)S(1)} collective-permute-done((bf16[272,128]{1,0:T(8,128)(2,1)S(1)}, bf16[272,128]{1,0:T(8,128)(2,1)S(1)}, u32[]{:S(2)}, u32[]{:S(2)}) %collective-permute-start.11) | collective-permute-done | bytes 69664 | tf_op jit(solution)/shard_map/ppermute | solution.py:350
  46.4 1.9 %shard_map.84 = (f32[64,1024]{1,0:T(8,128)S(1)}, bf16[64,1024]{1,0:T(8,128)(2,1)S(1)}, bf16[64,1024]{1,0:T(8,128)(2,1)S(1)}, bf16[64,1024]{1,0:T(8,128)(2,1)S(1)}, bf16[64,512]{1,0:T(8,128)(2,1)S(1)}) custom-call(s32[8]{0:T(128)S(1)} %fusion.index_ref, bf16[512,8192]{1,0:T(8,128)(2,1)S(1)} %bitcast.1, bf16[272,128]{1,0:T(8,128)(2,1)S(1)} %shard_map.83.refs_0_, ...), custom_call_target="tpu_custom_call" | custom-call | flops 3300000000 | bytes 1048576 | tf_op jit(solution)/shard_map/pallas_call | solution.py:303
  48.3 1.9 %collective-permute-start.17 = (bf16[64,1024]{1,0:T(8,128)(2,1)S(1)}, bf16[64,1024]{1,0:T(8,128)(2,1)S(1)}, u32[]{:S(2)}, u32[]{:S(2)}) collective-permute-start(bf16[64,1024]{1,0:T(8,128)(2,1)S(1)} %get-tuple-element.82), channel_id=1, source_target_pairs={{0,1},{1,2},{2,3},{3,0},{4,5},{5,6},{6,7},{7,4},{8,9},{9,10},{10,1... | collective-permute-start | bytes 393224 | tf_op jit(solution)/shard_map/ppermute | solution.py:356
  50.2 2.9 %collective-permute-start.18 = (bf16[64,1024]{1,0:T(8,128)(2,1)S(1)}, bf16[64,1024]{1,0:T(8,128)(2,1)S(1)}, u32[]{:S(2)}, u32[]{:S(2)}) collective-permute-start(bf16[64,1024]{1,0:T(8,128)(2,1)S(1)} %get-tuple-element.83), channel_id=1, source_target_pairs={{0,2},{1,3},{2,0},{3,1},{4,6},{5,7},{6,4},{7,5},{8,10},{9,11},{10,... | collective-permute-start | bytes 393224 | tf_op jit(solution)/shard_map/ppermute | solution.py:356
  53.1 1.3 %collective-permute-start.19 = (bf16[64,1024]{1,0:T(8,128)(2,1)S(1)}, bf16[64,1024]{1,0:T(8,128)(2,1)S(1)}, u32[]{:S(2)}, u32[]{:S(2)}) collective-permute-start(bf16[64,1024]{1,0:T(8,128)(2,1)S(1)} %get-tuple-element.84), channel_id=1, source_target_pairs={{0,3},{1,0},{2,1},{3,2},{4,7},{5,4},{6,5},{7,6},{8,11},{9,8},{10,9... | collective-permute-start | bytes 393224 | tf_op jit(solution)/shard_map/ppermute | solution.py:356
  54.4 1.4 %shard_map.85 = (f32[64,1024]{1,0:T(8,128)S(1)}, bf16[64,1024]{1,0:T(8,128)(2,1)S(1)}, bf16[64,1024]{1,0:T(8,128)(2,1)S(1)}, bf16[64,1024]{1,0:T(8,128)(2,1)S(1)}) custom-call(s32[8]{0:T(128)S(1)} %fusion.index_ref, bf16[512,8192]{1,0:T(8,128)(2,1)S(1)} %bitcast.1, bf16[64,512]{1,0:T(8,128)(2,1)S(1)} %get-tuple-element.76.refs_0_), custom_call_target="tpu_custom_call" | custom-call | flops 3300000000 | bytes 1048576 | tf_op jit(solution)/shard_map/pallas_call | solution.py:303
  57.4 2.0 %collective-permute-start.16 = (bf16[64,1024]{1,0:T(8,128)(2,1)S(1)}, bf16[64,1024]{1,0:T(8,128)(2,1)S(1)}, u32[]{:S(2)}, u32[]{:S(2)}) collective-permute-start(bf16[64,1024]{1,0:T(8,128)(2,1)S(1)} %get-tuple-element.80), channel_id=1, source_target_pairs={{0,3},{1,0},{2,1},{3,2},{4,7},{5,4},{6,5},{7,6},{8,11},{9,8},{10,9... | collective-permute-start | bytes 393224 | tf_op jit(solution)/shard_map/ppermute | solution.py:358
  60.4 4.8 %collective-permute-start.20 = (bf16[64,1024]{1,0:T(8,128)(2,1)S(1)}, bf16[64,1024]{1,0:T(8,128)(2,1)S(1)}, u32[]{:S(2)}, u32[]{:S(2)}) collective-permute-start(bf16[64,1024]{1,0:T(8,128)(2,1)S(1)} %add_convert_fusion.1), channel_id=1, source_target_pairs={{0,4},{1,5},{2,6},{3,7},{4,0},{5,1},{6,2},{7,3},{8,12},{9,13},{10,... | collective-permute-start | bytes 393224 | tf_op jit(solution)/shard_map/ppermute | solution.py:363
  65.2 4.2 %collective-permute-done.20 = bf16[64,1024]{1,0:T(8,128)(2,1)S(1)} collective-permute-done((bf16[64,1024]{1,0:T(8,128)(2,1)S(1)}, bf16[64,1024]{1,0:T(8,128)(2,1)S(1)}, u32[]{:S(2)}, u32[]{:S(2)}) %collective-permute-start.20) | collective-permute-done | bytes 131104 | tf_op jit(solution)/shard_map/ppermute | solution.py:363
  (49 shorter events, 10.7 us)
Async XLA Ops:
  0.0 6.4 %collective-permute-start.1 = (bf16[64,512]{1,0:T(8,128)(2,1)}, bf16[64,512]{1,0:T(8,128)(2,1)S(1)}, u32[]{:S(2)}, u32[]{:S(2)}) collective-permute-start(bf16[64,512]{1,0:T(8,128)(2,1)} %a_ref.3), channel_id=1, source_target_pairs={{0,128},{8,136},{16,144},{24,152},{32,160},{40,168},{48,176},{56,1... | collective-permute-start | bytes 196616 | tf_op jit(solution)/shard_map/ppermute | solution.py:321
  2.1 9.2 %copy-start.1 = (bf16[64,128,128]{2,1,0:T(8,128)(2,1)S(1)}, bf16[64,128,128]{2,1,0:T(8,128)(2,1)}, u32[]{:S(2)}) copy-start(bf16[64,128,128]{2,1,0:T(8,128)(2,1)} %v_ref.1) | copy-start | bytes 6291460
  4.2 9.8 %collective-permute-start = (bf16[2048,128]{1,0:T(8,128)(2,1)}, bf16[2048,128]{1,0:T(8,128)(2,1)S(1)}, u32[]{:S(2)}, u32[]{:S(2)}) collective-permute-start(bf16[2048,128]{1,0:T(8,128)(2,1)} %shard_map.73.refs_2_), channel_id=1, source_target_pairs={{0,8},{8,0},{16,24},{24,16},{32,40},{40,32},{48,56},{56,48},{64,72... | collective-permute-start | bytes 1572872 | tf_op jit(solution)/shard_map/ppermute | solution.py:323
  4.3 20.5 %collective-permute-start.3 = (bf16[2048,128]{1,0:T(8,128)(2,1)}, bf16[2048,128]{1,0:T(8,128)(2,1)S(1)}, u32[]{:S(2)}, u32[]{:S(2)}) collective-permute-start(bf16[2048,128]{1,0:T(8,128)(2,1)} %shard_map.73.refs_2_), channel_id=1, source_target_pairs={{0,192},{8,200},{16,208},{24,216},{32,224},{40,232},{48,240},{56,2... | collective-permute-start | bytes 1572872 | tf_op jit(solution)/shard_map/ppermute | solution.py:324
  5.8 19.0 %collective-permute-start.2 = (bf16[2048,128]{1,0:T(8,128)(2,1)}, bf16[2048,128]{1,0:T(8,128)(2,1)S(1)}, u32[]{:S(2)}, u32[]{:S(2)}) collective-permute-start(bf16[2048,128]{1,0:T(8,128)(2,1)} %shard_map.73.refs_2_), channel_id=1, source_target_pairs={{0,64},{8,72},{16,80},{24,88},{32,96},{40,104},{48,112},{56,120},{... | collective-permute-start | bytes 1572872 | tf_op jit(solution)/shard_map/ppermute | solution.py:324
  6.6 8.0 %collective-permute-start.6 = (bf16[128,512]{1,0:T(8,128)(2,1)S(1)}, bf16[128,512]{1,0:T(8,128)(2,1)S(1)}, u32[]{:S(2)}, u32[]{:S(2)}) collective-permute-start(bf16[128,512]{1,0:T(8,128)(2,1)S(1)} %shard_map.75.refs_0_), channel_id=1, source_target_pairs={{0,48},{8,56},{16,0},{24,8},{32,16},{40,24},{48,32},{56,40},{64,11... | collective-permute-start | bytes 393224 | tf_op jit(solution)/shard_map/ppermute | solution.py:327
  13.9 9.4 %collective-permute-start.5 = (bf16[128,512]{1,0:T(8,128)(2,1)S(1)}, bf16[128,512]{1,0:T(8,128)(2,1)S(1)}, u32[]{:S(2)}, u32[]{:S(2)}) collective-permute-start(bf16[128,512]{1,0:T(8,128)(2,1)S(1)} %shard_map.75.refs_0_), channel_id=1, source_target_pairs={{0,32},{8,40},{16,48},{24,56},{32,0},{40,8},{48,16},{56,24},{64,96... | collective-permute-start | bytes 393224 | tf_op jit(solution)/shard_map/ppermute | solution.py:327
  14.0 9.3 %collective-permute-start.4 = (bf16[128,512]{1,0:T(8,128)(2,1)S(1)}, bf16[128,512]{1,0:T(8,128)(2,1)S(1)}, u32[]{:S(2)}, u32[]{:S(2)}) collective-permute-start(bf16[128,512]{1,0:T(8,128)(2,1)S(1)} %shard_map.75.refs_0_), channel_id=1, source_target_pairs={{0,16},{8,24},{16,32},{24,40},{32,48},{40,56},{48,0},{56,8},{64,80... | collective-permute-start | bytes 393224 | tf_op jit(solution)/shard_map/ppermute | solution.py:327
  16.2 16.4 %collective-permute-start.9 = (bf16[544,128]{1,0:T(8,128)(2,1)S(1)}, bf16[544,128]{1,0:T(8,128)(2,1)S(1)}, u32[]{:S(2)}, u32[]{:S(2)}) collective-permute-start(bf16[544,128]{1,0:T(8,128)(2,1)S(1)} %shard_map.80), channel_id=1, source_target_pairs={{0,128},{8,136},{16,144},{24,152},{32,160},{40,168},{48,176},{56,1... | collective-permute-start | bytes 417800 | tf_op jit(solution)/shard_map/ppermute | solution.py:334
  24.9 7.8 %collective-permute-start.10 = (bf16[544,128]{1,0:T(8,128)(2,1)S(1)}, bf16[544,128]{1,0:T(8,128)(2,1)S(1)}, u32[]{:S(2)}, u32[]{:S(2)}) collective-permute-start(bf16[544,128]{1,0:T(8,128)(2,1)S(1)} %shard_map.77), channel_id=1, source_target_pairs={{0,128},{8,136},{16,144},{24,152},{32,160},{40,168},{48,176},{56,1... | collective-permute-start | bytes 417800 | tf_op jit(solution)/shard_map/ppermute | solution.py:340
  27.6 5.0 %collective-permute-start.7 = (bf16[2048,128]{1,0:T(8,128)(2,1)S(1)}, bf16[2048,128]{1,0:T(8,128)(2,1)S(1)}, u32[]{:S(2)}, u32[]{:S(2)}) collective-permute-start(bf16[2048,128]{1,0:T(8,128)(2,1)S(1)} %collective-permute-done.2.refs_4_), channel_id=1, source_target_pairs={{0,8},{8,0},{16,24},{24,16},{32,40},{40,32},{48,56},{56,48},{64,72... | collective-permute-start | bytes 1572872 | tf_op jit(solution)/shard_map/ppermute | solution.py:341
  27.6 5.1 %collective-permute-start.8 = (bf16[2048,128]{1,0:T(8,128)(2,1)S(1)}, bf16[2048,128]{1,0:T(8,128)(2,1)S(1)}, u32[]{:S(2)}, u32[]{:S(2)}) collective-permute-start(bf16[2048,128]{1,0:T(8,128)(2,1)S(1)} %collective-permute-done.3.refs_5_), channel_id=1, source_target_pairs={{0,8},{8,0},{16,24},{24,16},{32,40},{40,32},{48,56},{56,48},{64,72... | collective-permute-start | bytes 1572872 | tf_op jit(solution)/shard_map/ppermute | solution.py:341
  32.7 13.8 %slice-start = ((s8[8388608]{0:T(1024)(128)(4,1)}), s8[4194304]{0:T(1024)(128)(4,1)S(1)}, s32[]{:S(2)}) async-start(s8[8388608]{0:T(1024)(128)(4,1)} %bitcast), calls=%async_computation | async-start | bytes 8388608
  34.0 12.5 %slice-start.1 = ((s8[8388608]{0:T(1024)(128)(4,1)}), s8[4194304]{0:T(1024)(128)(4,1)S(1)}, s32[]{:S(2)}) async-start(s8[8388608]{0:T(1024)(128)(4,1)} %bitcast), calls=%async_computation.1 | async-start | bytes 8388608
  36.0 7.0 %collective-permute-start.12 = (bf16[272,128]{1,0:T(8,128)(2,1)S(1)}, bf16[272,128]{1,0:T(8,128)(2,1)S(1)}, u32[]{:S(2)}, u32[]{:S(2)}) collective-permute-start(bf16[272,128]{1,0:T(8,128)(2,1)S(1)} %get-tuple-element.72), channel_id=1, source_target_pairs={{0,16},{8,24},{16,32},{24,40},{32,48},{40,56},{48,0},{56,8},{64,80... | collective-permute-start | bytes 208904 | tf_op jit(solution)/shard_map/ppermute | solution.py:350
  36.8 6.2 %collective-permute-start.13 = (bf16[272,128]{1,0:T(8,128)(2,1)S(1)}, bf16[272,128]{1,0:T(8,128)(2,1)S(1)}, u32[]{:S(2)}, u32[]{:S(2)}) collective-permute-start(bf16[272,128]{1,0:T(8,128)(2,1)S(1)} %get-tuple-element.73), channel_id=1, source_target_pairs={{0,48},{8,56},{16,0},{24,8},{32,16},{40,24},{48,32},{56,40},{64,11... | collective-permute-start | bytes 208904 | tf_op jit(solution)/shard_map/ppermute | solution.py:350
  39.9 6.5 %collective-permute-start.11 = (bf16[272,128]{1,0:T(8,128)(2,1)S(1)}, bf16[272,128]{1,0:T(8,128)(2,1)S(1)}, u32[]{:S(2)}, u32[]{:S(2)}) collective-permute-start(bf16[272,128]{1,0:T(8,128)(2,1)S(1)} %shard_map.81), channel_id=1, source_target_pairs={{0,32},{8,40},{16,48},{24,56},{32,0},{40,8},{48,16},{56,24},{64,96... | collective-permute-start | bytes 208904 | tf_op jit(solution)/shard_map/ppermute | solution.py:350
  48.3 9.1 %collective-permute-start.17 = (bf16[64,1024]{1,0:T(8,128)(2,1)S(1)}, bf16[64,1024]{1,0:T(8,128)(2,1)S(1)}, u32[]{:S(2)}, u32[]{:S(2)}) collective-permute-start(bf16[64,1024]{1,0:T(8,128)(2,1)S(1)} %get-tuple-element.82), channel_id=1, source_target_pairs={{0,1},{1,2},{2,3},{3,0},{4,5},{5,6},{6,7},{7,4},{8,9},{9,10},{10,1... | collective-permute-start | bytes 393224 | tf_op jit(solution)/shard_map/ppermute | solution.py:356
  50.2 10.2 %collective-permute-start.18 = (bf16[64,1024]{1,0:T(8,128)(2,1)S(1)}, bf16[64,1024]{1,0:T(8,128)(2,1)S(1)}, u32[]{:S(2)}, u32[]{:S(2)}) collective-permute-start(bf16[64,1024]{1,0:T(8,128)(2,1)S(1)} %get-tuple-element.83), channel_id=1, source_target_pairs={{0,2},{1,3},{2,0},{3,1},{4,6},{5,7},{6,4},{7,5},{8,10},{9,11},{10,... | collective-permute-start | bytes 393224 | tf_op jit(solution)/shard_map/ppermute | solution.py:356
  53.1 7.3 %collective-permute-start.19 = (bf16[64,1024]{1,0:T(8,128)(2,1)S(1)}, bf16[64,1024]{1,0:T(8,128)(2,1)S(1)}, u32[]{:S(2)}, u32[]{:S(2)}) collective-permute-start(bf16[64,1024]{1,0:T(8,128)(2,1)S(1)} %get-tuple-element.84), channel_id=1, source_target_pairs={{0,3},{1,0},{2,1},{3,2},{4,7},{5,4},{6,5},{7,6},{8,11},{9,8},{10,9... | collective-permute-start | bytes 393224 | tf_op jit(solution)/shard_map/ppermute | solution.py:356
  55.8 9.4 %collective-permute-start.14 = (bf16[64,1024]{1,0:T(8,128)(2,1)S(1)}, bf16[64,1024]{1,0:T(8,128)(2,1)S(1)}, u32[]{:S(2)}, u32[]{:S(2)}) collective-permute-start(bf16[64,1024]{1,0:T(8,128)(2,1)S(1)} %get-tuple-element.78), channel_id=1, source_target_pairs={{0,1},{1,2},{2,3},{3,0},{4,5},{5,6},{6,7},{7,4},{8,9},{9,10},{10,1... | collective-permute-start | bytes 393224 | tf_op jit(solution)/shard_map/ppermute | solution.py:358
  56.6 8.6 %collective-permute-start.15 = (bf16[64,1024]{1,0:T(8,128)(2,1)S(1)}, bf16[64,1024]{1,0:T(8,128)(2,1)S(1)}, u32[]{:S(2)}, u32[]{:S(2)}) collective-permute-start(bf16[64,1024]{1,0:T(8,128)(2,1)S(1)} %get-tuple-element.79), channel_id=1, source_target_pairs={{0,2},{1,3},{2,0},{3,1},{4,6},{5,7},{6,4},{7,5},{8,10},{9,11},{10,... | collective-permute-start | bytes 393224 | tf_op jit(solution)/shard_map/ppermute | solution.py:358
  57.4 7.9 %collective-permute-start.16 = (bf16[64,1024]{1,0:T(8,128)(2,1)S(1)}, bf16[64,1024]{1,0:T(8,128)(2,1)S(1)}, u32[]{:S(2)}, u32[]{:S(2)}) collective-permute-start(bf16[64,1024]{1,0:T(8,128)(2,1)S(1)} %get-tuple-element.80), channel_id=1, source_target_pairs={{0,3},{1,0},{2,1},{3,2},{4,7},{5,4},{6,5},{7,6},{8,11},{9,8},{10,9... | collective-permute-start | bytes 393224 | tf_op jit(solution)/shard_map/ppermute | solution.py:358
  60.4 9.0 %collective-permute-start.20 = (bf16[64,1024]{1,0:T(8,128)(2,1)S(1)}, bf16[64,1024]{1,0:T(8,128)(2,1)S(1)}, u32[]{:S(2)}, u32[]{:S(2)}) collective-permute-start(bf16[64,1024]{1,0:T(8,128)(2,1)S(1)} %add_convert_fusion.1), channel_id=1, source_target_pairs={{0,4},{1,5},{2,6},{3,7},{4,0},{5,1},{6,2},{7,3},{8,12},{9,13},{10,... | collective-permute-start | bytes 393224 | tf_op jit(solution)/shard_map/ppermute | solution.py:363
  (4 other events, 28.8 us)
